TPU v7x, 32 devices: a whole 2x2x4 slice. The times are simulated.
32 devices in a mesh: fsdp: 4 (over y, x), tensor: 8 (over z, core).
Axes of the slice: x: 2, y: 2, z: 4, core: 2. Of those that a mesh axis runs over, the one named last changes fastest.
Arguments:
- tokens: bfloat16 [640, 4096], P('fsdp', 'tensor'), may hold values from -6 to 6
- out_grad: bfloat16 [640, 4096], P('fsdp', 'tensor'), may hold values from -0.26953125 to 0.26953125
- gate_weight: bfloat16 [4096, 16384], P('fsdp', 'tensor'), may hold values from -0.125 to 0.125
- up_weight: bfloat16 [4096, 16384], P('fsdp', 'tensor'), may hold values from -0.125 to 0.125
- down_weight: bfloat16 [16384, 4096], P('tensor', 'fsdp'), may hold values from -1.796875 to 1.796875
- gate_mask: int32 [32, 128], replicated, may hold values from 0 to 1, as said below
- up_mask: int32 [32, 128], replicated, may hold values from 0 to 1, as said below
- down_mask: int32 [128, 32], replicated, may hold values from 0 to 1, as said below
Outputs:
- input_grad: bfloat16 [640, 4096], P('fsdp', 'tensor')
- down_grad: bfloat16 [16384, 4096], P('tensor', 'fsdp')
Inputs may be any that keep to these rules, and one draw needn't show every extreme that they name: `gate_mask`: seen as regions of 8 x 16 blocks (the block rows of one index of fsdp and the block columns of one index of tensor), each region keeps between 32 and 80 blocks, and some region keeps exactly 80. `up_mask`: seen as regions of 8 x 16 blocks as for gate_mask, each region keeps between 32 and 80 blocks, and some region keeps exactly 80. `down_mask`: seen as regions of 16 x 8 blocks (the block rows of one index of tensor and the block columns of one index of fsdp), each region keeps between 32 and 80 blocks, and some region keeps exactly 80.
All inputs are finite; a program needn't handle non-finite values.
Results may differ from a plain program's by a relative error of at most 0.013.
Values may be sent and summed in bfloat16 or wider, within the bound.
No kernel may reach another device: no remote copies, remote signals or barrier semaphores. Data moves between devices by JAX's collectives and lax.ppermute only.
A program may use at most 256 MiB of HBM per device.

v0:
```python
import jax
import jax.numpy as jnp
from jax import lax
from jax.sharding import PartitionSpec as P

BLOCK = 128


def slot_hits(kept_flags, capacity):
    slot_rank = jnp.cumsum(kept_flags, axis=-1) - 1
    slot_ids = jnp.arange(capacity, dtype=jnp.int32)
    chosen = (kept_flags[..., None, :] == 1) & (slot_rank[..., None, :] == slot_ids[:, None])
    return chosen.astype(jnp.int32)


def slot_table(kept_flags, d_of_block, f_of_block, capacity, row_blocks):
    chosen = slot_hits(kept_flags, capacity)
    owners = kept_flags.shape[0]
    owner_base = (jnp.arange(owners, dtype=jnp.int32) * row_blocks)[:, None]
    d_index = owner_base + jnp.sum(chosen * d_of_block, axis=-1)
    f_index = jnp.sum(chosen * f_of_block, axis=-1)
    filled = jnp.sum(chosen, axis=-1)
    return (d_index.reshape(-1), f_index.reshape(-1), filled.reshape(-1))


def pack_blocks(blocks, own_flags, capacity):
    chosen = slot_hits(own_flags, capacity).astype(jnp.bfloat16)
    packed = jnp.einsum("cs,sij->cij", chosen, blocks, preferred_element_type=jnp.float32)
    return packed.astype(jnp.bfloat16)


def unpack_blocks(packed, kept_flags):
    capacity = packed.shape[0]
    slot_rank = jnp.cumsum(kept_flags, axis=-1) - 1
    source = jnp.where(kept_flags == 1, slot_rank, capacity)
    padded = jnp.concatenate([packed, jnp.zeros((1,) + packed.shape[1:], packed.dtype)], axis=0)
    return jnp.take(padded, source, axis=0)


def per_device(
    tokens, out_grad, gate_weight, up_weight, down_weight, gate_mask, up_mask, down_mask
):
    tok_rows = tokens.shape[0]
    owners = lax.axis_size("fsdp")
    row_blocks = gate_weight.shape[0] // BLOCK
    col_blocks = gate_weight.shape[1] // BLOCK
    region = row_blocks * col_blocks
    capacity = region * 5 // 8
    fsdp_index = lax.axis_index("fsdp")
    tensor_index = lax.axis_index("tensor")
    block_ids = jnp.arange(region, dtype=jnp.int32)

    def gate_layout(mask_blocks):
        band = lax.dynamic_slice_in_dim(mask_blocks, tensor_index * col_blocks, col_blocks, 1)
        return band.reshape(owners, region)

    down_band = lax.dynamic_slice_in_dim(down_mask, tensor_index * col_blocks, col_blocks, 0)
    down_flags = (
        down_band.reshape(col_blocks, owners, row_blocks).transpose(1, 0, 2).reshape(owners, region)
    )
    gate_flags = gate_layout(gate_mask)
    up_flags = gate_layout(up_mask)
    down_d_of = block_ids % row_blocks
    down_f_of = block_ids // row_blocks

    def own_row(kept_flags):
        return lax.dynamic_index_in_dim(kept_flags, fsdp_index, 0, keepdims=False)

    gate_local = (
        gate_weight.reshape(row_blocks, BLOCK, col_blocks, BLOCK)
        .transpose(0, 2, 1, 3)
        .reshape(region, BLOCK, BLOCK)
    )
    up_local = (
        up_weight.reshape(row_blocks, BLOCK, col_blocks, BLOCK)
        .transpose(0, 2, 1, 3)
        .reshape(region, BLOCK, BLOCK)
    )
    down_local = (
        down_weight.reshape(col_blocks, BLOCK, row_blocks, BLOCK)
        .transpose(0, 2, 1, 3)
        .reshape(region, BLOCK, BLOCK)
    )
    gate_pack = pack_blocks(gate_local, own_row(gate_flags), capacity)
    up_pack = pack_blocks(up_local, own_row(up_flags), capacity)
    down_pack = pack_blocks(down_local, own_row(down_flags), capacity)
    gate_all, up_all, down_all = (
        lax.all_gather(gate_pack, "fsdp", axis=0, tiled=True),
        lax.all_gather(up_pack, "fsdp", axis=0, tiled=True),
        lax.all_gather(down_pack, "fsdp", axis=0, tiled=True),
    )
    tokens_full, grad_full = (
        lax.all_gather(tokens, "tensor", axis=1, tiled=True),
        lax.all_gather(out_grad, "tensor", axis=1, tiled=True),
    )
    width = tokens_full.shape[1]
    hidden_width = col_blocks * BLOCK

    def dense_in(packed_all, kept_flags):
        blocks = jax.vmap(unpack_blocks)(
            packed_all.reshape(owners, capacity, BLOCK, BLOCK), kept_flags
        )
        blocks = blocks.reshape(owners, row_blocks, col_blocks, BLOCK, BLOCK).transpose(
            0, 1, 3, 2, 4
        )
        return blocks.reshape(width, hidden_width)

    gate_dense = dense_in(gate_all, gate_flags)
    up_dense = dense_in(up_all, up_flags)
    down_blocks = jax.vmap(unpack_blocks)(
        down_all.reshape(owners, capacity, BLOCK, BLOCK), down_flags
    )
    down_dense = down_blocks.reshape(owners, col_blocks, row_blocks, BLOCK, BLOCK).transpose(
        1, 3, 0, 2, 4
    )
    down_dense = down_dense.reshape(hidden_width, width)
    gate_pre = jnp.dot(tokens_full, gate_dense, preferred_element_type=jnp.float32)
    up_pre = jnp.dot(tokens_full, up_dense, preferred_element_type=jnp.float32)
    hidden_grad = lax.dot_general(
        grad_full, down_dense, (((1,), (1,)), ((), ())), preferred_element_type=jnp.float32
    )
    gate_sig = jax.nn.sigmoid(gate_pre)
    gate_act = gate_pre * gate_sig
    hidden = (gate_act * up_pre).astype(jnp.bfloat16)
    gate_grad = (hidden_grad * up_pre * (gate_sig * (1.0 + gate_pre * (1.0 - gate_sig)))).astype(
        jnp.bfloat16
    )
    up_grad = (hidden_grad * gate_act).astype(jnp.bfloat16)
    term = lax.dot_general(
        gate_dense, gate_grad, (((1,), (1,)), ((), ())), preferred_element_type=jnp.float32
    )
    input_term_sum = lax.psum_scatter(
        (
            term
            + lax.dot_general(
                up_dense, up_grad, (((1,), (1,)), ((), ())), preferred_element_type=jnp.float32
            )
        ).astype(jnp.bfloat16),
        "tensor",
        scatter_dimension=0,
        tiled=True,
    ).astype(jnp.float32)
    input_grad = input_term_sum.T.astype(jnp.bfloat16)
    own_down = own_row(down_flags)
    grad_blocks = grad_full.reshape(tok_rows, width // BLOCK, BLOCK)
    down_d, down_f, down_fill = slot_table(down_flags, down_d_of, down_f_of, capacity, row_blocks)
    hidden_blocks = hidden.reshape(tok_rows, col_blocks, BLOCK)
    chosen_hidden = jnp.take(hidden_blocks, down_f, axis=1)
    chosen_grad = jnp.take(grad_blocks, down_d, axis=1)
    partial_value = jnp.einsum(
        "tni,tnj->nij", chosen_hidden, chosen_grad, preferred_element_type=jnp.float32
    )
    partial_value = partial_value * down_fill[:, None, None].astype(jnp.float32)
    summed = lax.psum_scatter(
        partial_value.reshape(owners, capacity, BLOCK, BLOCK).astype(jnp.bfloat16),
        "fsdp",
        scatter_dimension=0,
        tiled=True,
    ).astype(jnp.float32)[0]
    dense_blocks = unpack_blocks(summed, own_down)
    down_grad = dense_blocks.reshape(col_blocks, row_blocks, BLOCK, BLOCK).transpose(0, 2, 1, 3)
    down_grad = down_grad.reshape(col_blocks * BLOCK, row_blocks * BLOCK).astype(jnp.bfloat16)
    return (input_grad, down_grad)


def solution(mesh):
    return jax.shard_map(
        per_device,
        mesh=mesh,
        in_specs=(
            P("fsdp", "tensor"),
            P("fsdp", "tensor"),
            P("fsdp", "tensor"),
            P("fsdp", "tensor"),
            P("tensor", "fsdp"),
            P(),
            P(),
            P(),
        ),
        out_specs=(P("fsdp", "tensor"), P("tensor", "fsdp")),
        check_vma=False,
    )
```

profile of v0, /device:TPU:0, one launch (start us, length us, event | category | flops | bytes accessed | tf_op | source)
XLA Modules:
  0.0 543.8 jit_solution(13178667264627739655)
XLA Ops:
  8.0 3.6 copy.87
  16.1 4.6 convolution_convert_fusion
  20.9 3.6 copy.84
  28.9 4.6 convolution_convert_fusion.1
  45.9 12.0 %gather_fusion.1 = bf16[320,160,128]{2,1,0:T(8,128)(2,1)} fusion(bf16[160,32,128]{2,0,1:T(8,128)(2,1)S(1)} %copy_bitcast_fusion.1, s32[1024]{0:T(1024)S(1)} %pad_clamp_fusion.1), kind=kCustom, calls=%fused_computation.4 | custom fusion | bytes 26215680 | tf_op jit(solution)/shard_map/jit(_take)/gather | solution.py:149
  57.9 84.3 %all-gather.12.cloned.1.call-done = bf16[320,128,128]{2,0,1:T(8,128)(2,1)} async-done(((bf16[80,128,128]{2,0,1:T(8,128)(2,1)}), bf16[320,128,128]{2,0,1:T(8,128)(2,1)}) %all-gather.12.cloned.1.call-update) | async-done | bytes 10485776 | tf_op jit(solution)/shard_map/all_gather | solution.py:89
  142.2 15.5 %copy.76 = bf16[4,80,128,128]{3,2,1,0:T(8,128)(2,1)} copy(bf16[4,80,128,128]{3,1,0,2:T(8,128)(2,1)} %bitcast.177) | data formatting | bytes 20971520 | tf_op jit(solution)/shard_map/reshape | solution.py:101
  157.7 10.4 %concatenate.16 = bf16[4,81,128,128]{3,2,1,0:T(8,128)(2,1)} pad(bf16[4,80,128,128]{3,2,1,0:T(8,128)(2,1)} %copy.76, bf16[]{:T(256)} %constant.129.clone.1), padding=0_0x0_1x0_0x0_0 | pad | bytes 21102594 | tf_op jit(solution)/shard_map/vmap()/concatenate | solution.py:36
  168.1 14.8 %gather_fusion.5 = bf16[512,128,128]{2,1,0:T(8,128)(2,1)} fusion(bf16[4,81,128,128]{3,2,1,0:T(8,128)(2,1)} %concatenate.16, s32[512]{0:T(512)S(1)} %get-tuple-element.12), kind=kCustom, calls=%fused_computation.2.clone | custom fusion | bytes 33558528 | tf_op jit(solution)/shard_map/vmap(jit(_take))/gather | solution.py:37
  182.9 9.1 %broadcast_select_fusion = bf16[4,128,128,128]{3,2,1,0:T(8,128)(2,1)S(1)} fusion(bf16[4,128,128,128]{3,2,1,0:T(8,128)(2,1)} %bitcast.162, pred[4,128]{1,0:T(4,128)(4,1)S(1)} %get-tuple-element.14), kind=kLoop, calls=%fused_computation.15 | loop fusion | flops 8388608 | bytes 33554944 | tf_op jit(solution)/shard_map/vmap(jit(_take))/select_n | solution.py:37
  192.0 12.4 %copy.77 = bf16[4,8,128,16,128]{4,3,2,1,0:T(8,128)(2,1)} copy(bf16[4,8,128,16,128]{4,2,3,1,0:T(8,128)(2,1)S(1)} %bitcast.163) | data formatting | bytes 33554432 | tf_op jit(solution)/shard_map/transpose | solution.py:103
  204.4 44.8 %all-gather.6.cloned.1.call-done = bf16[320,128,128]{2,0,1:T(8,128)(2,1)} async-done(((bf16[80,128,128]{2,0,1:T(8,128)(2,1)}), bf16[320,128,128]{2,0,1:T(8,128)(2,1)}) %all-gather.6.cloned.1.call-update) | async-done | bytes 10485776 | tf_op jit(solution)/shard_map/all_gather | solution.py:88
  249.2 14.7 %copy.67 = bf16[4,80,128,128]{3,2,1,0:T(8,128)(2,1)} copy(bf16[4,80,128,128]{3,1,0,2:T(8,128)(2,1)} %bitcast.179) | data formatting | bytes 20971520 | tf_op jit(solution)/shard_map/reshape | solution.py:101
  263.9 10.4 %concatenate.14 = bf16[4,81,128,128]{3,2,1,0:T(8,128)(2,1)} pad(bf16[4,80,128,128]{3,2,1,0:T(8,128)(2,1)} %copy.67, bf16[]{:T(256)} %constant.129.clone.1), padding=0_0x0_1x0_0x0_0 | pad | bytes 21102594 | tf_op jit(solution)/shard_map/vmap()/concatenate | solution.py:36
  274.3 15.2 %gather_fusion.3 = bf16[512,128,128]{2,1,0:T(8,128)(2,1)} fusion(bf16[4,81,128,128]{3,2,1,0:T(8,128)(2,1)} %concatenate.14, s32[512]{0:T(512)S(1)} %get-tuple-element.13), kind=kCustom, calls=%fused_computation.clone | custom fusion | bytes 33558528 | tf_op jit(solution)/shard_map/vmap(jit(_take))/gather | solution.py:37
  289.5 8.7 %broadcast_select_fusion.2 = bf16[4,128,128,128]{3,2,1,0:T(8,128)(2,1)S(1)} fusion(bf16[4,128,128,128]{3,2,1,0:T(8,128)(2,1)} %bitcast.160, pred[4,128]{1,0:T(4,128)(4,1)S(1)} %get-tuple-element.15), kind=kLoop, calls=%fused_computation.17 | loop fusion | flops 8388608 | bytes 33554944 | tf_op jit(solution)/shard_map/vmap(jit(_take))/select_n | solution.py:37
  298.3 12.2 %copy.68 = bf16[4,8,128,16,128]{4,3,2,1,0:T(8,128)(2,1)} copy(bf16[4,8,128,16,128]{4,2,3,1,0:T(8,128)(2,1)S(1)} %bitcast.164) | data formatting | bytes 33554432 | tf_op jit(solution)/shard_map/transpose | solution.py:103
  310.5 12.4 %fusion.34 = f32[160,2048]{1,0:T(8,128)S(1)} fusion(bf16[160,4096]{1,0:T(8,128)(2,1)} %all-gather.14.cloned.1.call-done, bf16[512,8,16,128]{3,2,1,0:T(8,128)(2,1)} %bitcast.169), kind=kOutput, calls=%fused_computation.43 | convolution fusion | flops 2684354560 | bytes 19398656 | tf_op jit(solution)/shard_map/dot_general | solution.py:117
  322.9 10.5 %fusion.37 = f32[160,2048]{1,0:T(8,128)S(1)} fusion(bf16[160,4096]{1,0:T(8,128)(2,1)S(1)} %copy-done.9, bf16[512,8,16,128]{3,2,1,0:T(8,128)(2,1)} %bitcast.167), kind=kOutput, calls=%fused_computation.44 | convolution fusion | flops 2684354560 | bytes 19398656 | tf_op jit(solution)/shard_map/dot_general | solution.py:118
  333.8 11.8 %gather_fusion = bf16[320,160,128]{2,1,0:T(8,128)(2,1)} fusion(bf16[160,16,128]{2,0,1:T(8,128)(2,1)S(1)} %copy_bitcast_fusion.2, s32[1024]{0:T(1024)S(1)} %pad_clamp_fusion.2), kind=kCustom, calls=%fused_computation.3 | custom fusion | bytes 26215680 | tf_op jit(solution)/shard_map/jit(_take)/gather | solution.py:148
  345.6 17.9 %multiply_convert_fusion = bf16[320,128,128]{2,1,0:T(8,128)(2,1)} fusion(f32[320]{0:T(512)S(1)} %convert_element_type.90, bf16[320,160,128]{2,1,0:T(8,128)(2,1)} %gather_fusion.1, pred[320]{0:T(512)(128)(4,1)S(1)} %get-tuple-element.16, bf16[320,160,128]{2,1,0:T(8,128)(2,1)} %gather_fusion, pred[320]{0:T(512)(128)(4,1)S(1)} %get-tuple-element.17), kind=kOutput, calls=%fused_computation.6 | convolution fusion | flops 1701314560 | bytes 36702080 | tf_op jit(solution)/shard_map/tni,tnj->nij/dot_general | solution.py:150
  363.8 17.2 %all-gather.8.cloned.1.call-done = bf16[320,128,128]{2,0,1:T(8,128)(2,1)} async-done(((bf16[80,128,128]{2,0,1:T(8,128)(2,1)}), bf16[320,128,128]{2,0,1:T(8,128)(2,1)}) %all-gather.8.cloned.1.call-update) | async-done | bytes 10485776 | tf_op jit(solution)/shard_map/all_gather | solution.py:90
  381.0 14.7 %copy.72 = bf16[4,80,128,128]{3,2,1,0:T(8,128)(2,1)} copy(bf16[4,80,128,128]{3,1,0,2:T(8,128)(2,1)} %bitcast.178) | data formatting | bytes 20971520 | tf_op jit(solution)/shard_map/reshape | solution.py:111
  395.7 10.7 %concatenate.15 = bf16[4,81,128,128]{3,2,1,0:T(8,128)(2,1)} pad(bf16[4,80,128,128]{3,2,1,0:T(8,128)(2,1)} %copy.72, bf16[]{:T(256)} %constant.129.clone.1), padding=0_0x0_1x0_0x0_0 | pad | bytes 21102594 | tf_op jit(solution)/shard_map/vmap()/concatenate | solution.py:36
  406.3 15.2 %gather_fusion.4 = bf16[512,128,128]{2,1,0:T(8,128)(2,1)} fusion(bf16[4,81,128,128]{3,2,1,0:T(8,128)(2,1)} %concatenate.15, s32[512]{0:T(512)S(1)} %fusion.65), kind=kCustom, calls=%fused_computation.1.clone | custom fusion | bytes 33558528 | tf_op jit(solution)/shard_map/vmap(jit(_take))/gather | solution.py:37
  421.5 9.3 %broadcast_select_fusion.1 = bf16[4,128,128,128]{3,2,1,0:T(8,128)(2,1)S(1)} fusion(bf16[4,128,128,128]{3,2,1,0:T(8,128)(2,1)} %bitcast.161, pred[4,128]{1,0:T(4,128)(4,1)S(1)} %copy-done.7), kind=kLoop, calls=%fused_computation.16 | loop fusion | flops 8388608 | bytes 33554944 | tf_op jit(solution)/shard_map/vmap(jit(_take))/select_n | solution.py:37
  430.9 11.6 %copy.73 = bf16[16,128,4,8,128]{4,3,2,1,0:T(8,128)(2,1)} copy(bf16[16,128,4,8,128]{4,1,3,0,2:T(8,128)(2,1)S(1)} %bitcast.165) | data formatting | bytes 33554432 | tf_op jit(solution)/shard_map/transpose | solution.py:113
  442.5 25.7 %reshape.322 = bf16[2048,4096]{1,0:T(8,128)(2,1)} reshape(bf16[16,128,4,8,128]{4,3,2,1,0:T(8,128)(2,1)} %copy.73) | data formatting | bytes 33554432 | tf_op jit(solution)/shard_map/reshape | solution.py:116
  468.1 9.8 %convolution_bitcast_fusion = f32[160,2048]{1,0:T(8,128)S(1)} fusion(bf16[2048,4096]{1,0:T(8,128)(2,1)} %reshape.322, bf16[160,4096]{1,0:T(8,128)(2,1)} %all-gather.10.cloned.1.call-done), kind=kOutput, calls=%fused_computation.42 | convolution fusion | flops 2684354560 | bytes 19398656 | tf_op jit(solution)/shard_map/dot_general | solution.py:119
  478.0 11.9 %fusion = f32[4096,160]{0,1:T(8,128)S(1)} fusion(bf16[512,8,16,128]{3,2,1,0:T(8,128)(2,1)} %bitcast.168, f32[160,2048]{1,0:T(8,128)S(1)} %convolution_bitcast_fusion, f32[160,2048]{1,0:T(8,128)S(1)} %fusion.34), kind=kOutput, calls=%fused_computation.7 | convolution fusion | flops 2686320640 | bytes 22020096 | tf_op jit(solution)/shard_map/dot_general | solution.py:135
  489.9 13.0 %fusion.27 = bf16[4096,160]{0,1:T(8,128)(2,1)} fusion(f32[4096,160]{0,1:T(8,128)S(1)} %fusion, bf16[512,8,16,128]{3,2,1,0:T(8,128)(2,1)} %bitcast.170, f32[160,2048]{1,0:T(8,128)S(1)} %fusion.34, f32[160,2048]{1,0:T(8,128)S(1)} %convolution_bitcast_fusion, f32[160,2048]{1,0:T(8,128)S(1)} %fusion.37), kind=kOutput, calls=%fused_computation.32 | convolution fusion | flops 2688942080 | bytes 24641536 | tf_op jit(solution)/shard_map/dot_general | solution.py:129
  518.1 18.4 %reduce-scatter.5.cloned.1.call-done = bf16[512,160]{0,1:T(8,128)(2,1)} async-done(((bf16[4096,160]{0,1:T(8,128)(2,1)}), bf16[512,160]{0,1:T(8,128)(2,1)}) %reduce-scatter.5.cloned.1.call-update) | async-done | bytes 163856 | tf_op jit(solution)/shard_map/reduce_scatter | solution.py:132
  (100 shorter events, 37.9 us)
Async XLA Ops:
  7.2 8.4 %copy-start = (s32[32,128]{1,0:T(8,128)S(1)}, s32[32,128]{1,0:T(8,128)}, u32[]{:S(2)}) copy-start(s32[32,128]{1,0:T(8,128)} %param.16) | copy-start | bytes 49156
  7.2 36.9 %all-gather.10.cloned.1.call-start = ((), (), s32[]{:S(2)}) async-start(), calls=%async_computation.4 | async-start | bytes 1474560 | tf_op jit(solution)/shard_map/all_gather | solution.py:94
  7.9 134.3 %all-gather.12.cloned.1.call-start = ((), (), s32[]{:S(2)}) async-start(), calls=%async_computation.5 | async-start | bytes 13107200 | tf_op jit(solution)/shard_map/all_gather | solution.py:89
  16.1 4.6 copy-start.2
  20.7 228.5 %all-gather.6.cloned.1.call-start = ((), (), s32[]{:S(2)}) async-start(), calls=%async_computation.2 | async-start | bytes 13107200 | tf_op jit(solution)/shard_map/all_gather | solution.py:88
  28.9 5.3 copy-start.3
  33.6 276.9 %all-gather.14.cloned.1.call-start = ((), (), s32[]{:S(2)}) async-start(), calls=%async_computation.6 | async-start | bytes 1474560 | tf_op jit(solution)/shard_map/all_gather | solution.py:93
  34.1 346.9 %all-gather.8.cloned.1.call-start = ((), (), s32[]{:S(2)}) async-start(), calls=%async_computation.3 | async-start | bytes 13107200 | tf_op jit(solution)/shard_map/all_gather | solution.py:90
  39.3 2.4 copy-start.4
  41.6 461.5 %reduce-scatter.7.cloned.1.call-start = ((), (), s32[]{:S(2)}) async-start(), calls=%async_computation.8 | async-start | bytes 13107200
  310.5 12.5 %copy-start.9 = (bf16[160,4096]{1,0:T(8,128)(2,1)S(1)}, bf16[160,4096]{1,0:T(8,128)(2,1)}, u32[]{:S(2)}) copy-start(bf16[160,4096]{1,0:T(8,128)(2,1)} %all-gather.14.cloned.1.call-done) | copy-start | bytes 3932164
  363.5 172.9 %reduce-scatter.5.cloned.1.call-start = ((), (), s32[]{:S(2)}) async-start(), calls=%async_computation.7 | async-start | bytes 1474560 | tf_op jit(solution)/shard_map/reduce_scatter | solution.py:132
  406.3 15.2 %copy-start.7 = (pred[4,128]{1,0:T(4,128)(4,1)S(1)}, pred[4,128]{1,0:T(4,128)(4,1)}, u32[]{:S(2)}) copy-start(pred[4,128]{1,0:T(4,128)(4,1)} %get-tuple-element.8) | copy-start | bytes 1540
  489.9 13.0 %copy-start.5 = (s32[128]{0:T(128)S(1)}, s32[128]{0:T(128)}, u32[]{:S(2)}) copy-start(s32[128]{0:T(128)} %copy-done.4) | copy-start | bytes 1540
  489.9 13.1 %copy-start.8 = (pred[128]{0:T(512)(128)(4,1)S(1)}, pred[128]{0:T(512)(128)(4,1)}, u32[]{:S(2)}) copy-start(pred[128]{0:T(512)(128)(4,1)} %get-tuple-element.10) | copy-start | bytes 388
  489.9 13.2 %copy-start.6 = (s32[128]{0:T(128)S(1)}, s32[128]{0:T(128)}, u32[]{:S(2)}) copy-start(s32[128]{0:T(128)} %get-tuple-element.3) | copy-start | bytes 1540
  515.0 21.5 %copy-start.1 = (s32[32,128]{1,0:T(8,128)S(1)}, s32[32,128]{1,0:T(8,128)}, u32[]{:S(2)}) copy-start(s32[32,128]{1,0:T(8,128)} %param.16) | copy-start | bytes 49156
Sparse Core Ops, SparseCore 0:
  9.6 26.1 all-gather.9
  37.6 104.5 all-gather.11
  144.1 105.0 all-gather.5
  250.6 23.4 all-gather.13
  276.4 104.5 all-gather.7
  383.9 103.5 reduce-scatter.6
  503.0 33.4 reduce-scatter.4
where the time goes:
time: 553 us; the launch traced here: 544 us
  local copies, waits for them, and re-layouts  241 us (44%)
  waiting for transfers between devices  166 us (30%)
  matrix products  87.1 us (16%)
  other arithmetic  34.6 us (6%)
  between operations  14.9 us (3%)
    all_gather x1, waiting for transfers between devices, per_device(): lax.all_gather(up_pack, 'fsdp', axis=0, tiled=True)  84.3 us
    gather x4, local copies, waits for them, and re-layouts, unpack_blocks(): return jnp.take(padded, source, axis=0)  48.4 us
    all_gather x1, waiting for transfers between devices, per_device(): lax.all_gather(gate_pack, 'fsdp', axis=0, tiled=True)  44.8 us
    concatenate x4, local copies, waits for them, and re-layouts, unpack_blocks(): jnp.concatenate([packed, jnp.zeros((1,) + packed.shape[1:], packed.dtype)...  33.4 us
    reshape x2, local copies, waits for them, and re-layouts, dense_in(): packed_all.reshape(owners, capacity, BLOCK, BLOCK)  30.2 us
    select_n x4, other arithmetic, unpack_blocks(): return jnp.take(padded, source, axis=0)  27.9 us
    reshape x1, local copies, waits for them, and re-layouts, per_device(): down_dense = down_dense.reshape(hidden_width, width)  25.7 us
    transpose x2, local copies, waits for them, and re-layouts, dense_in(): blocks.reshape(owners, row_blocks, col_blocks, BLOCK, BLOCK)  24.6 us
  transfers between devices with their start and end apart: 7, of which 4 were waited for; matrix products, arithmetic and copies ran while one was open for 67% of the time, Pallas kernels for 0%

commit v1 on v0

v1 whole, which is shorter than its diff:
```python
import jax
import jax.numpy as jnp
from jax import lax
from jax.sharding import PartitionSpec as P

BLOCK = 128
AXES = ("fsdp", "tensor")


def per_device(
    tokens, out_grad, gate_weight, up_weight, down_weight, gate_mask, up_mask, down_mask
):
    n_f = lax.axis_size("fsdp")
    n_t = lax.axis_size("tensor")
    ratio = n_t // n_f
    rows, width = tokens.shape
    row_blocks = gate_weight.shape[0] // BLOCK
    col_blocks = gate_weight.shape[1] // BLOCK
    f_index = lax.axis_index("fsdp")
    t_index = lax.axis_index("tensor")
    swap = [
        (f * n_t + ratio * a + c, a * n_t + ratio * f + c)
        for f in range(n_f)
        for a in range(n_f)
        for c in range(ratio)
    ]

    def columns_of_owner(x):
        moved = lax.ppermute(x, AXES, swap)
        pieces = lax.all_gather(moved, "tensor", axis=0)
        pieces = pieces.reshape(n_f, ratio, rows, width).transpose(0, 2, 1, 3)
        return pieces.reshape(n_f * rows, ratio * width)

    def keep(weight, mask, row_start, col_start):
        rb, cb = weight.shape[0] // BLOCK, weight.shape[1] // BLOCK
        own = lax.dynamic_slice(mask, (row_start * rb, col_start * cb), (rb, cb))
        wide = jnp.repeat(jnp.repeat(own, BLOCK, axis=0), BLOCK, axis=1)
        return jnp.where(wide == 1, weight, jnp.zeros((), weight.dtype)), wide

    x_cols = columns_of_owner(tokens)
    g_cols = columns_of_owner(out_grad)
    gate, _ = keep(gate_weight, gate_mask, f_index, t_index)
    up, _ = keep(up_weight, up_mask, f_index, t_index)
    down, down_wide = keep(down_weight, down_mask, t_index, f_index)

    def owner_sum(part):
        return lax.psum_scatter(
            part.astype(jnp.bfloat16), "fsdp", scatter_dimension=0, tiled=True
        ).astype(jnp.float32)

    gate_pre = owner_sum(jnp.dot(x_cols, gate, preferred_element_type=jnp.float32))
    up_pre = owner_sum(jnp.dot(x_cols, up, preferred_element_type=jnp.float32))
    hidden_grad = owner_sum(
        lax.dot_general(
            g_cols, down, (((1,), (1,)), ((), ())), preferred_element_type=jnp.float32
        )
    )
    sig = jax.nn.sigmoid(gate_pre)
    act = gate_pre * sig
    hidden = (act * up_pre).astype(jnp.bfloat16)
    gate_grad = (hidden_grad * up_pre * (sig * (1.0 + gate_pre * (1.0 - sig)))).astype(jnp.bfloat16)
    up_grad = (hidden_grad * act).astype(jnp.bfloat16)

    gate_grad = lax.all_gather(gate_grad, "fsdp", axis=0, tiled=True)
    up_grad = lax.all_gather(up_grad, "fsdp", axis=0, tiled=True)
    hidden = lax.all_gather(hidden, "fsdp", axis=0, tiled=True)
    term = lax.dot_general(
        gate_grad, gate, (((1,), (1,)), ((), ())), preferred_element_type=jnp.float32
    ) + lax.dot_general(
        up_grad, up, (((1,), (1,)), ((), ())), preferred_element_type=jnp.float32
    )
    term = term.astype(jnp.bfloat16).reshape(n_f, rows, ratio, width).transpose(0, 2, 1, 3)
    term = term.reshape(n_t, rows, width)
    own_term = lax.psum_scatter(term, "tensor", scatter_dimension=0, tiled=False)
    input_grad = lax.ppermute(own_term, AXES, swap)
    down_grad = lax.dot_general(
        hidden, g_cols, (((0,), (0,)), ((), ())), preferred_element_type=jnp.float32
    )
    down_grad = jnp.where(down_wide == 1, down_grad, 0.0).astype(jnp.bfloat16)
    return (input_grad, down_grad)


def solution(mesh):
    return jax.shard_map(
        per_device,
        mesh=mesh,
        in_specs=(
            P("fsdp", "tensor"),
            P("fsdp", "tensor"),
            P("fsdp", "tensor"),
            P("fsdp", "tensor"),
            P("tensor", "fsdp"),
            P(),
            P(),
            P(),
        ),
        out_specs=(P("fsdp", "tensor"), P("tensor", "fsdp")),
        check_vma=False,
    )
```

time: 553 us -> 392 us (0.71); the launches traced: 544 us -> 392 us
  local copies, waits for them, and re-layouts: 241 us -> 45.3 us
  waiting for transfers between devices: 166 us -> 284 us
  matrix products: 87.1 us -> 38.7 us
  other arithmetic: 34.6 us -> 5.15 us
    reduce_scatter x1 -> x4, waiting for transfers between devices: 18.4 us -> 131 us  [the longest x3 98.3 us: owner_sum(): lax.psum_scatter(part.astype(jnp.bfloat16), 'fsdp', scatter_dimension=0,...]
    gather x6 -> x0, local copies, waits for them, and re-layouts: 72.2 us -> none  [the longest x4 48.4 us: unpack_blocks(): return jnp.take(padded, source, axis=0)]
    reshape x10 -> x3, local copies, waits for them, and re-layouts: 72.8 us -> 8.88 us  [the longest x2 5.33 us: columns_of_owner(): pieces = pieces.reshape(n_f, ratio, rows, width).transpose(0, 2, 1, 3)]
    dot_general x9 -> x6, matrix products: 87.1 us -> 38.7 us  [the longest x1 8.03 us: per_device(): lax.dot_general(up_grad, up, (((1,), (1,)), ((), ())), preferred_element_...]
    transpose x9 -> x1, local copies, waits for them, and re-layouts: 44.3 us -> 1.29 us  [per_device(): term.astype(jnp.bfloat16).reshape(n_f, rows, ratio, width)]
    concatenate x4 -> x0, local copies, waits for them, and re-layouts: 33.4 us -> none  [unpack_blocks(): jnp.concatenate([packed, jnp.zeros((1,) + packed.shape[1:], packed.dtype)...]
    select_n x8 -> x0, other arithmetic: 27.9 us -> none  [the longest x4 27.9 us: unpack_blocks(): return jnp.take(padded, source, axis=0)]
    broadcast_in_dim x0 -> x6, local copies, waits for them, and re-layouts: none -> 20.4 us  [keep(): wide = jnp.repeat(jnp.repeat(own, BLOCK, axis=0), BLOCK, axis=1)]
  transfers between devices with their start and end apart: 7 -> 12, of which waited for: 4 -> 8; matrix products, arithmetic and copies ran while one was open for 67% -> 17% of each run, Pallas kernels for 0% -> 0%
where the time goes in v1:
time: 392 us
  waiting for transfers between devices  284 us (72%)
  local copies, waits for them, and re-layouts  45.3 us (12%)
  matrix products  38.7 us (10%)
  between operations  14 us (4%)
  starting transfers between devices  5.26 us (1%)
  other arithmetic  5.15 us (1%)
    reduce_scatter x3, waiting for transfers between devices, owner_sum(): lax.psum_scatter(part.astype(jnp.bfloat16), 'fsdp', scatter_dimension=0,...  98.3 us
    all_gather x1, waiting for transfers between devices, per_device(): hidden = lax.all_gather(hidden, 'fsdp', axis=0, tiled=True)  40.4 us
    all_gather x1, waiting for transfers between devices, per_device(): up_grad = lax.all_gather(up_grad, 'fsdp', axis=0, tiled=True)  39 us
    all_gather x2, waiting for transfers between devices, columns_of_owner(): pieces = lax.all_gather(moved, 'tensor', axis=0)  38.3 us
    all_gather x1, waiting for transfers between devices, per_device(): gate_grad = lax.all_gather(gate_grad, 'fsdp', axis=0, tiled=True)  33.5 us
    reduce_scatter x1, waiting for transfers between devices, per_device(): lax.psum_scatter(term, 'tensor', scatter_dimension=0, tiled=False)  32.6 us
    broadcast_in_dim x6, local copies, waits for them, and re-layouts, keep(): wide = jnp.repeat(jnp.repeat(own, BLOCK, axis=0), BLOCK, axis=1)  20.4 us
    unnamed x28, local copies, waits for them, and re-layouts  14.6 us
  transfers between devices with their start and end apart: 12, of which 8 were waited for; matrix products, arithmetic and copies ran while one was open for 17% of the time, Pallas kernels for 0%

profile of v1, /device:TPU:0, one launch (start us, length us, event | category | flops | bytes accessed | tf_op | source)
XLA Modules:
  0.0 392.0 jit_solution(1266222010133324417)
XLA Ops:
  7.2 1.6 collective-permute-start.1
  9.5 1.6 collective-permute-start
  11.8 0.8 dynamic-slice_compare_fusion
  12.6 38.3 %all-gather.16.cloned.1.call-done = bf16[1280,512]{1,0:T(8,128)(2,1)} async-done(((bf16[160,512]{1,0:T(8,128)(2,1)}), bf16[1280,512]{1,0:T(8,128)(2,1)}) %all-gather.16.cloned.1.call-update) | async-done | bytes 1310736 | tf_op jit(solution)/shard_map/all_gather | solution.py:30
  51.0 2.7 copy.26
  54.0 6.9 %broadcast_in_dim.38 = pred[1024,16,128]{2,1,0:T(8,128)(4,1)S(1)} broadcast(pred[1024,16]{1,0:T(8,128)(4,1)S(1)} %bitcast.70), dimensions={0,1} | broadcast | bytes 2113536 | tf_op jit(solution)/shard_map/broadcast_in_dim | solution.py:37
  61.0 1.3 copy-done.2
  62.3 4.5 %fusion.3 = bf16[640,2048]{0,1:T(8,128)(2,1)S(1)} fusion(bf16[640,1024]{1,0:T(8,128)(2,1)S(1)} %bitcast.67, bf16[1024,2048]{1,0:T(8,128)(2,1)S(1)} %copy-done.10, pred[128,8,16,128]{3,2,1,0:T(8,128)(4,1)S(1)} %bitcast.59), kind=kOutput, calls=%fused_computation.9 | convolution fusion | flops 2687762432 | bytes 10223616 | tf_op jit(solution)/shard_map/dot_general | solution.py:51
  66.8 2.7 copy.34
  69.7 6.9 %broadcast_in_dim.35 = pred[1024,16,128]{2,1,0:T(8,128)(4,1)S(1)} broadcast(pred[1024,16]{1,0:T(8,128)(4,1)S(1)} %bitcast.71), dimensions={0,1} | broadcast | bytes 2113536 | tf_op jit(solution)/shard_map/broadcast_in_dim | solution.py:37
  76.6 1.3 copy-done.4
  77.9 6.5 %fusion.2 = bf16[640,2048]{0,1:T(8,128)(2,1)S(1)} fusion(bf16[640,1024]{1,0:T(8,128)(2,1)} %bitcast.68, bf16[1024,2048]{1,0:T(8,128)(2,1)} %param.11, pred[128,8,16,128]{3,2,1,0:T(8,128)(4,1)S(1)} %bitcast.61), kind=kOutput, calls=%fused_computation.8 | convolution fusion | flops 2687762432 | bytes 10223616 | tf_op jit(solution)/shard_map/dot_general | solution.py:52
  84.4 2.6 copy.32
  88.1 2.7 copy.24
  91.2 6.4 %broadcast_in_dim.32 = pred[2048,8,128]{2,1,0:T(8,128)(4,1)S(1)} broadcast(pred[2048,8]{1,0:T(8,128)(4,1)S(1)} %bitcast.69), dimensions={0,1} | broadcast | bytes 2113536 | tf_op jit(solution)/shard_map/broadcast_in_dim | solution.py:37
  97.6 1.3 copy-done
  99.0 4.0 %fusion.4 = bf16[640,2048]{0,1:T(8,128)(2,1)S(1)} fusion(bf16[640,1024]{1,0:T(8,128)(2,1)S(1)} %bitcast.63, bf16[2048,1024]{1,0:T(8,128)(2,1)S(1)} %copy-done.9, pred[256,8,8,128]{3,2,1,0:T(8,128)(4,1)S(1)} %bitcast.57), kind=kOutput, calls=%fused_computation.10 | convolution fusion | flops 2687762432 | bytes 10223616 | tf_op jit(solution)/shard_map/dot_general | solution.py:54
  102.9 2.7 copy.30
  105.7 12.8 %reduce-scatter.17.cloned.1.call-done = bf16[160,2048]{1,0:T(8,128)(2,1)} async-done(((bf16[640,2048]{1,0:T(8,128)(2,1)}), bf16[160,2048]{1,0:T(8,128)(2,1)}) %reduce-scatter.17.cloned.1.call-update) | async-done | bytes 655376 | tf_op jit(solution)/shard_map/reduce_scatter | solution.py:47
  118.6 43.0 %reduce-scatter.15.cloned.1.call-done = bf16[160,2048]{1,0:T(8,128)(2,1)} async-done(((bf16[640,2048]{1,0:T(8,128)(2,1)}), bf16[160,2048]{1,0:T(8,128)(2,1)}) %reduce-scatter.15.cloned.1.call-update) | async-done | bytes 655376 | tf_op jit(solution)/shard_map/reduce_scatter | solution.py:47
  161.6 42.4 %reduce-scatter.13.cloned.1.call-done = bf16[160,2048]{1,0:T(8,128)(2,1)} async-done(((bf16[640,2048]{1,0:T(8,128)(2,1)}), bf16[160,2048]{1,0:T(8,128)(2,1)}) %reduce-scatter.13.cloned.1.call-update) | async-done | bytes 655376 | tf_op jit(solution)/shard_map/reduce_scatter | solution.py:47
  204.0 3.6 fusion.15
  208.4 39.0 %all-gather.10.cloned.1.call-done = bf16[640,2048]{1,0:T(8,128)(2,1)} async-done(((bf16[160,2048]{1,0:T(8,128)(2,1)}), bf16[640,2048]{1,0:T(8,128)(2,1)}) %all-gather.10.cloned.1.call-update) | async-done | bytes 2621456 | tf_op jit(solution)/shard_map/all_gather | solution.py:65
  247.4 8.0 %fusion.5 = f32[640,1024]{1,0:T(8,128)} fusion(bf16[640,2048]{1,0:T(8,128)(2,1)} %all-gather.10.cloned.1.call-done, bf16[1024,2048]{1,0:T(8,128)(2,1)} %param.11, pred[128,8,16,128]{3,2,1,0:T(8,128)(4,1)} %bitcast.62), kind=kOutput, calls=%fused_computation.12 | convolution fusion | flops 2686451712 | bytes 11534336 | tf_op jit(solution)/shard_map/dot_general | solution.py:69
  255.4 33.5 %all-gather.8.cloned.1.call-done = bf16[640,2048]{1,0:T(8,128)(2,1)} async-done(((bf16[160,2048]{1,0:T(8,128)(2,1)}), bf16[640,2048]{1,0:T(8,128)(2,1)}) %all-gather.8.cloned.1.call-update) | async-done | bytes 2621456 | tf_op jit(solution)/shard_map/all_gather | solution.py:64
  288.9 7.8 %add_convert_fusion = bf16[640,1024]{1,0:T(8,128)(2,1)} fusion(f32[640,1024]{1,0:T(8,128)} %fusion.5, bf16[640,2048]{1,0:T(8,128)(2,1)} %all-gather.8.cloned.1.call-done, bf16[1024,2048]{1,0:T(8,128)(2,1)} %param.10, pred[128,8,16,128]{3,2,1,0:T(8,128)(4,1)S(1)} %bitcast.60), kind=kOutput, calls=%fused_computation.11 | convolution fusion | flops 2687762432 | bytes 12845056 | tf_op jit(solution)/shard_map/dot_general | solution.py:67
  296.7 3.6 reshape.44
  300.3 1.3 copy.29
  302.4 32.6 %reduce-scatter.11.cloned.1.call-done = bf16[1,160,512]{2,1,0:T(8,128)(2,1)} async-done(((bf16[8,160,512]{2,1,0:T(8,128)(2,1)}), bf16[1,160,512]{2,1,0:T(8,128)(2,1)}) %reduce-scatter.11.cloned.1.call-update) | async-done | bytes 163856 | tf_op jit(solution)/shard_map/reduce_scatter | solution.py:74
  334.9 1.6 collective-permute-start.2
  336.5 40.4 %all-gather.12.cloned.1.call-done = bf16[640,2048]{1,0:T(8,128)(2,1)} async-done(((bf16[160,2048]{1,0:T(8,128)(2,1)}), bf16[640,2048]{1,0:T(8,128)(2,1)}) %all-gather.12.cloned.1.call-update) | async-done | bytes 2621456 | tf_op jit(solution)/shard_map/all_gather | solution.py:66
  376.9 7.9 %select_convert_fusion = bf16[2048,1024]{1,0:T(8,128)(2,1)} fusion(pred[256,8,8,128]{3,2,1,0:T(8,128)(4,1)S(1)} %bitcast.58, bf16[640,2048]{1,0:T(8,128)(2,1)} %all-gather.12.cloned.1.call-done, bf16[640,1024]{1,0:T(8,128)(2,1)} %bitcast.64), kind=kOutput, calls=%fused_computation | convolution fusion | flops 2688548864 | bytes 10223616 | tf_op jit(solution)/shard_map/dot_general | solution.py:76
  (49 shorter events, 5.7 us)
Async XLA Ops:
  7.2 43.8 %all-gather.16.cloned.1.call-start = ((), (), s32[]{:S(2)}) async-start(), calls=%async_computation.9 | async-start | bytes 1474560 | tf_op jit(solution)/shard_map/all_gather | solution.py:30
  7.2 1.6 collective-permute-start.1
  8.8 0.7 copy-start.8
  9.5 78.7 %all-gather.14.cloned.1.call-start = ((), (), s32[]{:S(2)}) async-start(), calls=%async_computation.8 | async-start | bytes 1474560 | tf_op jit(solution)/shard_map/all_gather | solution.py:30
  9.5 1.6 collective-permute-start
  11.1 0.7 copy-start.7
  11.8 106.8 %reduce-scatter.17.cloned.1.call-start = ((), (), s32[]{:S(2)}) async-start(), calls=%async_computation.12 | async-start | bytes 3276800 | tf_op jit(solution)/shard_map/reduce_scatter | solution.py:47
  53.6 8.6 %copy-start.10 = (bf16[1024,2048]{1,0:T(8,128)(2,1)S(1)}, bf16[1024,2048]{1,0:T(8,128)(2,1)}, u32[]{:S(2)}) copy-start(bf16[1024,2048]{1,0:T(8,128)(2,1)} %param.10) | copy-start | bytes 12582916
  54.0 7.0 %copy-start.6 = (bf16[80,8,2,512]{3,1,2,0:T(8,128)(2,1)}, bf16[80,8,2,512]{3,1,2,0:T(8,128)(2,1)S(1)}, u32[]{:S(2)}) copy-start(bf16[80,8,2,512]{3,1,2,0:T(8,128)(2,1)S(1)} %copy.39) | copy-start | bytes 3932164
  61.0 1.3 copy-start.2
  69.6 92.0 %reduce-scatter.15.cloned.1.call-start = ((), (), s32[]{:S(2)}) async-start(), calls=%async_computation.11 | async-start | bytes 3276800 | tf_op jit(solution)/shard_map/reduce_scatter | solution.py:47
  76.6 1.3 copy-start.4
  87.0 117.0 %reduce-scatter.13.cloned.1.call-start = ((), (), s32[]{:S(2)}) async-start(), calls=%async_computation.10 | async-start | bytes 3276800 | tf_op jit(solution)/shard_map/reduce_scatter | solution.py:47
  90.8 8.1 %copy-start.9 = (bf16[2048,1024]{1,0:T(8,128)(2,1)S(1)}, bf16[2048,1024]{1,0:T(8,128)(2,1)}, u32[]{:S(2)}) copy-start(bf16[2048,1024]{1,0:T(8,128)(2,1)} %param.12) | copy-start | bytes 12582916
  91.1 6.5 %copy-start.5 = (bf16[80,8,2,512]{3,1,2,0:T(8,128)(2,1)}, bf16[80,8,2,512]{3,1,2,0:T(8,128)(2,1)S(1)}, u32[]{:S(2)}) copy-start(bf16[80,8,2,512]{3,1,2,0:T(8,128)(2,1)S(1)} %copy.37) | copy-start | bytes 3932164
  97.6 1.3 copy-start
  105.7 141.8 %all-gather.10.cloned.1.call-start = ((), (), s32[]{:S(2)}) async-start(), calls=%async_computation.5 | async-start | bytes 3276800 | tf_op jit(solution)/shard_map/all_gather | solution.py:65
  207.6 81.3 %all-gather.8.cloned.1.call-start = ((), (), s32[]{:S(2)}) async-start(), calls=%async_computation.4 | async-start | bytes 3276800 | tf_op jit(solution)/shard_map/all_gather | solution.py:64
  208.4 80.6 %copy-start.3 = (pred[1024,16,128]{2,1,0:T(8,128)(4,1)S(1)}, pred[1024,16,128]{2,1,0:T(8,128)(4,1)}, u32[]{:S(2)}) copy-start(pred[1024,16,128]{2,1,0:T(8,128)(4,1)} %copy-done.2) | copy-start | bytes 6291460
  208.4 126.5 %reduce-scatter.11.cloned.1.call-start = ((), (), s32[]{:S(2)}) async-start(), calls=%async_computation.6 | async-start | bytes 1474560 | tf_op jit(solution)/shard_map/reduce_scatter | solution.py:74
  300.3 76.6 %copy-start.1 = (pred[2048,8,128]{2,1,0:T(8,128)(4,1)S(1)}, pred[2048,8,128]{2,1,0:T(8,128)(4,1)}, u32[]{:S(2)}) copy-start(pred[2048,8,128]{2,1,0:T(8,128)(4,1)} %copy-done) | copy-start | bytes 6291460
  301.6 75.3 %all-gather.12.cloned.1.call-start = ((), (), s32[]{:S(2)}) async-start(), calls=%async_computation.7 | async-start | bytes 3276800 | tf_op jit(solution)/shard_map/all_gather | solution.py:66
  334.9 49.9 %collective-permute-start.2 = (bf16[160,512]{1,0:T(8,128)(2,1)}, bf16[160,512]{1,0:T(8,128)(2,1)S(1)}, u32[]{:S(2)}, u32[]{:S(2)}) collective-permute-start(bf16[160,512]{1,0:T(8,128)(2,1)} %bitcast.72), channel_id=1, source_target_pairs={{0,0},{1,1},{2,8},{3,9},{4,16},{5,17},{6,24},{7,25},{8,2},{9,3},{1... | collective-permute-start | bytes 491528 | tf_op jit(solution)/shard_map/ppermute | solution.py:75
Sparse Core Ops, SparseCore 0:
  10.2 40.7 all-gather.15
  52.6 23.8 all-gather.13
  79.5 39.0 reduce-scatter.16
  122.0 39.5 reduce-scatter.14
  164.4 39.5 reduce-scatter.12
  207.7 39.6 all-gather.9
  249.3 39.6 all-gather.7
  301.7 33.1 reduce-scatter.10
  336.8 40.0 all-gather.11

commit v2 on v1

v2 whole, which is shorter than its diff:
```python
import functools

import jax
import jax.numpy as jnp
from jax import lax
from jax.experimental import pallas as pl
from jax.experimental.pallas import tpu as pltpu
from jax.sharding import PartitionSpec as P

BLOCK = 128
AXES = ("fsdp", "tensor")
VMEM_BYTES = 48 * 1024 * 1024


def keep_blocks(weight, flag_of):
    rows = []
    for i in range(weight.shape[0] // BLOCK):
        row = []
        for j in range(weight.shape[1] // BLOCK):
            block = weight[i * BLOCK : (i + 1) * BLOCK, j * BLOCK : (j + 1) * BLOCK]
            row.append(jnp.where(flag_of(i, j) == 1, block, jnp.zeros_like(block)))
        rows.append(jnp.concatenate(row, axis=1))
    return jnp.concatenate(rows, axis=0)


def forward_kernel(order, half, transposed, place, flags, own, other, weight, kept, sent, x_all):
    groups, rows, width = own.shape
    step = pl.program_id(0)
    tile = kept.shape[2]
    blocks = tile // BLOCK

    @pl.when(step == 0)
    def _():
        low = place[1] == 0
        for i in range(groups):
            k = order[i] ^ place[0]
            a, b = own[k], other[k]
            x_all[i * rows : (i + 1) * rows, :width] = jnp.where(low, a, b)
            x_all[i * rows : (i + 1) * rows, width:] = jnp.where(low, b, a)

    first = (half * pl.num_programs(0) + step) * blocks
    if transposed:
        masked = keep_blocks(weight[...], lambda i, j: flags[first + i, j])
        dims = (((1,), (1,)), ((), ()))
    else:
        masked = keep_blocks(weight[...], lambda i, j: flags[i, first + j])
        dims = (((1,), (0,)), ((), ()))
    part = lax.dot_general(x_all[...], masked, dims, preferred_element_type=jnp.float32)
    part = part.reshape(groups, rows, tile)
    kept[...] = part[: groups // 2]
    sent[...] = part[groups // 2 :].astype(jnp.bfloat16)


def forward_half(place, flags, own, other, weight, order, half, transposed):
    groups, rows, width = own.shape
    inner = 2 * width
    span = weight.shape[0 if transposed else 1] // 2
    tile = min(512, span)
    steps = span // tile
    full = pl.BlockSpec((groups, rows, width), lambda j, *_: (0, 0, 0))
    if transposed:
        weight_spec = pl.BlockSpec((tile, inner), lambda j, *_: (half * steps + j, 0))
    else:
        weight_spec = pl.BlockSpec((inner, tile), lambda j, *_: (0, half * steps + j))
    out_spec = pl.BlockSpec((groups // 2, rows, tile), lambda j, *_: (0, 0, j))
    shape = (groups // 2, rows, span)
    return pl.pallas_call(
        functools.partial(forward_kernel, order, half, transposed),
        grid_spec=pltpu.PrefetchScalarGridSpec(
            num_scalar_prefetch=2,
            grid=(steps,),
            in_specs=[full, full, weight_spec],
            out_specs=[out_spec, out_spec],
            scratch_shapes=[pltpu.VMEM((groups * rows, inner), jnp.bfloat16)],
        ),
        out_shape=[
            jax.ShapeDtypeStruct(shape, jnp.float32),
            jax.ShapeDtypeStruct(shape, jnp.bfloat16),
        ],
        compiler_params=pltpu.CompilerParams(vmem_limit_bytes=VMEM_BYTES),
        cost_estimate=pl.CostEstimate(
            flops=2 * groups * rows * inner * span,
            bytes_accessed=2 * inner * (groups * rows + span) + 3 * groups * rows * span,
            transcendentals=0,
        ),
    )(place, flags, own, other, weight)


def input_kernel(groups, own_side, place, gate_flags, up_flags, *refs):
    count = 2 * groups
    pieces, (gate, up, out, stacked) = refs[: 2 * count], refs[2 * count :]
    rows, span = pieces[0].shape
    tile = out.shape[2]
    step = pl.program_id(0)
    tiles = pl.num_programs(0)

    @pl.when(step == 0)
    def _():
        for side in range(2):
            for half in range(2):
                for rel in range(groups):
                    piece = pieces[side * count + half * groups + rel]
                    start = (2 * side + half) * span
                    stacked[rel ^ place[0], :, start : start + span] = piece[...]

    side_of = place[1] if own_side else 1 - place[1]
    first = (side_of * tiles + step) * (tile // BLOCK)
    grads = stacked[...].reshape(groups * rows, 4 * span)
    dims = (((1,), (1,)), ((), ()))
    gate_kept = keep_blocks(gate[...], lambda i, j: gate_flags[first + i, j])
    up_kept = keep_blocks(up[...], lambda i, j: up_flags[first + i, j])
    total = lax.dot_general(
        grads[:, : 2 * span], gate_kept, dims, preferred_element_type=jnp.float32
    ) + lax.dot_general(grads[:, 2 * span :], up_kept, dims, preferred_element_type=jnp.float32)
    out[...] = total.reshape(groups, rows, tile).astype(out.dtype)


def input_side(place, gate_flags, up_flags, pieces, gate, up, groups, width, own_side):
    rows, span = pieces[0].shape
    tile = min(256, width)
    tiles = width // tile
    whole = pl.BlockSpec((rows, span), lambda j, *_: (0, 0))

    def weight_block(j, place, *_):
        side = place[1] if own_side else 1 - place[1]
        return (side * tiles + j, 0)

    weight_spec = pl.BlockSpec((tile, gate.shape[1]), weight_block)
    return pl.pallas_call(
        functools.partial(input_kernel, groups, own_side),
        grid_spec=pltpu.PrefetchScalarGridSpec(
            num_scalar_prefetch=3,
            grid=(tiles,),
            in_specs=[whole] * len(pieces) + [weight_spec, weight_spec],
            out_specs=pl.BlockSpec((groups, rows, tile), lambda j, *_: (0, 0, j)),
            scratch_shapes=[pltpu.VMEM((groups, rows, 4 * span), jnp.bfloat16)],
        ),
        out_shape=jax.ShapeDtypeStruct(
            (groups, rows, width), jnp.float32 if own_side else jnp.bfloat16
        ),
        compiler_params=pltpu.CompilerParams(vmem_limit_bytes=VMEM_BYTES),
        cost_estimate=pl.CostEstimate(
            flops=2 * groups * rows * 4 * span * width,
            bytes_accessed=8 * span * (groups * rows + width) + 4 * groups * rows * width,
            transcendentals=0,
        ),
    )(place, gate_flags, up_flags, *pieces, gate, up)


def down_product(place, flags, own, other, halves):
    groups, rows, width = own.shape
    span = halves[0][0].shape[1]
    tile = min(512, span)
    steps = span // tile
    full = pl.BlockSpec((groups, rows, width), lambda j, *_: (0, 0, 0))

    def kernel(place, flags, *refs):
        first, second = refs[:groups], refs[groups : 2 * groups]
        own, other, out, hidden, grads = refs[2 * groups :]
        step = pl.program_id(0)
        blocks = tile // BLOCK

        @pl.when(step == 0)
        def _():
            low = place[1] == 0
            for rel in range(groups):
                k = rel ^ place[0]
                a, b = own[k], other[k]
                grads[rel * rows : (rel + 1) * rows, :width] = jnp.where(low, a, b)
                grads[rel * rows : (rel + 1) * rows, width:] = jnp.where(low, b, a)

        @pl.when(step < steps)
        def _():
            for rel in range(groups):
                hidden[rel * rows : (rel + 1) * rows, :] = first[rel][...]

        @pl.when(step >= steps)
        def _():
            for rel in range(groups):
                hidden[rel * rows : (rel + 1) * rows, :] = second[rel][...]

        total = lax.dot_general(
            hidden[...], grads[...], (((0,), (0,)), ((), ())), preferred_element_type=jnp.float32
        )
        out[...] = keep_blocks(total, lambda i, j: flags[step * blocks + i, j]).astype(out.dtype)

    first_spec = pl.BlockSpec((rows, tile), lambda j, *_: (0, jnp.minimum(j, steps - 1)))
    second_spec = pl.BlockSpec((rows, tile), lambda j, *_: (0, jnp.maximum(j - steps, 0)))
    return pl.pallas_call(
        kernel,
        grid_spec=pltpu.PrefetchScalarGridSpec(
            num_scalar_prefetch=2,
            grid=(2 * steps,),
            in_specs=[first_spec] * groups + [second_spec] * groups + [full, full],
            out_specs=pl.BlockSpec((tile, 2 * width), lambda j, *_: (j, 0)),
            scratch_shapes=[
                pltpu.VMEM((groups * rows, tile), jnp.bfloat16),
                pltpu.VMEM((groups * rows, 2 * width), jnp.bfloat16),
            ],
        ),
        out_shape=jax.ShapeDtypeStruct((2 * span, 2 * width), jnp.bfloat16),
        compiler_params=pltpu.CompilerParams(vmem_limit_bytes=VMEM_BYTES),
        cost_estimate=pl.CostEstimate(
            flops=8 * groups * rows * span * width,
            bytes_accessed=4 * groups * rows * (span + width) + 8 * span * width,
            transcendentals=0,
        ),
    )(place, flags, *halves[0], *halves[1], own, other)


def per_device(
    tokens, out_grad, gate_weight, up_weight, down_weight, gate_mask, up_mask, down_mask
):
    n_f = lax.axis_size("fsdp")
    n_t = lax.axis_size("tensor")
    assert n_t == 2 * n_f and n_f & (n_f - 1) == 0
    bits = n_f.bit_length() - 1
    rows, width = tokens.shape
    f_index = lax.axis_index("fsdp")
    t_index = lax.axis_index("tensor")
    owner, core = t_index // 2, t_index % 2
    place = jnp.stack([owner ^ f_index, core]).astype(jnp.int32)
    swap = [
        (f * n_t + 2 * a + c, a * n_t + 2 * f + c)
        for f in range(n_f)
        for a in range(n_f)
        for c in range(2)
    ]
    bit_orders = (tuple(range(bits)), tuple(reversed(range(bits))))

    def group_order(bit_order):
        order = []
        for i in range(n_f):
            order.append(sum(((i >> (bits - 1 - p)) & 1) << b for p, b in enumerate(bit_order)))
        return tuple(order)

    def across(x, bit):
        return lax.ppermute(x, "fsdp", [(f, f ^ (1 << bit)) for f in range(n_f)])

    def along(x, k):
        return lax.ppermute(x, "tensor", [(t, t ^ (2 * k)) for t in range(n_t)])

    def exchange(x):
        return lax.ppermute(x, "tensor", [(t, t ^ 1) for t in range(n_t)])

    def owner_columns(x):
        moved = lax.ppermute(x, AXES, swap)
        own = jnp.stack([moved] + [along(moved, k) for k in range(1, n_f)])
        return own, exchange(own)

    def own_flags(mask, weight, row, col):
        rb, cb = weight.shape[0] // BLOCK, weight.shape[1] // BLOCK
        return lax.dynamic_slice(mask, (row * rb, col * cb), (rb, cb))

    gate_flags = own_flags(gate_mask, gate_weight, f_index, t_index)
    up_flags = own_flags(up_mask, up_weight, f_index, t_index)
    down_flags = own_flags(down_mask, down_weight, t_index, f_index)

    def owner_sum(kept, sent, bit_order):
        for bit in bit_order:
            total = kept + across(sent, bit).astype(jnp.float32)
            groups = total.shape[0]
            kept, sent = total[: groups // 2], total[groups // 2 :].astype(jnp.bfloat16)
        return total[0]

    def gathered(piece, bit_order):
        held = {0: piece}
        for bit in bit_order:
            for rel in list(held):
                held[rel | 1 << bit] = across(held[rel], bit)
        return [held[rel] for rel in range(n_f)]

    def forward(columns, weight, flags, transposed):
        sums = []
        for half in range(2):
            kept, sent = forward_half(
                place, flags, *columns, weight, group_order(bit_orders[half]), half, transposed
            )
            sums.append(owner_sum(kept, sent, bit_orders[half]))
        return sums

    x_cols = owner_columns(tokens)
    g_cols = owner_columns(out_grad)
    gate_pre = forward(x_cols, gate_weight, gate_flags, False)
    up_pre = forward(x_cols, up_weight, up_flags, False)
    hidden_grad = forward(g_cols, down_weight, down_flags, True)

    gate_pieces, up_pieces, hidden_pieces = [], [], []
    for half in range(2):
        v, u, d = gate_pre[half], up_pre[half], hidden_grad[half]
        sig = jax.nn.sigmoid(v)
        act = v * sig
        hidden = (act * u).astype(jnp.bfloat16)
        gate_grad = (d * u * (sig * (1.0 + v * (1.0 - sig)))).astype(jnp.bfloat16)
        up_grad = (d * act).astype(jnp.bfloat16)
        gate_pieces += gathered(gate_grad, bit_orders[half])
        up_pieces += gathered(up_grad, bit_orders[half])
        hidden_pieces.append(gathered(hidden, bit_orders[half]))

    def side(own_side):
        return input_side(
            place,
            gate_flags,
            up_flags,
            gate_pieces + up_pieces,
            gate_weight,
            up_weight,
            n_f,
            width,
            own_side,
        )

    from_core = exchange(side(False))
    chip_sum = side(True) + from_core.astype(jnp.float32)
    to_send = chip_sum.astype(jnp.bfloat16)
    total = chip_sum[0]
    for k in range(1, n_f):
        total = total + along(to_send[k], k).astype(jnp.float32)
    input_grad = lax.ppermute(total.astype(jnp.bfloat16), AXES, swap)
    down_grad = down_product(place, down_flags, *g_cols, hidden_pieces)
    return (input_grad, down_grad)


def solution(mesh):
    return jax.shard_map(
        per_device,
        mesh=mesh,
        in_specs=(
            P("fsdp", "tensor"),
            P("fsdp", "tensor"),
            P("fsdp", "tensor"),
            P("fsdp", "tensor"),
            P("tensor", "fsdp"),
            P(),
            P(),
            P(),
        ),
        out_specs=(P("fsdp", "tensor"), P("tensor", "fsdp")),
        check_vma=False,
    )
```

time: 392 us -> 244 us (0.62)
  waiting for transfers between devices: 284 us -> 99.3 us
  starting transfers between devices: 5.26 us -> 85.8 us
  Pallas kernels: 0 us -> 41.8 us
  local copies, waits for them, and re-layouts: 45.3 us -> 4.38 us
  matrix products: 38.7 us -> 0 us
  between operations: 14 us -> 1 us
    all_gather x5 -> x0, waiting for transfers between devices: 151 us -> none  [the longest x1 40.4 us: per_device(): hidden = lax.all_gather(hidden, 'fsdp', axis=0, tiled=True)]
    reduce_scatter x4 -> x0, waiting for transfers between devices: 131 us -> none  [the longest x3 98.3 us: owner_sum(): lax.psum_scatter(part.astype(jnp.bfloat16), 'fsdp', scatter_dimension=0,...]
    ppermute x3 -> x45, waiting for transfers between devices: 0.01 us -> 99.3 us  [the longest x30 79 us: across(): return lax.ppermute(x, 'fsdp', [(f, f ^ 1 << bit) for f in range(n_f)])]
    ppermute x3 -> x45, starting transfers between devices: 4.71 us -> 85.8 us  [the longest x9 43.2 us: along(): return lax.ppermute(x, 'tensor', [(t, t ^ 2 * k) for t in range(n_t)])]
    pallas_call x0 -> x9, Pallas kernels: none -> 41.8 us  [the longest x6 22.9 us: forward_half(): pl.pallas_call(functools.partial(forward_kernel, order, half, transposed)...]
    dot_general x6 -> x0, matrix products: 38.7 us -> none  [the longest x1 8.03 us: per_device(): lax.dot_general(up_grad, up, (((1,), (1,)), ((), ())), preferred_element_...]
    broadcast_in_dim x6 -> x0, local copies, waits for them, and re-layouts: 20.4 us -> none  [keep(): wide = jnp.repeat(jnp.repeat(own, BLOCK, axis=0), BLOCK, axis=1)]
    unnamed x28 -> x6, local copies, waits for them, and re-layouts: 14.6 us -> 1.8 us
  transfers between devices with their start and end apart: 12 -> 45, of which waited for: 8 -> 18; matrix products, arithmetic and copies ran while one was open for 17% -> 5% of each run, Pallas kernels for 0% -> 15%
where the time goes in v2:
time: 244 us; the launch traced here: 241 us
  waiting for transfers between devices  99.3 us (41%)
  starting transfers between devices  85.8 us (35%)
  Pallas kernels  41.8 us (17%)
  other arithmetic  8.64 us (4%)
  local copies, waits for them, and re-layouts  4.38 us (2%)
    ppermute x30, waiting for transfers between devices, across(): return lax.ppermute(x, 'fsdp', [(f, f ^ 1 << bit) for f in range(n_f)])  79 us
    ppermute x9, starting transfers between devices, along(): return lax.ppermute(x, 'tensor', [(t, t ^ 2 * k) for t in range(n_t)])  43.2 us
    ppermute x30, starting transfers between devices, across(): return lax.ppermute(x, 'fsdp', [(f, f ^ 1 << bit) for f in range(n_f)])  38.6 us
    pallas_call x6, Pallas kernels, forward_half(): pl.pallas_call(functools.partial(forward_kernel, order, half, transposed)...  22.9 us
    ppermute x9, waiting for transfers between devices, along(): return lax.ppermute(x, 'tensor', [(t, t ^ 2 * k) for t in range(n_t)])  20.3 us
    pallas_call x2, Pallas kernels, input_side(): pl.pallas_call(functools.partial(input_kernel, groups, own_side), grid_sp...  12.5 us
    pallas_call x1, Pallas kernels, down_product(): pl.pallas_call(kernel, grid_spec=pltpu.PrefetchScalarGridSpec(num_scalar_...  6.41 us
    add x6, other arithmetic, owner_sum(): total = kept + across(sent, bit).astype(jnp.float32)  5.69 us
  transfers between devices with their start and end apart: 45, of which 18 were waited for; matrix products, arithmetic and copies ran while one was open for 5% of the time, Pallas kernels for 15%

profile of v2, /device:TPU:0, one launch (start us, length us, event | category | flops | bytes accessed | tf_op | source)
XLA Modules:
  0.0 240.9 jit_solution(8309675560930635576)
XLA Ops:
  3.8 13.7 %collective-permute-start.10 = (bf16[160,512]{1,0:T(8,128)(2,1)S(1)}, bf16[160,512]{1,0:T(8,128)(2,1)S(1)}, u32[]{:S(2)}, u32[]{:S(2)}) collective-permute-start(bf16[160,512]{1,0:T(8,128)(2,1)S(1)} %collective-permute-done.7), channel_id=1, source_target_pairs={{0,6},{1,7},{2,4},{3,5},{4,2},{5,3},{6,0},{7,1},{8,14},{9,15},{10,... | collective-permute-start | bytes 491528 | tf_op jit(solution)/shard_map/ppermute | solution.py:241
  17.5 13.2 %collective-permute-start.9 = (bf16[160,512]{1,0:T(8,128)(2,1)S(1)}, bf16[160,512]{1,0:T(8,128)(2,1)S(1)}, u32[]{:S(2)}, u32[]{:S(2)}) collective-permute-start(bf16[160,512]{1,0:T(8,128)(2,1)S(1)} %collective-permute-done.7), channel_id=1, source_target_pairs={{0,4},{1,5},{2,6},{3,7},{4,0},{5,1},{6,2},{7,3},{8,12},{9,13},{10,... | collective-permute-start | bytes 491528 | tf_op jit(solution)/shard_map/ppermute | solution.py:241
  34.3 8.2 %collective-permute-start.1 = (bf16[160,512]{1,0:T(8,128)(2,1)S(1)}, bf16[160,512]{1,0:T(8,128)(2,1)S(1)}, u32[]{:S(2)}, u32[]{:S(2)}) collective-permute-start(bf16[160,512]{1,0:T(8,128)(2,1)S(1)} %collective-permute-done), channel_id=1, source_target_pairs={{0,2},{1,3},{2,0},{3,1},{4,6},{5,7},{6,4},{7,5},{8,10},{9,11},{10,... | collective-permute-start | bytes 491528 | tf_op jit(solution)/shard_map/ppermute | solution.py:241
  42.5 5.7 %collective-permute-done.9 = bf16[160,512]{1,0:T(8,128)(2,1)S(1)} collective-permute-done((bf16[160,512]{1,0:T(8,128)(2,1)S(1)}, bf16[160,512]{1,0:T(8,128)(2,1)S(1)}, u32[]{:S(2)}, u32[]{:S(2)}) %collective-permute-start.9) | collective-permute-done | bytes 163872 | tf_op jit(solution)/shard_map/ppermute | solution.py:241
  48.3 5.6 %collective-permute-done.2 = bf16[160,512]{1,0:T(8,128)(2,1)S(1)} collective-permute-done((bf16[160,512]{1,0:T(8,128)(2,1)S(1)}, bf16[160,512]{1,0:T(8,128)(2,1)S(1)}, u32[]{:S(2)}, u32[]{:S(2)}) %collective-permute-start.2) | collective-permute-done | bytes 163872 | tf_op jit(solution)/shard_map/ppermute | solution.py:241
  55.0 3.8 %shard_map.96 = (f32[2,160,1024]{2,1,0:T(8,128)S(1)}, bf16[2,160,1024]{2,1,0:T(8,128)(2,1)S(1)}) custom-call(s32[2]{0:T(128)S(1)} %pad_add_fusion.place, s32[8,16]{1,0:T(8,128)S(1)} %dynamic_slice.10.flags.up_flags, bf16[4,160,512]{2,1,0:T(8,128)(2,1)S(1)} %pad_maximum_fusion.1.own, bf16[4,160,512]{2,1,0:T(8,128)(2,1)S(1)} %collective-permute-done.11.other, ...), custom_call_target="tpu_custom_call" | custom-call | flops 1342177280 | bytes 5373952 | tf_op jit(solution)/shard_map/pallas_call | solution.py:67
  59.8 3.3 %collective-permute-start.12 = (bf16[2,160,1024]{2,1,0:T(8,128)(2,1)S(1)}, bf16[2,160,1024]{2,1,0:T(8,128)(2,1)}, u32[]{:S(2)}, u32[]{:S(2)}) collective-permute-start(bf16[2,160,1024]{2,1,0:T(8,128)(2,1)S(1)} %get-tuple-element.17), channel_id=1, source_target_pairs={{0,8},{8,0},{16,24},{24,16},{1,9},{9,1},{17,25},{25,17},{2,10},{10... | collective-permute-start | bytes 1966088 | tf_op jit(solution)/shard_map/ppermute | solution.py:238
  64.7 3.8 %shard_map.97 = (f32[2,160,1024]{2,1,0:T(8,128)S(1)}, bf16[2,160,1024]{2,1,0:T(8,128)(2,1)S(1)}) custom-call(s32[2]{0:T(128)S(1)} %pad_add_fusion.place, s32[8,16]{1,0:T(8,128)S(1)} %dynamic_slice.9.flags.gate_flags, bf16[4,160,512]{2,1,0:T(8,128)(2,1)S(1)} %pad_maximum_fusion.1.own, bf16[4,160,512]{2,1,0:T(8,128)(2,1)S(1)} %collective-permute-done.11.other, ...), custom_call_target="tpu_custom_call" | custom-call | flops 1342177280 | bytes 5373952 | tf_op jit(solution)/shard_map/pallas_call | solution.py:67
  68.6 3.9 %shard_map.95 = (f32[2,160,1024]{2,1,0:T(8,128)S(1)}, bf16[2,160,1024]{2,1,0:T(8,128)(2,1)S(1)}) custom-call(s32[2]{0:T(128)S(1)} %pad_add_fusion.place, s32[16,8]{1,0:T(8,128)S(1)} %copy.11.flags, bf16[4,160,512]{2,1,0:T(8,128)(2,1)S(1)} %pad_maximum_fusion.own.refs_8_, bf16[4,160,512]{2,1,0:T(8,128)(2,1)S(1)} %collective-permute-done.4.other.refs_9_, ...), custom_call_target="tpu_custom_call" | custom-call | flops 1342177280 | bytes 5373952 | tf_op jit(solution)/shard_map/pallas_call | solution.py:67
  74.6 3.8 %shard_map.99 = (f32[2,160,1024]{2,1,0:T(8,128)S(1)}, bf16[2,160,1024]{2,1,0:T(8,128)(2,1)S(1)}) custom-call(s32[2]{0:T(128)S(1)} %pad_add_fusion.place, s32[8,16]{1,0:T(8,128)S(1)} %dynamic_slice.10.flags.up_flags, bf16[4,160,512]{2,1,0:T(8,128)(2,1)S(1)} %pad_maximum_fusion.1.own, bf16[4,160,512]{2,1,0:T(8,128)(2,1)S(1)} %collective-permute-done.11.other, ...), custom_call_target="tpu_custom_call" | custom-call | flops 1342177280 | bytes 5373952 | tf_op jit(solution)/shard_map/pallas_call | solution.py:67
  79.4 3.8 %shard_map.100 = (f32[2,160,1024]{2,1,0:T(8,128)S(1)}, bf16[2,160,1024]{2,1,0:T(8,128)(2,1)S(1)}) custom-call(s32[2]{0:T(128)S(1)} %pad_add_fusion.place, s32[8,16]{1,0:T(8,128)S(1)} %dynamic_slice.9.flags.gate_flags, bf16[4,160,512]{2,1,0:T(8,128)(2,1)S(1)} %pad_maximum_fusion.1.own, bf16[4,160,512]{2,1,0:T(8,128)(2,1)S(1)} %collective-permute-done.11.other, ...), custom_call_target="tpu_custom_call" | custom-call | flops 1342177280 | bytes 5373952 | tf_op jit(solution)/shard_map/pallas_call | solution.py:67
  84.3 3.9 %shard_map.98 = (f32[2,160,1024]{2,1,0:T(8,128)S(1)}, bf16[2,160,1024]{2,1,0:T(8,128)(2,1)S(1)}) custom-call(s32[2]{0:T(128)S(1)} %pad_add_fusion.place, s32[16,8]{1,0:T(8,128)S(1)} %copy.11.flags, bf16[4,160,512]{2,1,0:T(8,128)(2,1)S(1)} %pad_maximum_fusion.own.refs_8_, bf16[4,160,512]{2,1,0:T(8,128)(2,1)S(1)} %collective-permute-done.4.other.refs_9_, ...), custom_call_target="tpu_custom_call" | custom-call | flops 1342177280 | bytes 5373952 | tf_op jit(solution)/shard_map/pallas_call | solution.py:67
  92.9 2.9 %collective-permute-start.13 = (bf16[1,160,1024]{2,1,0:T(8,128)(2,1)S(1)}, bf16[1,160,1024]{2,1,0:T(8,128)(2,1)S(1)}, u32[]{:S(2)}, u32[]{:S(2)}) collective-permute-start(bf16[1,160,1024]{2,1,0:T(8,128)(2,1)S(1)} %slice.158), channel_id=1, source_target_pairs={{0,16},{8,24},{16,0},{24,8},{1,17},{9,25},{17,1},{25,9},{2,18},{10... | collective-permute-start | bytes 983048 | tf_op jit(solution)/shard_map/ppermute | solution.py:238
  97.2 9.5 %collective-permute-done.5 = bf16[2,160,1024]{2,1,0:T(8,128)(2,1)} collective-permute-done((bf16[2,160,1024]{2,1,0:T(8,128)(2,1)S(1)}, bf16[2,160,1024]{2,1,0:T(8,128)(2,1)}, u32[]{:S(2)}, u32[]{:S(2)}) %collective-permute-start.5) | collective-permute-done | bytes 655392 | tf_op jit(solution)/shard_map/ppermute | solution.py:238
  106.7 2.7 %collective-permute-start.15 = (bf16[1,160,1024]{2,1,0:T(8,128)(2,1)S(1)}, bf16[1,160,1024]{2,1,0:T(8,128)(2,1)S(1)}, u32[]{:S(2)}, u32[]{:S(2)}) collective-permute-start(bf16[1,160,1024]{2,1,0:T(8,128)(2,1)S(1)} %slice.157), channel_id=1, source_target_pairs={{0,16},{8,24},{16,0},{24,8},{1,17},{9,25},{17,1},{25,9},{2,18},{10... | collective-permute-start | bytes 983048 | tf_op jit(solution)/shard_map/ppermute | solution.py:238
  113.6 10.5 %collective-permute-done.19 = bf16[2,160,1024]{2,1,0:T(8,128)(2,1)S(1)} collective-permute-done((bf16[2,160,1024]{2,1,0:T(8,128)(2,1)S(1)}, bf16[2,160,1024]{2,1,0:T(8,128)(2,1)S(1)}, u32[]{:S(2)}, u32[]{:S(2)}) %collective-permute-start.19) | collective-permute-done | bytes 655392 | tf_op jit(solution)/shard_map/ppermute | solution.py:238
  125.4 5.8 %collective-permute-done.13 = bf16[1,160,1024]{2,1,0:T(8,128)(2,1)S(1)} collective-permute-done((bf16[1,160,1024]{2,1,0:T(8,128)(2,1)S(1)}, bf16[1,160,1024]{2,1,0:T(8,128)(2,1)S(1)}, u32[]{:S(2)}, u32[]{:S(2)}) %collective-permute-start.13) | collective-permute-done | bytes 327712 | tf_op jit(solution)/shard_map/ppermute | solution.py:238
  132.1 6.1 %collective-permute-done.15 = bf16[1,160,1024]{2,1,0:T(8,128)(2,1)S(1)} collective-permute-done((bf16[1,160,1024]{2,1,0:T(8,128)(2,1)S(1)}, bf16[1,160,1024]{2,1,0:T(8,128)(2,1)S(1)}, u32[]{:S(2)}, u32[]{:S(2)}) %collective-permute-start.15) | collective-permute-done | bytes 327712 | tf_op jit(solution)/shard_map/ppermute | solution.py:238
  138.2 5.6 %collective-permute-done.6 = bf16[1,160,1024]{2,1,0:T(8,128)(2,1)S(1)} collective-permute-done((bf16[1,160,1024]{2,1,0:T(8,128)(2,1)S(1)}, bf16[1,160,1024]{2,1,0:T(8,128)(2,1)S(1)}, u32[]{:S(2)}, u32[]{:S(2)}) %collective-permute-start.6) | collective-permute-done | bytes 327712 | tf_op jit(solution)/shard_map/ppermute | solution.py:238
  150.3 4.7 %collective-permute-done.16.refs_1_ = bf16[160,1024]{1,0:T(8,128)(2,1)S(1)} collective-permute-done((bf16[160,1024]{1,0:T(8,128)(2,1)S(1)}, bf16[160,1024]{1,0:T(8,128)(2,1)S(1)}, u32[]{:S(2)}, u32[]{:S(2)}) %collective-permute-start.16) | collective-permute-done | bytes 327712 | tf_op jit(solution)/shard_map/ppermute | solution.py:238
  158.1 4.0 %collective-permute-done.25.refs_5_ = bf16[160,1024]{1,0:T(8,128)(2,1)S(1)} collective-permute-done((bf16[160,1024]{1,0:T(8,128)(2,1)S(1)}, bf16[160,1024]{1,0:T(8,128)(2,1)S(1)}, u32[]{:S(2)}, u32[]{:S(2)}) %collective-permute-start.25) | collective-permute-done | bytes 327712 | tf_op jit(solution)/shard_map/ppermute | solution.py:238
  165.1 4.0 %collective-permute-done.28.refs_9_ = bf16[160,1024]{1,0:T(8,128)(2,1)S(1)} collective-permute-done((bf16[160,1024]{1,0:T(8,128)(2,1)S(1)}, bf16[160,1024]{1,0:T(8,128)(2,1)S(1)}, u32[]{:S(2)}, u32[]{:S(2)}) %collective-permute-start.28) | collective-permute-done | bytes 327712 | tf_op jit(solution)/shard_map/ppermute | solution.py:238
  172.1 5.3 %collective-permute-done.32.refs_14_ = bf16[160,1024]{1,0:T(8,128)(2,1)S(1)} collective-permute-done((bf16[160,1024]{1,0:T(8,128)(2,1)S(1)}, bf16[160,1024]{1,0:T(8,128)(2,1)S(1)}, u32[]{:S(2)}, u32[]{:S(2)}) %collective-permute-start.32) | collective-permute-done | bytes 327712 | tf_op jit(solution)/shard_map/ppermute | solution.py:238
  178.2 6.3 %collective-permute-done.18.refs_3_ = bf16[160,1024]{1,0:T(8,128)(2,1)S(1)} collective-permute-done((bf16[160,1024]{1,0:T(8,128)(2,1)S(1)}, bf16[160,1024]{1,0:T(8,128)(2,1)S(1)}, u32[]{:S(2)}, u32[]{:S(2)}) %collective-permute-start.18) | collective-permute-done | bytes 327712 | tf_op jit(solution)/shard_map/ppermute | solution.py:238
  184.4 4.8 %collective-permute-done.30.refs_11_ = bf16[160,1024]{1,0:T(8,128)(2,1)S(1)} collective-permute-done((bf16[160,1024]{1,0:T(8,128)(2,1)S(1)}, bf16[160,1024]{1,0:T(8,128)(2,1)S(1)}, u32[]{:S(2)}, u32[]{:S(2)}) %collective-permute-start.30) | collective-permute-done | bytes 327712 | tf_op jit(solution)/shard_map/ppermute | solution.py:238
  189.2 5.8 %shard_map.102 = bf16[4,160,512]{2,1,0:T(8,128)(2,1)S(1)} custom-call(s32[2]{0:T(128)S(1)} %pad_add_fusion.place, s32[8,16]{1,0:T(8,128)S(1)} %dynamic_slice.9.flags.gate_flags, s32[8,16]{1,0:T(8,128)S(1)} %dynamic_slice.10.flags.up_flags, bf16[160,1024]{1,0:T(8,128)(2,1)S(1)} %get-tuple-element.32.refs_0_, ...), custom_call_target="tpu_custom_call" | custom-call | flops 2684354560 | bytes 10747904 | tf_op jit(solution)/shard_map/pallas_call | solution.py:129
  197.2 6.8 %shard_map.101 = f32[4,160,512]{2,1,0:T(8,128)} custom-call(s32[2]{0:T(128)S(1)} %pad_add_fusion.place, s32[8,16]{1,0:T(8,128)S(1)} %dynamic_slice.9.flags.gate_flags, s32[8,16]{1,0:T(8,128)S(1)} %dynamic_slice.10.flags.up_flags, bf16[160,1024]{1,0:T(8,128)(2,1)S(1)} %get-tuple-element.32.refs_0_, bf16[160,1024]{1,0:T(8,128)(2,1)S(1)} %collective-permute-done.16.refs_1_, ...), custom_call_target="tpu_custom_call" | custom-call | flops 2684354560 | bytes 10747904 | tf_op jit(solution)/shard_map/pallas_call | solution.py:129
  205.6 2.7 %collective-permute-start.37 = (bf16[160,512]{1,0:T(8,128)(2,1)S(1)}, bf16[160,512]{1,0:T(8,128)(2,1)S(1)}, u32[]{:S(2)}, u32[]{:S(2)}) collective-permute-start(bf16[160,512]{1,0:T(8,128)(2,1)S(1)} %get-tuple-element.35), channel_id=1, source_target_pairs={{0,6},{1,7},{2,4},{3,5},{4,2},{5,3},{6,0},{7,1},{8,14},{9,15},{10,... | collective-permute-start | bytes 491528 | tf_op jit(solution)/shard_map/ppermute | solution.py:241
  212.1 2.6 %collective-permute-done.37 = bf16[160,512]{1,0:T(8,128)(2,1)S(1)} collective-permute-done((bf16[160,512]{1,0:T(8,128)(2,1)S(1)}, bf16[160,512]{1,0:T(8,128)(2,1)S(1)}, u32[]{:S(2)}, u32[]{:S(2)}) %collective-permute-start.37) | collective-permute-done | bytes 163872 | tf_op jit(solution)/shard_map/ppermute | solution.py:241
  215.0 6.5 %collective-permute-done.36 = bf16[160,512]{1,0:T(8,128)(2,1)S(1)} collective-permute-done((bf16[160,512]{1,0:T(8,128)(2,1)S(1)}, bf16[160,512]{1,0:T(8,128)(2,1)S(1)}, u32[]{:S(2)}, u32[]{:S(2)}) %collective-permute-start.36) | collective-permute-done | bytes 163872 | tf_op jit(solution)/shard_map/ppermute | solution.py:241
  225.7 8.1 %collective-permute-done.44.refs_7_ = bf16[160,1024]{1,0:T(8,128)(2,1)S(1)} collective-permute-done((bf16[160,1024]{1,0:T(8,128)(2,1)S(1)}, bf16[160,1024]{1,0:T(8,128)(2,1)S(1)}, u32[]{:S(2)}, u32[]{:S(2)}) %collective-permute-start.44) | collective-permute-done | bytes 327712 | tf_op jit(solution)/shard_map/ppermute | solution.py:238
  233.8 6.4 %shard_map.103 = bf16[2048,1024]{1,0:T(8,128)(2,1)} custom-call(s32[2]{0:T(128)S(1)} %pad_add_fusion.place, s32[16,8]{1,0:T(8,128)S(1)} %copy.11.flags, bf16[160,1024]{1,0:T(8,128)(2,1)S(1)} %get-tuple-element.31.refs_0_, bf16[160,1024]{1,0:T(8,128)(2,1)S(1)} %collective-permute-done.39.refs_1_, bf16[160,1024]{1,0:T(8,128)(2,1)S(1)} %collective-permute-done.40.refs_2_, ...), custom_call_target="tpu_custom_call" | custom-call | flops 2684354560 | bytes 8126464 | tf_op jit(solution)/shard_map/pallas_call | solution.py:189
  (96 shorter events, 56.2 us)
Async XLA Ops:
  2.2 28.6 %collective-permute-start = (bf16[160,512]{1,0:T(8,128)(2,1)}, bf16[160,512]{1,0:T(8,128)(2,1)S(1)}, u32[]{:S(2)}, u32[]{:S(2)}) collective-permute-start(bf16[160,512]{1,0:T(8,128)(2,1)} %param.9), channel_id=1, source_target_pairs={{0,0},{1,1},{2,8},{3,9},{4,16},{5,17},{6,24},{7,25},{8,2},{9,3},{1... | collective-permute-start | bytes 491528 | tf_op jit(solution)/shard_map/ppermute | solution.py:247
  3.8 30.5 %collective-permute-start.10 = (bf16[160,512]{1,0:T(8,128)(2,1)S(1)}, bf16[160,512]{1,0:T(8,128)(2,1)S(1)}, u32[]{:S(2)}, u32[]{:S(2)}) collective-permute-start(bf16[160,512]{1,0:T(8,128)(2,1)S(1)} %collective-permute-done.7), channel_id=1, source_target_pairs={{0,6},{1,7},{2,4},{3,5},{4,2},{5,3},{6,0},{7,1},{8,14},{9,15},{10,... | collective-permute-start | bytes 491528 | tf_op jit(solution)/shard_map/ppermute | solution.py:241
  17.5 30.6 %collective-permute-start.9 = (bf16[160,512]{1,0:T(8,128)(2,1)S(1)}, bf16[160,512]{1,0:T(8,128)(2,1)S(1)}, u32[]{:S(2)}, u32[]{:S(2)}) collective-permute-start(bf16[160,512]{1,0:T(8,128)(2,1)S(1)} %collective-permute-done.7), channel_id=1, source_target_pairs={{0,4},{1,5},{2,6},{3,7},{4,0},{5,1},{6,2},{7,3},{8,12},{9,13},{10,... | collective-permute-start | bytes 491528 | tf_op jit(solution)/shard_map/ppermute | solution.py:241
  30.8 17.4 %collective-permute-start.8 = (bf16[160,512]{1,0:T(8,128)(2,1)S(1)}, bf16[160,512]{1,0:T(8,128)(2,1)S(1)}, u32[]{:S(2)}, u32[]{:S(2)}) collective-permute-start(bf16[160,512]{1,0:T(8,128)(2,1)S(1)} %collective-permute-done.7), channel_id=1, source_target_pairs={{0,2},{1,3},{2,0},{3,1},{4,6},{5,7},{6,4},{7,5},{8,10},{9,11},{10,... | collective-permute-start | bytes 491528 | tf_op jit(solution)/shard_map/ppermute | solution.py:241
  30.8 17.6 %collective-permute-start.3 = (bf16[160,512]{1,0:T(8,128)(2,1)S(1)}, bf16[160,512]{1,0:T(8,128)(2,1)S(1)}, u32[]{:S(2)}, u32[]{:S(2)}) collective-permute-start(bf16[160,512]{1,0:T(8,128)(2,1)S(1)} %collective-permute-done), channel_id=1, source_target_pairs={{0,6},{1,7},{2,4},{3,5},{4,2},{5,3},{6,0},{7,1},{8,14},{9,15},{10,... | collective-permute-start | bytes 491528 | tf_op jit(solution)/shard_map/ppermute | solution.py:241
  32.2 21.7 %collective-permute-start.2 = (bf16[160,512]{1,0:T(8,128)(2,1)S(1)}, bf16[160,512]{1,0:T(8,128)(2,1)S(1)}, u32[]{:S(2)}, u32[]{:S(2)}) collective-permute-start(bf16[160,512]{1,0:T(8,128)(2,1)S(1)} %collective-permute-done), channel_id=1, source_target_pairs={{0,4},{1,5},{2,6},{3,7},{4,0},{5,1},{6,2},{7,3},{8,12},{9,13},{10,... | collective-permute-start | bytes 491528 | tf_op jit(solution)/shard_map/ppermute | solution.py:241
  34.3 19.7 %collective-permute-start.1 = (bf16[160,512]{1,0:T(8,128)(2,1)S(1)}, bf16[160,512]{1,0:T(8,128)(2,1)S(1)}, u32[]{:S(2)}, u32[]{:S(2)}) collective-permute-start(bf16[160,512]{1,0:T(8,128)(2,1)S(1)} %collective-permute-done), channel_id=1, source_target_pairs={{0,2},{1,3},{2,0},{3,1},{4,6},{5,7},{6,4},{7,5},{8,10},{9,11},{10,... | collective-permute-start | bytes 491528 | tf_op jit(solution)/shard_map/ppermute | solution.py:241
  54.0 14.6 %collective-permute-start.4 = (bf16[4,160,512]{2,1,0:T(8,128)(2,1)S(1)}, bf16[4,160,512]{2,1,0:T(8,128)(2,1)S(1)}, u32[]{:S(2)}, u32[]{:S(2)}) collective-permute-start(bf16[4,160,512]{2,1,0:T(8,128)(2,1)S(1)} %pad_maximum_fusion.own.refs_8_), channel_id=1, source_target_pairs={{0,1},{1,0},{2,3},{3,2},{4,5},{5,4},{6,7},{7,6},{8,9},{9,8},{10,11... | collective-permute-start | bytes 1966088 | tf_op jit(solution)/shard_map/ppermute | solution.py:244
  59.8 28.4 %collective-permute-start.12 = (bf16[2,160,1024]{2,1,0:T(8,128)(2,1)S(1)}, bf16[2,160,1024]{2,1,0:T(8,128)(2,1)}, u32[]{:S(2)}, u32[]{:S(2)}) collective-permute-start(bf16[2,160,1024]{2,1,0:T(8,128)(2,1)S(1)} %get-tuple-element.17), channel_id=1, source_target_pairs={{0,8},{8,0},{16,24},{24,16},{1,9},{9,1},{17,25},{25,17},{2,10},{10... | collective-permute-start | bytes 1966088 | tf_op jit(solution)/shard_map/ppermute | solution.py:238
  68.5 24.4 %collective-permute-start.14 = (bf16[2,160,1024]{2,1,0:T(8,128)(2,1)S(1)}, bf16[2,160,1024]{2,1,0:T(8,128)(2,1)}, u32[]{:S(2)}, u32[]{:S(2)}) collective-permute-start(bf16[2,160,1024]{2,1,0:T(8,128)(2,1)S(1)} %get-tuple-element.19), channel_id=1, source_target_pairs={{0,8},{8,0},{16,24},{24,16},{1,9},{9,1},{17,25},{25,17},{2,10},{10... | collective-permute-start | bytes 1966088 | tf_op jit(solution)/shard_map/ppermute | solution.py:238
  72.5 34.2 %collective-permute-start.5 = (bf16[2,160,1024]{2,1,0:T(8,128)(2,1)S(1)}, bf16[2,160,1024]{2,1,0:T(8,128)(2,1)}, u32[]{:S(2)}, u32[]{:S(2)}) collective-permute-start(bf16[2,160,1024]{2,1,0:T(8,128)(2,1)S(1)} %get-tuple-element.15), channel_id=1, source_target_pairs={{0,8},{8,0},{16,24},{24,16},{1,9},{9,1},{17,25},{25,17},{2,10},{10... | collective-permute-start | bytes 1966088 | tf_op jit(solution)/shard_map/ppermute | solution.py:238
  78.4 32.5 %collective-permute-start.21 = (bf16[2,160,1024]{2,1,0:T(8,128)(2,1)S(1)}, bf16[2,160,1024]{2,1,0:T(8,128)(2,1)}, u32[]{:S(2)}, u32[]{:S(2)}) collective-permute-start(bf16[2,160,1024]{2,1,0:T(8,128)(2,1)S(1)} %get-tuple-element.23), channel_id=1, source_target_pairs={{0,16},{8,24},{16,0},{24,8},{1,17},{9,25},{17,1},{25,9},{2,18},{10... | collective-permute-start | bytes 1966088 | tf_op jit(solution)/shard_map/ppermute | solution.py:238
  83.2 29.0 %collective-permute-start.23 = (bf16[2,160,1024]{2,1,0:T(8,128)(2,1)S(1)}, bf16[2,160,1024]{2,1,0:T(8,128)(2,1)S(1)}, u32[]{:S(2)}, u32[]{:S(2)}) collective-permute-start(bf16[2,160,1024]{2,1,0:T(8,128)(2,1)S(1)} %get-tuple-element.25), channel_id=1, source_target_pairs={{0,16},{8,24},{16,0},{24,8},{1,17},{9,25},{17,1},{25,9},{2,18},{10... | collective-permute-start | bytes 1966088 | tf_op jit(solution)/shard_map/ppermute | solution.py:238
  88.2 35.9 %collective-permute-start.19 = (bf16[2,160,1024]{2,1,0:T(8,128)(2,1)S(1)}, bf16[2,160,1024]{2,1,0:T(8,128)(2,1)S(1)}, u32[]{:S(2)}, u32[]{:S(2)}) collective-permute-start(bf16[2,160,1024]{2,1,0:T(8,128)(2,1)S(1)} %get-tuple-element.21), channel_id=1, source_target_pairs={{0,16},{8,24},{16,0},{24,8},{1,17},{9,25},{17,1},{25,9},{2,18},{10... | collective-permute-start | bytes 1966088 | tf_op jit(solution)/shard_map/ppermute | solution.py:238
  92.9 38.3 %collective-permute-start.13 = (bf16[1,160,1024]{2,1,0:T(8,128)(2,1)S(1)}, bf16[1,160,1024]{2,1,0:T(8,128)(2,1)S(1)}, u32[]{:S(2)}, u32[]{:S(2)}) collective-permute-start(bf16[1,160,1024]{2,1,0:T(8,128)(2,1)S(1)} %slice.158), channel_id=1, source_target_pairs={{0,16},{8,24},{16,0},{24,8},{1,17},{9,25},{17,1},{25,9},{2,18},{10... | collective-permute-start | bytes 983048 | tf_op jit(solution)/shard_map/ppermute | solution.py:238
  106.7 31.5 %collective-permute-start.15 = (bf16[1,160,1024]{2,1,0:T(8,128)(2,1)S(1)}, bf16[1,160,1024]{2,1,0:T(8,128)(2,1)S(1)}, u32[]{:S(2)}, u32[]{:S(2)}) collective-permute-start(bf16[1,160,1024]{2,1,0:T(8,128)(2,1)S(1)} %slice.157), channel_id=1, source_target_pairs={{0,16},{8,24},{16,0},{24,8},{1,17},{9,25},{17,1},{25,9},{2,18},{10... | collective-permute-start | bytes 983048 | tf_op jit(solution)/shard_map/ppermute | solution.py:238
  110.8 33.0 %collective-permute-start.6 = (bf16[1,160,1024]{2,1,0:T(8,128)(2,1)S(1)}, bf16[1,160,1024]{2,1,0:T(8,128)(2,1)S(1)}, u32[]{:S(2)}, u32[]{:S(2)}) collective-permute-start(bf16[1,160,1024]{2,1,0:T(8,128)(2,1)S(1)} %slice.159), channel_id=1, source_target_pairs={{0,16},{8,24},{16,0},{24,8},{1,17},{9,25},{17,1},{25,9},{2,18},{10... | collective-permute-start | bytes 983048 | tf_op jit(solution)/shard_map/ppermute | solution.py:238
  112.3 35.2 %collective-permute-start.22 = (bf16[1,160,1024]{2,1,0:T(8,128)(2,1)S(1)}, bf16[1,160,1024]{2,1,0:T(8,128)(2,1)S(1)}, u32[]{:S(2)}, u32[]{:S(2)}) collective-permute-start(bf16[1,160,1024]{2,1,0:T(8,128)(2,1)S(1)} %slice.155), channel_id=1, source_target_pairs={{0,8},{8,0},{16,24},{24,16},{1,9},{9,1},{17,25},{25,17},{2,10},{10... | collective-permute-start | bytes 983048 | tf_op jit(solution)/shard_map/ppermute | solution.py:238
  124.2 23.3 %collective-permute-start.24 = (bf16[1,160,1024]{2,1,0:T(8,128)(2,1)S(1)}, bf16[1,160,1024]{2,1,0:T(8,128)(2,1)S(1)}, u32[]{:S(2)}, u32[]{:S(2)}) collective-permute-start(bf16[1,160,1024]{2,1,0:T(8,128)(2,1)S(1)} %slice.154), channel_id=1, source_target_pairs={{0,8},{8,0},{16,24},{24,16},{1,9},{9,1},{17,25},{25,17},{2,10},{10... | collective-permute-start | bytes 983048 | tf_op jit(solution)/shard_map/ppermute | solution.py:238
  131.2 16.3 %collective-permute-start.20 = (bf16[1,160,1024]{2,1,0:T(8,128)(2,1)S(1)}, bf16[1,160,1024]{2,1,0:T(8,128)(2,1)S(1)}, u32[]{:S(2)}, u32[]{:S(2)}) collective-permute-start(bf16[1,160,1024]{2,1,0:T(8,128)(2,1)S(1)} %slice.156), channel_id=1, source_target_pairs={{0,8},{8,0},{16,24},{24,16},{1,9},{9,1},{17,25},{25,17},{2,10},{10... | collective-permute-start | bytes 983048 | tf_op jit(solution)/shard_map/ppermute | solution.py:238
  148.3 15.0 %collective-permute-start.26 = (bf16[160,1024]{1,0:T(8,128)(2,1)S(1)}, bf16[160,1024]{1,0:T(8,128)(2,1)S(1)}, u32[]{:S(2)}, u32[]{:S(2)}) collective-permute-start(bf16[160,1024]{1,0:T(8,128)(2,1)S(1)} %get-tuple-element.29.refs_4_), channel_id=1, source_target_pairs={{0,16},{8,24},{16,0},{24,8},{1,17},{9,25},{17,1},{25,9},{2,18},{10... | collective-permute-start | bytes 983048 | tf_op jit(solution)/shard_map/ppermute | solution.py:238
  149.0 20.1 %collective-permute-start.28 = (bf16[160,1024]{1,0:T(8,128)(2,1)S(1)}, bf16[160,1024]{1,0:T(8,128)(2,1)S(1)}, u32[]{:S(2)}, u32[]{:S(2)}) collective-permute-start(bf16[160,1024]{1,0:T(8,128)(2,1)S(1)} %get-tuple-element.33.refs_8_), channel_id=1, source_target_pairs={{0,8},{8,0},{16,24},{24,16},{1,9},{9,1},{17,25},{25,17},{2,10},{10... | collective-permute-start | bytes 983048 | tf_op jit(solution)/shard_map/ppermute | solution.py:238
  155.1 15.3 %collective-permute-start.29 = (bf16[160,1024]{1,0:T(8,128)(2,1)S(1)}, bf16[160,1024]{1,0:T(8,128)(2,1)S(1)}, u32[]{:S(2)}, u32[]{:S(2)}) collective-permute-start(bf16[160,1024]{1,0:T(8,128)(2,1)S(1)} %get-tuple-element.33.refs_8_), channel_id=1, source_target_pairs={{0,16},{8,24},{16,0},{24,8},{1,17},{9,25},{17,1},{25,9},{2,18},{10... | collective-permute-start | bytes 983048 | tf_op jit(solution)/shard_map/ppermute | solution.py:238
  156.4 21.0 %collective-permute-start.32 = (bf16[160,1024]{1,0:T(8,128)(2,1)S(1)}, bf16[160,1024]{1,0:T(8,128)(2,1)S(1)}, u32[]{:S(2)}, u32[]{:S(2)}) collective-permute-start(bf16[160,1024]{1,0:T(8,128)(2,1)S(1)} %get-tuple-element.30.refs_12_), channel_id=1, source_target_pairs={{0,16},{8,24},{16,0},{24,8},{1,17},{9,25},{17,1},{25,9},{2,18},{10... | collective-permute-start | bytes 983048 | tf_op jit(solution)/shard_map/ppermute | solution.py:238
  162.1 16.1 %collective-permute-start.31 = (bf16[160,1024]{1,0:T(8,128)(2,1)S(1)}, bf16[160,1024]{1,0:T(8,128)(2,1)S(1)}, u32[]{:S(2)}, u32[]{:S(2)}) collective-permute-start(bf16[160,1024]{1,0:T(8,128)(2,1)S(1)} %get-tuple-element.30.refs_12_), channel_id=1, source_target_pairs={{0,8},{8,0},{16,24},{24,16},{1,9},{9,1},{17,25},{25,17},{2,10},{10... | collective-permute-start | bytes 983048 | tf_op jit(solution)/shard_map/ppermute | solution.py:238
  163.4 21.1 %collective-permute-start.18 = (bf16[160,1024]{1,0:T(8,128)(2,1)S(1)}, bf16[160,1024]{1,0:T(8,128)(2,1)S(1)}, u32[]{:S(2)}, u32[]{:S(2)}) collective-permute-start(bf16[160,1024]{1,0:T(8,128)(2,1)S(1)} %collective-permute-done.16.refs_1_), channel_id=1, source_target_pairs={{0,16},{8,24},{16,0},{24,8},{1,17},{9,25},{17,1},{25,9},{2,18},{10... | collective-permute-start | bytes 983048 | tf_op jit(solution)/shard_map/ppermute | solution.py:238
  169.1 15.3 %collective-permute-start.27 = (bf16[160,1024]{1,0:T(8,128)(2,1)S(1)}, bf16[160,1024]{1,0:T(8,128)(2,1)S(1)}, u32[]{:S(2)}, u32[]{:S(2)}) collective-permute-start(bf16[160,1024]{1,0:T(8,128)(2,1)S(1)} %collective-permute-done.26.refs_6_), channel_id=1, source_target_pairs={{0,8},{8,0},{16,24},{24,16},{1,9},{9,1},{17,25},{25,17},{2,10},{10... | collective-permute-start | bytes 983048 | tf_op jit(solution)/shard_map/ppermute | solution.py:238
  170.4 18.8 %collective-permute-start.30 = (bf16[160,1024]{1,0:T(8,128)(2,1)S(1)}, bf16[160,1024]{1,0:T(8,128)(2,1)S(1)}, u32[]{:S(2)}, u32[]{:S(2)}) collective-permute-start(bf16[160,1024]{1,0:T(8,128)(2,1)S(1)} %collective-permute-done.28.refs_9_), channel_id=1, source_target_pairs={{0,16},{8,24},{16,0},{24,8},{1,17},{9,25},{17,1},{25,9},{2,18},{10... | collective-permute-start | bytes 983048 | tf_op jit(solution)/shard_map/ppermute | solution.py:238
  195.1 15.0 %collective-permute-start.39 = (bf16[160,1024]{1,0:T(8,128)(2,1)S(1)}, bf16[160,1024]{1,0:T(8,128)(2,1)S(1)}, u32[]{:S(2)}, u32[]{:S(2)}) collective-permute-start(bf16[160,1024]{1,0:T(8,128)(2,1)S(1)} %get-tuple-element.31.refs_0_), channel_id=1, source_target_pairs={{0,8},{8,0},{16,24},{24,16},{1,9},{9,1},{17,25},{25,17},{2,10},{10... | collective-permute-start | bytes 983048 | tf_op jit(solution)/shard_map/ppermute | solution.py:238
  195.5 14.9 %collective-permute-start.43 = (bf16[160,1024]{1,0:T(8,128)(2,1)S(1)}, bf16[160,1024]{1,0:T(8,128)(2,1)S(1)}, u32[]{:S(2)}, u32[]{:S(2)}) collective-permute-start(bf16[160,1024]{1,0:T(8,128)(2,1)S(1)} %get-tuple-element.28.refs_4_), channel_id=1, source_target_pairs={{0,16},{8,24},{16,0},{24,8},{1,17},{9,25},{17,1},{25,9},{2,18},{10... | collective-permute-start | bytes 983048 | tf_op jit(solution)/shard_map/ppermute | solution.py:238
  208.3 14.6 %collective-permute-start.35 = (bf16[160,512]{1,0:T(8,128)(2,1)S(1)}, bf16[160,512]{1,0:T(8,128)(2,1)S(1)}, u32[]{:S(2)}, u32[]{:S(2)}) collective-permute-start(bf16[160,512]{1,0:T(8,128)(2,1)S(1)} %get-tuple-element.34), channel_id=1, source_target_pairs={{0,2},{1,3},{2,0},{3,1},{4,6},{5,7},{6,4},{7,5},{8,10},{9,11},{10,... | collective-permute-start | bytes 491528 | tf_op jit(solution)/shard_map/ppermute | solution.py:241
  222.9 17.3 %collective-permute-start.38 = (bf16[160,512]{1,0:T(8,128)(2,1)S(1)}, bf16[160,512]{1,0:T(8,128)(2,1)S(1)}, u32[]{:S(2)}, u32[]{:S(2)}) collective-permute-start(bf16[160,512]{1,0:T(8,128)(2,1)S(1)} %fusion.11), channel_id=1, source_target_pairs={{0,0},{1,1},{2,8},{3,9},{4,16},{5,17},{6,24},{7,25},{8,2},{9,3},{1... | collective-permute-start | bytes 491528 | tf_op jit(solution)/shard_map/ppermute | solution.py:319
  (15 other events, 145.7 us)

commit v3 on v2

v3 whole, which is shorter than its diff:
```python
import functools

import jax
import jax.numpy as jnp
from jax import lax
from jax.experimental import pallas as pl
from jax.experimental.pallas import tpu as pltpu
from jax.sharding import PartitionSpec as P

BLOCK = 128
VMEM_BYTES = 48 * 1024 * 1024


def keep_blocks(weight, flag_of):
    rows = []
    for i in range(weight.shape[0] // BLOCK):
        row = []
        for j in range(weight.shape[1] // BLOCK):
            block = weight[i * BLOCK : (i + 1) * BLOCK, j * BLOCK : (j + 1) * BLOCK]
            row.append(jnp.where(flag_of(i, j) == 1, block, jnp.zeros_like(block)))
        rows.append(jnp.concatenate(row, axis=1))
    return jnp.concatenate(rows, axis=0)


def fill_columns(target, start, low, own, other):
    rows, width = own.shape
    target[start : start + rows, :width] = jnp.where(low, own, other)
    target[start : start + rows, width:] = jnp.where(low, other, own)


def forward_half(place, weights, all_flags, parts, order, half, transposed):
    groups, rows, width = parts[0][0].shape
    n_parts, n_weights = len(parts), len(weights)
    inner = 2 * width
    span = weights[0].shape[0 if transposed else 1] // 2
    tile = min(512, span)
    steps = span // tile
    blocks = tile // BLOCK
    group_rows = n_parts * rows

    def kernel(place, *refs):
        flags, refs = refs[:n_weights], refs[n_weights:]
        columns, refs = refs[: 2 * n_parts], refs[2 * n_parts :]
        blocks_in, (kept, sent, x_all) = refs[:n_weights], refs[n_weights:]
        step = pl.program_id(0)

        @pl.when(step == 0)
        def _():
            low = place[0] == 0
            for i in range(groups):
                for p in range(n_parts):
                    g, start = order[i], i * group_rows + p * rows
                    fill_columns(x_all, start, low, columns[2 * p][g], columns[2 * p + 1][g])

        first = (half * steps + step) * blocks
        for w in range(n_weights):
            flag = flags[w]
            if transposed:
                masked = keep_blocks(blocks_in[w][...], lambda i, j: flag[first + i, j])
                dims = (((1,), (1,)), ((), ()))
            else:
                masked = keep_blocks(blocks_in[w][...], lambda i, j: flag[i, first + j])
                dims = (((1,), (0,)), ((), ()))
            part = lax.dot_general(x_all[...], masked, dims, preferred_element_type=jnp.float32)
            part = part.reshape(groups, group_rows, tile)
            kept[:, w] = part[: groups // 2]
            sent[:, w] = part[groups // 2 :].astype(jnp.bfloat16)

    full = pl.BlockSpec((groups, rows, width), lambda j, *_: (0, 0, 0))
    if transposed:
        weight_spec = pl.BlockSpec((tile, inner), lambda j, *_: (half * steps + j, 0))
    else:
        weight_spec = pl.BlockSpec((inner, tile), lambda j, *_: (0, half * steps + j))
    out_spec = pl.BlockSpec((groups // 2, n_weights, group_rows, tile), lambda j, *_: (0, 0, 0, j))
    shape = (groups // 2, n_weights, group_rows, span)
    return pl.pallas_call(
        kernel,
        grid_spec=pltpu.PrefetchScalarGridSpec(
            num_scalar_prefetch=1 + n_weights,
            grid=(steps,),
            in_specs=[full] * (2 * n_parts) + [weight_spec] * n_weights,
            out_specs=[out_spec, out_spec],
            scratch_shapes=[pltpu.VMEM((groups * group_rows, inner), jnp.bfloat16)],
        ),
        out_shape=[
            jax.ShapeDtypeStruct(shape, jnp.float32),
            jax.ShapeDtypeStruct(shape, jnp.bfloat16),
        ],
        compiler_params=pltpu.CompilerParams(vmem_limit_bytes=VMEM_BYTES),
        cost_estimate=pl.CostEstimate(
            flops=2 * groups * group_rows * inner * span * n_weights,
            bytes_accessed=2 * inner * (groups * group_rows + n_weights * span)
            + 3 * groups * group_rows * span * n_weights,
            transcendentals=0,
        ),
    )(place, *all_flags, *[x for part in parts for x in part], *weights)


def input_side(place, gate_flags, up_flags, pieces, gate, up, width, own_side):
    groups = len(pieces) // 2
    _, rows, span = pieces[0].shape
    tile = min(256, width)
    tiles = width // tile
    blocks = tile // BLOCK

    def side_of(place):
        return place[0] if own_side else 1 - place[0]

    def kernel(place, gate_flags, up_flags, *refs):
        held, (gate, up, out, stacked) = refs[: 2 * groups], refs[2 * groups :]
        step = pl.program_id(0)

        @pl.when(step == 0)
        def _():
            for half in range(2):
                for rel in range(groups):
                    piece = held[half * groups + rel]
                    for which in range(2):
                        start = (2 * which + half) * span
                        stacked[rel, :, start : start + span] = piece[which]

        first = (side_of(place) * tiles + step) * blocks
        grads = stacked[...].reshape(groups * rows, 4 * span)
        dims = (((1,), (1,)), ((), ()))
        gate_kept = keep_blocks(gate[...], lambda i, j: gate_flags[first + i, j])
        up_kept = keep_blocks(up[...], lambda i, j: up_flags[first + i, j])
        total = lax.dot_general(
            grads[:, : 2 * span], gate_kept, dims, preferred_element_type=jnp.float32
        ) + lax.dot_general(
            grads[:, 2 * span :], up_kept, dims, preferred_element_type=jnp.float32
        )
        out[...] = total.reshape(groups, rows, tile).astype(out.dtype)

    whole = pl.BlockSpec((2, rows, span), lambda j, *_: (0, 0, 0))
    weight_spec = pl.BlockSpec(
        (tile, gate.shape[1]), lambda j, place, *_: (side_of(place) * tiles + j, 0)
    )
    return pl.pallas_call(
        kernel,
        grid_spec=pltpu.PrefetchScalarGridSpec(
            num_scalar_prefetch=3,
            grid=(tiles,),
            in_specs=[whole] * len(pieces) + [weight_spec, weight_spec],
            out_specs=pl.BlockSpec((groups, rows, tile), lambda j, *_: (0, 0, j)),
            scratch_shapes=[pltpu.VMEM((groups, rows, 4 * span), jnp.bfloat16)],
        ),
        out_shape=jax.ShapeDtypeStruct(
            (groups, rows, width), jnp.float32 if own_side else jnp.bfloat16
        ),
        compiler_params=pltpu.CompilerParams(vmem_limit_bytes=VMEM_BYTES),
        cost_estimate=pl.CostEstimate(
            flops=2 * groups * rows * 4 * span * width,
            bytes_accessed=8 * span * (groups * rows + width) + 4 * groups * rows * width,
            transcendentals=0,
        ),
    )(place, gate_flags, up_flags, *pieces, gate, up)


def down_product(place, flags, parts, halves):
    groups, rows, width = parts[0][0].shape
    n_parts = len(parts)
    group_rows = n_parts * rows
    span = halves[0][0].shape[1]
    tile = min(512, span)
    steps = span // tile
    blocks = tile // BLOCK

    def kernel(place, flags, *refs):
        first, second = refs[:groups], refs[groups : 2 * groups]
        columns, refs = refs[2 * groups : 2 * groups + 2 * n_parts], refs[2 * groups + 2 * n_parts :]
        out, hidden, grads = refs
        step = pl.program_id(0)

        @pl.when(step == 0)
        def _():
            low = place[0] == 0
            for rel in range(groups):
                for p in range(n_parts):
                    start = rel * group_rows + p * rows
                    fill_columns(grads, start, low, columns[2 * p][rel], columns[2 * p + 1][rel])

        @pl.when(step < steps)
        def _():
            for rel in range(groups):
                hidden[rel * group_rows : (rel + 1) * group_rows, :] = first[rel][...]

        @pl.when(step >= steps)
        def _():
            for rel in range(groups):
                hidden[rel * group_rows : (rel + 1) * group_rows, :] = second[rel][...]

        total = lax.dot_general(
            hidden[...], grads[...], (((0,), (0,)), ((), ())), preferred_element_type=jnp.float32
        )
        out[...] = keep_blocks(total, lambda i, j: flags[step * blocks + i, j]).astype(out.dtype)

    full = pl.BlockSpec((groups, rows, width), lambda j, *_: (0, 0, 0))
    first_spec = pl.BlockSpec((group_rows, tile), lambda j, *_: (0, jnp.minimum(j, steps - 1)))
    second_spec = pl.BlockSpec((group_rows, tile), lambda j, *_: (0, jnp.maximum(j - steps, 0)))
    return pl.pallas_call(
        kernel,
        grid_spec=pltpu.PrefetchScalarGridSpec(
            num_scalar_prefetch=2,
            grid=(2 * steps,),
            in_specs=[first_spec] * groups + [second_spec] * groups + [full] * (2 * n_parts),
            out_specs=pl.BlockSpec((tile, 2 * width), lambda j, *_: (j, 0)),
            scratch_shapes=[
                pltpu.VMEM((groups * group_rows, tile), jnp.bfloat16),
                pltpu.VMEM((groups * group_rows, 2 * width), jnp.bfloat16),
            ],
        ),
        out_shape=jax.ShapeDtypeStruct((2 * span, 2 * width), jnp.bfloat16),
        compiler_params=pltpu.CompilerParams(vmem_limit_bytes=VMEM_BYTES),
        cost_estimate=pl.CostEstimate(
            flops=8 * groups * group_rows * span * width,
            bytes_accessed=4 * groups * group_rows * (span + width) + 8 * span * width,
            transcendentals=0,
        ),
    )(place, flags, *halves[0], *halves[1], *[x for part in parts for x in part])


def after(x, *others):
    return lax.optimization_barrier((x, others))[0]


def per_device(
    tokens, out_grad, gate_weight, up_weight, down_weight, gate_mask, up_mask, down_mask
):
    n_f = lax.axis_size("fsdp")
    n_t = lax.axis_size("tensor")
    assert n_t == 2 * n_f and n_f & (n_f - 1) == 0
    bits = n_f.bit_length() - 1
    rows, width = tokens.shape
    sub = rows // n_f
    f_index = lax.axis_index("fsdp")
    t_index = lax.axis_index("tensor")
    plane = t_index // 2
    place = jnp.reshape(t_index % 2, (1,)).astype(jnp.int32)
    bit_orders = (tuple(range(bits)), tuple(reversed(range(bits))))

    def group_order(bit_order):
        order = []
        for i in range(n_f):
            order.append(sum(((i >> (bits - 1 - p)) & 1) << b for p, b in enumerate(bit_order)))
        return tuple(order)

    def across(x, k):
        return lax.ppermute(x, "fsdp", [(f, f ^ k) for f in range(n_f)])

    def along(x, k):
        return lax.ppermute(x, "tensor", [(t, t ^ (2 * k)) for t in range(n_t)])

    def exchange(x):
        return lax.ppermute(x, "tensor", [(t, t ^ 1) for t in range(n_t)])

    def reordered(x, index):
        for b in range(bits):
            pairs = x.reshape(-1, 2, 1 << b, *x.shape[1:])
            flipped = pairs[:, ::-1].reshape(x.shape)
            x = jnp.where((index >> b) & 1 == 1, flipped, x)
        return x

    def swapped(x, move):
        return jnp.stack([x[0]] + [move(x[k], k) for k in range(1, n_f)])

    def own_flags(mask, weight, row, col):
        rb, cb = weight.shape[0] // BLOCK, weight.shape[1] // BLOCK
        return lax.dynamic_slice(mask, (row * rb, col * cb), (rb, cb))

    gate_flags = own_flags(gate_mask, gate_weight, f_index, t_index)
    up_flags = own_flags(up_mask, up_weight, f_index, t_index)
    down_flags = own_flags(down_mask, down_weight, t_index, f_index)

    both = jnp.stack([tokens.reshape(n_f, sub, width), out_grad.reshape(n_f, sub, width)], axis=1)
    both = swapped(reordered(both, plane), along)
    both = swapped(reordered(both, plane ^ f_index), across)
    x_own, g_own = both[:, 0], both[:, 1]

    def part_of(pieces):
        own = jnp.concatenate(pieces, axis=1)
        return own, exchange(own)

    def owner_sum(kept, sent, bit_order):
        for bit in bit_order:
            total = kept + across(sent, 1 << bit).astype(jnp.float32)
            groups = total.shape[0]
            kept, sent = total[: groups // 2], total[groups // 2 :].astype(jnp.bfloat16)
        return total[0]

    def gathered(piece, bit_order):
        held = {0: piece}
        for bit in bit_order:
            for rel in list(held):
                held[rel | 1 << bit] = across(held[rel], 1 << bit)
        return [held[rel] for rel in range(n_f)]

    def forward(parts, weights, flags, transposed, previous=()):
        products = []
        for half in range(2):
            turn = after(place, *previous)
            order = group_order(bit_orders[half])
            products.append(forward_half(turn, weights, flags, parts, order, half, transposed))
            previous = products[-1]
        return products

    def sums(products):
        return [owner_sum(*products[half], bit_orders[half]) for half in range(2)]

    projections = ([gate_weight, up_weight], [gate_flags, up_flags], False)
    near = [x_own] + [along(x_own, k) for k in range(1, n_f // 2)]
    far_own = after(x_own, near[-1])
    far = [along(far_own, k) for k in range(n_f // 2, n_f)]
    part_a = part_of(near)
    products_a = forward([part_a], *projections)
    part_b = part_of(far)
    products_b = forward([part_b], *projections, products_a[1])
    g_start = after(g_own, far[-1], products_a[1])
    g_parts = [part_of([g_start] + [along(g_start, k) for k in range(1, n_f)])]
    products_g = forward(g_parts, [down_weight], [down_flags], True, products_b[1])
    pre = [sums(products_a), sums(products_b)]
    hidden_grad = sums(products_g)

    part_rows = rows // 2
    grads, hidden = [[], []], [[], []]
    for half in range(2):
        for p in range(2):
            v, u = pre[p][half][0], pre[p][half][1]
            d = hidden_grad[half][0, p * part_rows : (p + 1) * part_rows]
            sig = jax.nn.sigmoid(v)
            act = v * sig
            hidden[half].append((act * u).astype(jnp.bfloat16))
            gate_grad = d * u * (sig * (1.0 + v * (1.0 - sig)))
            grads[p].append(jnp.stack([gate_grad, d * act]).astype(jnp.bfloat16))

    def chip_sum(pieces, *previous):
        args = (gate_flags, up_flags, pieces, gate_weight, up_weight, width)
        for_core = input_side(after(place, *previous), *args, False)
        mine = input_side(after(place, for_core), *args, True)
        return mine + exchange(for_core).astype(jnp.float32), mine

    def both_halves(p):
        return [x for half in range(2) for x in gathered(grads[p][half], bit_orders[half])]

    def plane_sums(part, first):
        return [
            along(part[:, i * sub : (i + 1) * sub].astype(jnp.bfloat16), first + i)
            for i in range(part.shape[1] // sub)
            if first + i
        ]

    hidden_pieces = [
        gathered(jnp.concatenate(hidden[half]), bit_orders[half]) for half in range(2)
    ]
    far_part, far_mine = chip_sum(
        both_halves(1), *[x for held in hidden_pieces for x in held[:-1]]
    )
    far_sums = plane_sums(far_part, n_f // 2)
    near_part, near_mine = chip_sum(both_halves(0), far_mine)
    near_sums = plane_sums(near_part, 0)
    down_grad = down_product(after(place, near_mine), down_flags, g_parts, hidden_pieces)
    near_sums[-1] = after(near_sums[-1], down_grad)
    total = near_part[:, :sub]
    for received in far_sums + near_sums:
        total = total + received.astype(jnp.float32)
    back = swapped(total.astype(jnp.bfloat16), across)
    back = swapped(reordered(back, plane ^ f_index), along)
    input_grad = reordered(back, plane).reshape(rows, width)
    return (input_grad, down_grad)


def solution(mesh):
    return jax.shard_map(
        per_device,
        mesh=mesh,
        in_specs=(
            P("fsdp", "tensor"),
            P("fsdp", "tensor"),
            P("fsdp", "tensor"),
            P("fsdp", "tensor"),
            P("tensor", "fsdp"),
            P(),
            P(),
            P(),
        ),
        out_specs=(P("fsdp", "tensor"), P("tensor", "fsdp")),
        check_vma=False,
    )
```

time: 244 us -> 222 us (0.910)
  starting transfers between devices: 85.8 us -> 61.3 us
  Pallas kernels: 41.8 us -> 48.1 us
  other arithmetic: 8.64 us -> 5.88 us
  waiting for transfers between devices: 99.3 us -> 102 us
    ppermute x9 -> x15, starting transfers between devices: 43.2 us -> 25.9 us  [along(): return lax.ppermute(x, 'tensor', [(t, t ^ 2 * k) for t in range(n_t)])]
    ppermute x9 -> x15, waiting for transfers between devices: 20.3 us -> 30 us  [along(): return lax.ppermute(x, 'tensor', [(t, t ^ 2 * k) for t in range(n_t)])]
    ppermute x33 -> x36, waiting for transfers between devices: 79 us -> 71.5 us  [across(): return lax.ppermute(x, 'fsdp', [(f, f ^ k) for f in range(n_f)])]
    ppermute x33 -> x36, starting transfers between devices: 42.4 us -> 35.1 us  [across(): return lax.ppermute(x, 'fsdp', [(f, f ^ k) for f in range(n_f)])]
    pallas_call x8 -> x10, Pallas kernels: 35.4 us -> 41.7 us  [the longest x6 24.6 us: forward_half(): pl.pallas_call(kernel, grid_spec=pltpu.PrefetchScalarGridSpec(num_scalar_...]
    add x6 -> x11, other arithmetic: 5.69 us -> 1.67 us  [the longest x10 1.58 us: owner_sum(): total = kept + across(sent, 1 << bit).astype(jnp.float32)]
  transfers between devices with their start and end apart: 45 -> 56, of which waited for: 18 -> 28; matrix products, arithmetic and copies ran while one was open for 5% -> 3% of each run, Pallas kernels for 15% -> 20%
where the time goes in v3:
time: 222 us; the launch traced here: 221 us
  waiting for transfers between devices  102 us (46%)
  starting transfers between devices  61.3 us (28%)
  Pallas kernels  48.1 us (22%)
  other arithmetic  5.88 us (3%)
  local copies, waits for them, and re-layouts  2.98 us (1%)
    ppermute x36, waiting for transfers between devices, across(): return lax.ppermute(x, 'fsdp', [(f, f ^ k) for f in range(n_f)])  71.5 us
    ppermute x36, starting transfers between devices, across(): return lax.ppermute(x, 'fsdp', [(f, f ^ k) for f in range(n_f)])  35.1 us
    ppermute x15, waiting for transfers between devices, along(): return lax.ppermute(x, 'tensor', [(t, t ^ 2 * k) for t in range(n_t)])  30 us
    ppermute x15, starting transfers between devices, along(): return lax.ppermute(x, 'tensor', [(t, t ^ 2 * k) for t in range(n_t)])  25.9 us
    pallas_call x6, Pallas kernels, forward_half(): pl.pallas_call(kernel, grid_spec=pltpu.PrefetchScalarGridSpec(num_scalar_...  24.6 us
    pallas_call x4, Pallas kernels, input_side(): pl.pallas_call(kernel, grid_spec=pltpu.PrefetchScalarGridSpec(num_scalar_...  17.2 us
    pallas_call x1, Pallas kernels, down_product(): pl.pallas_call(kernel, grid_spec=pltpu.PrefetchScalarGridSpec(num_scalar_...  6.42 us
  transfers between devices with their start and end apart: 56, of which 28 were waited for; matrix products, arithmetic and copies ran while one was open for 3% of the time, Pallas kernels for 20%

profile of v3, /device:TPU:0, one launch (start us, length us, event | category | flops | bytes accessed | tf_op | source)
XLA Modules:
  0.0 221.2 jit_solution(8878309752861097814)
XLA Ops:
  2.1 5.1 %collective-permute-start.2 = (bf16[2,40,512]{2,1,0:T(8,128)(2,1)S(1)}, bf16[2,40,512]{2,1,0:T(8,128)(2,1)S(1)}, u32[]{:S(2)}, u32[]{:S(2)}) collective-permute-start(bf16[2,40,512]{2,1,0:T(8,128)(2,1)S(1)} %get-tuple-element.73), channel_id=1, source_target_pairs={{0,6},{1,7},{2,4},{3,5},{4,2},{5,3},{6,0},{7,1},{8,14},{9,15},{10,... | collective-permute-start | bytes 245768 | tf_op jit(solution)/shard_map/ppermute | solution.py:251
  7.8 2.4 %collective-permute-done.2 = bf16[2,40,512]{2,1,0:T(8,128)(2,1)S(1)} collective-permute-done((bf16[2,40,512]{2,1,0:T(8,128)(2,1)S(1)}, bf16[2,40,512]{2,1,0:T(8,128)(2,1)S(1)}, u32[]{:S(2)}, u32[]{:S(2)}) %collective-permute-start.2) | collective-permute-done | bytes 81952 | tf_op jit(solution)/shard_map/ppermute | solution.py:251
  10.2 3.8 %collective-permute-done.1 = bf16[2,40,512]{2,1,0:T(8,128)(2,1)S(1)} collective-permute-done((bf16[2,40,512]{2,1,0:T(8,128)(2,1)S(1)}, bf16[2,40,512]{2,1,0:T(8,128)(2,1)S(1)}, u32[]{:S(2)}, u32[]{:S(2)}) %collective-permute-start.1) | collective-permute-done | bytes 81952 | tf_op jit(solution)/shard_map/ppermute | solution.py:251
  14.4 2.5 %collective-permute-start.5 = (bf16[2,40,512]{2,1,0:T(8,128)(2,1)S(1)}, bf16[2,40,512]{2,1,0:T(8,128)(2,1)S(1)}, u32[]{:S(2)}, u32[]{:S(2)}) collective-permute-start(bf16[2,40,512]{2,1,0:T(8,128)(2,1)S(1)} %get-tuple-element.69), channel_id=1, source_target_pairs={{0,24},{8,16},{16,8},{24,0},{1,25},{9,17},{17,9},{25,1},{2,26},{10... | collective-permute-start | bytes 245768 | tf_op jit(solution)/shard_map/ppermute | solution.py:248
  22.9 4.4 %collective-permute-done.6 = bf16[4,40,512]{2,1,0:T(8,128)(2,1)S(1)} collective-permute-done((bf16[4,40,512]{2,1,0:T(8,128)(2,1)S(1)}, bf16[4,40,512]{2,1,0:T(8,128)(2,1)S(1)}, u32[]{:S(2)}, u32[]{:S(2)}) %collective-permute-start.6) | collective-permute-done | bytes 163872 | tf_op jit(solution)/shard_map/ppermute | solution.py:251
  28.7 2.3 %collective-permute-start.11 = (bf16[4,40,512]{2,1,0:T(8,128)(2,1)S(1)}, bf16[4,40,512]{2,1,0:T(8,128)(2,1)S(1)}, u32[]{:S(2)}, u32[]{:S(2)}) collective-permute-start(bf16[4,40,512]{2,1,0:T(8,128)(2,1)S(1)} %get-tuple-element.33), channel_id=1, source_target_pairs={{0,6},{1,7},{2,4},{3,5},{4,2},{5,3},{6,0},{7,1},{8,14},{9,15},{10,... | collective-permute-start | bytes 491528 | tf_op jit(solution)/shard_map/ppermute | solution.py:251
  33.3 6.5 %collective-permute-done.10 = bf16[4,40,512]{2,1,0:T(8,128)(2,1)S(1)} collective-permute-done((bf16[4,40,512]{2,1,0:T(8,128)(2,1)S(1)}, bf16[4,40,512]{2,1,0:T(8,128)(2,1)S(1)}, u32[]{:S(2)}, u32[]{:S(2)}) %collective-permute-start.10) | collective-permute-done | bytes 163872 | tf_op jit(solution)/shard_map/ppermute | solution.py:251
  40.0 4.2 %shard_map.95 = (f32[2,2,80,1024]{3,2,1,0:T(8,128)S(1)}, bf16[2,2,80,1024]{3,2,1,0:T(8,128)(2,1)S(1)}) custom-call(s32[1]{0:T(128)} %bitcast.place, s32[8,16]{1,0:T(8,128)S(1)} %dynamic_slice.9.refs_0_.gate_flags, s32[8,16]{1,0:T(8,128)S(1)} %dynamic_slice.10.refs_1_.up_flags, bf16[4,80,512]{2,1,0:T(8,128)(2,1)S(1)} %pad_maximum_fusion.3.refs_2_, ...), custom_call_target="tpu_custom_call" | custom-call | flops 1342177280 | bytes 6815744 | tf_op jit(solution)/shard_map/pallas_call | solution.py:76
  44.7 4.2 %shard_map.96 = (f32[2,2,80,1024]{3,2,1,0:T(8,128)S(1)}, bf16[2,2,80,1024]{3,2,1,0:T(8,128)(2,1)S(1)}) custom-call(s32[1]{0:T(128)} %bitcast.place, s32[8,16]{1,0:T(8,128)S(1)} %dynamic_slice.9.refs_0_.gate_flags, s32[8,16]{1,0:T(8,128)S(1)} %dynamic_slice.10.refs_1_.up_flags, bf16[4,80,512]{2,1,0:T(8,128)(2,1)S(1)} %pad_maximum_fusion.3.refs_2_, ...), custom_call_target="tpu_custom_call" | custom-call | flops 1342177280 | bytes 6815744 | tf_op jit(solution)/shard_map/pallas_call | solution.py:76
  50.6 3.0 %collective-permute-start.23 = (bf16[4,40,512]{2,1,0:T(8,128)(2,1)S(1)}, bf16[4,40,512]{2,1,0:T(8,128)(2,1)S(1)}, u32[]{:S(2)}, u32[]{:S(2)}) collective-permute-start(bf16[4,40,512]{2,1,0:T(8,128)(2,1)S(1)} %get-tuple-element.41), channel_id=1, source_target_pairs={{0,2},{1,3},{2,0},{3,1},{4,6},{5,7},{6,4},{7,5},{8,10},{9,11},{10,... | collective-permute-start | bytes 491528 | tf_op jit(solution)/shard_map/ppermute | solution.py:251
  56.1 4.2 %shard_map.97 = (f32[2,2,80,1024]{3,2,1,0:T(8,128)S(1)}, bf16[2,2,80,1024]{3,2,1,0:T(8,128)(2,1)S(1)}) custom-call(s32[1]{0:T(128)} %bitcast.place, s32[8,16]{1,0:T(8,128)S(1)} %dynamic_slice.9.refs_0_.gate_flags, s32[8,16]{1,0:T(8,128)S(1)} %dynamic_slice.10.refs_1_.up_flags, bf16[4,80,512]{2,1,0:T(8,128)(2,1)S(1)} %constant_dynamic-update-slice_fusion.refs_2_, ...), custom_call_target="tpu_custom_call" | custom-call | flops 1342177280 | bytes 6815744 | tf_op jit(solution)/shard_map/pallas_call | solution.py:76
  60.3 4.2 %shard_map.98 = (f32[2,2,80,1024]{3,2,1,0:T(8,128)S(1)}, bf16[2,2,80,1024]{3,2,1,0:T(8,128)(2,1)S(1)}) custom-call(s32[1]{0:T(128)} %bitcast.place, s32[8,16]{1,0:T(8,128)S(1)} %dynamic_slice.9.refs_0_.gate_flags, s32[8,16]{1,0:T(8,128)S(1)} %dynamic_slice.10.refs_1_.up_flags, bf16[4,80,512]{2,1,0:T(8,128)(2,1)S(1)} %constant_dynamic-update-slice_fusion.refs_2_, ...), custom_call_target="tpu_custom_call" | custom-call | flops 1342177280 | bytes 6815744 | tf_op jit(solution)/shard_map/pallas_call | solution.py:76
  66.0 2.6 %collective-permute-done.24 = bf16[4,40,512]{2,1,0:T(8,128)(2,1)S(1)} collective-permute-done((bf16[4,40,512]{2,1,0:T(8,128)(2,1)S(1)}, bf16[4,40,512]{2,1,0:T(8,128)(2,1)S(1)}, u32[]{:S(2)}, u32[]{:S(2)}) %collective-permute-start.24) | collective-permute-done | bytes 163872 | tf_op jit(solution)/shard_map/ppermute | solution.py:251
  73.0 9.2 %collective-permute-done.13 = bf16[2,2,80,1024]{3,2,1,0:T(8,128)(2,1)S(1)} collective-permute-done((bf16[2,2,80,1024]{3,2,1,0:T(8,128)(2,1)S(1)}, bf16[2,2,80,1024]{3,2,1,0:T(8,128)(2,1)S(1)}, u32[]{:S(2)}, u32[]{:S(2)}) %collective-permute-start.13) | collective-permute-done | bytes 655392 | tf_op jit(solution)/shard_map/ppermute | solution.py:248
  83.1 3.3 %collective-permute-done.19 = bf16[2,2,80,1024]{3,2,1,0:T(8,128)(2,1)S(1)} collective-permute-done((bf16[2,2,80,1024]{3,2,1,0:T(8,128)(2,1)S(1)}, bf16[2,2,80,1024]{3,2,1,0:T(8,128)(2,1)S(1)}, u32[]{:S(2)}, u32[]{:S(2)}) %collective-permute-start.19) | collective-permute-done | bytes 655392 | tf_op jit(solution)/shard_map/ppermute | solution.py:248
  88.2 3.9 %shard_map.99 = (f32[2,1,160,1024]{3,2,1,0:T(8,128)S(1)}, bf16[2,1,160,1024]{3,2,1,0:T(8,128)(2,1)S(1)}) custom-call(s32[1]{0:T(128)} %bitcast.place, s32[16,8]{1,0:T(8,128)S(1)} %copy.18.refs_0_.flags, bf16[4,160,512]{2,1,0:T(8,128)(2,1)S(1)} %constant_dynamic-update-slice_fusion.2.refs_1_.refs_8_, ...), custom_call_target="tpu_custom_call" | custom-call | flops 1342177280 | bytes 5373952 | tf_op jit(solution)/shard_map/pallas_call | solution.py:76
  92.7 3.9 %shard_map.100 = (f32[2,1,160,1024]{3,2,1,0:T(8,128)S(1)}, bf16[2,1,160,1024]{3,2,1,0:T(8,128)(2,1)S(1)}) custom-call(s32[1]{0:T(128)} %bitcast.place, s32[16,8]{1,0:T(8,128)S(1)} %copy.18.refs_0_.flags, bf16[4,160,512]{2,1,0:T(8,128)(2,1)S(1)} %constant_dynamic-update-slice_fusion.2.refs_1_.refs_8_, ...), custom_call_target="tpu_custom_call" | custom-call | flops 1342177280 | bytes 5373952 | tf_op jit(solution)/shard_map/pallas_call | solution.py:76
  101.1 10.2 %collective-permute-done.27 = bf16[2,1,160,1024]{3,2,1,0:T(8,128)(2,1)S(1)} collective-permute-done((bf16[2,1,160,1024]{3,2,1,0:T(8,128)(2,1)S(1)}, bf16[2,1,160,1024]{3,2,1,0:T(8,128)(2,1)S(1)}, u32[]{:S(2)}, u32[]{:S(2)}) %collective-permute-start.27) | collective-permute-done | bytes 655392 | tf_op jit(solution)/shard_map/ppermute | solution.py:248
  115.6 11.9 %collective-permute-done.28 = bf16[1,1,160,1024]{3,2,1,0:T(8,128)(2,1)S(1)} collective-permute-done((bf16[1,1,160,1024]{3,2,1,0:T(8,128)(2,1)S(1)}, bf16[1,1,160,1024]{3,2,1,0:T(8,128)(2,1)S(1)}, u32[]{:S(2)}, u32[]{:S(2)}) %collective-permute-start.28) | collective-permute-done | bytes 327712 | tf_op jit(solution)/shard_map/ppermute | solution.py:248
  128.6 9.6 %collective-permute-done.33 = bf16[1,1,160,1024]{3,2,1,0:T(8,128)(2,1)S(1)} collective-permute-done((bf16[1,1,160,1024]{3,2,1,0:T(8,128)(2,1)S(1)}, bf16[1,1,160,1024]{3,2,1,0:T(8,128)(2,1)S(1)}, u32[]{:S(2)}, u32[]{:S(2)}) %collective-permute-start.33) | collective-permute-done | bytes 327712 | tf_op jit(solution)/shard_map/ppermute | solution.py:248
  143.5 5.3 %collective-permute-done.29.refs_1_ = bf16[2,80,1024]{2,1,0:T(8,128)(2,1)S(1)} collective-permute-done((bf16[2,80,1024]{2,1,0:T(8,128)(2,1)S(1)}, bf16[2,80,1024]{2,1,0:T(8,128)(2,1)S(1)}, u32[]{:S(2)}, u32[]{:S(2)}) %collective-permute-start.29) | collective-permute-done | bytes 327712 | tf_op jit(solution)/shard_map/ppermute | solution.py:248
  150.8 6.1 %collective-permute-done.35.refs_6_ = bf16[2,80,1024]{2,1,0:T(8,128)(2,1)S(1)} collective-permute-done((bf16[2,80,1024]{2,1,0:T(8,128)(2,1)S(1)}, bf16[2,80,1024]{2,1,0:T(8,128)(2,1)S(1)}, u32[]{:S(2)}, u32[]{:S(2)}) %collective-permute-start.35) | collective-permute-done | bytes 327712 | tf_op jit(solution)/shard_map/ppermute | solution.py:248
  158.9 3.9 %collective-permute-done.37.refs_1_ = bf16[2,80,1024]{2,1,0:T(8,128)(2,1)S(1)} collective-permute-done((bf16[2,80,1024]{2,1,0:T(8,128)(2,1)S(1)}, bf16[2,80,1024]{2,1,0:T(8,128)(2,1)S(1)}, u32[]{:S(2)}, u32[]{:S(2)}) %collective-permute-start.37) | collective-permute-done | bytes 327712 | tf_op jit(solution)/shard_map/ppermute | solution.py:248
  167.5 4.2 %shard_map.101 = bf16[4,80,512]{2,1,0:T(8,128)(2,1)S(1)} custom-call(s32[1]{0:T(128)} %bitcast.place, s32[8,16]{1,0:T(8,128)S(1)} %dynamic_slice.9.refs_0_.gate_flags, s32[8,16]{1,0:T(8,128)S(1)} %dynamic_slice.10.refs_1_.up_flags, bf16[2,80,1024]{2,1,0:T(8,128)(2,1)S(1)} %pad_maximum_fusion.6.refs_0_, ...), custom_call_target="tpu_custom_call" | custom-call | flops 1342177280 | bytes 7471104 | tf_op jit(solution)/shard_map/pallas_call | solution.py:138
  171.8 4.4 %shard_map.102 = f32[4,80,512]{2,1,0:T(8,128)S(1)} custom-call(s32[1]{0:T(128)} %bitcast.place, s32[8,16]{1,0:T(8,128)S(1)} %dynamic_slice.9.refs_0_.gate_flags, s32[8,16]{1,0:T(8,128)S(1)} %dynamic_slice.10.refs_1_.up_flags, bf16[2,80,1024]{2,1,0:T(8,128)(2,1)S(1)} %pad_maximum_fusion.6.refs_0_, bf16[2,80,1024]{2,1,0:T(8,128)(2,1)S(1)} %collective-permute-done.29.refs_1_, ...), custom_call_target="tpu_custom_call" | custom-call | flops 1342177280 | bytes 7471104 | tf_op jit(solution)/shard_map/pallas_call | solution.py:138
  176.2 4.2 %shard_map.103 = bf16[4,80,512]{2,1,0:T(8,128)(2,1)S(1)} custom-call(s32[1]{0:T(128)} %bitcast.place, s32[8,16]{1,0:T(8,128)S(1)} %dynamic_slice.9.refs_0_.gate_flags, s32[8,16]{1,0:T(8,128)S(1)} %dynamic_slice.10.refs_1_.up_flags, bf16[2,80,1024]{2,1,0:T(8,128)(2,1)S(1)} %pad_maximum_fusion.8.refs_0_, ...), custom_call_target="tpu_custom_call" | custom-call | flops 1342177280 | bytes 7471104 | tf_op jit(solution)/shard_map/pallas_call | solution.py:138
  182.6 4.2 %shard_map.104 = f32[4,80,512]{2,1,0:T(8,128)S(1)} custom-call(s32[1]{0:T(128)} %bitcast.place, s32[8,16]{1,0:T(8,128)S(1)} %dynamic_slice.9.refs_0_.gate_flags, s32[8,16]{1,0:T(8,128)S(1)} %dynamic_slice.10.refs_1_.up_flags, bf16[2,80,1024]{2,1,0:T(8,128)(2,1)S(1)} %pad_maximum_fusion.8.refs_0_, bf16[2,80,1024]{2,1,0:T(8,128)(2,1)S(1)} %collective-permute-done.37.refs_1_, ...), custom_call_target="tpu_custom_call" | custom-call | flops 1342177280 | bytes 7471104 | tf_op jit(solution)/shard_map/pallas_call | solution.py:138
  187.0 3.3 %collective-permute-start.47 = (bf16[4,40,512]{2,1,0:T(8,128)(2,1)S(1)}, bf16[4,40,512]{2,1,0:T(8,128)(2,1)S(1)}, u32[]{:S(2)}, u32[]{:S(2)}) collective-permute-start(bf16[4,40,512]{2,1,0:T(8,128)(2,1)S(1)} %slice.320), channel_id=1, source_target_pairs={{0,2},{1,3},{2,0},{3,1},{4,6},{5,7},{6,4},{7,5},{8,10},{9,11},{10,... | collective-permute-start | bytes 491528 | tf_op jit(solution)/shard_map/ppermute | solution.py:251
  190.4 2.5 %collective-permute-start.46 = (bf16[4,40,512]{2,1,0:T(8,128)(2,1)S(1)}, bf16[4,40,512]{2,1,0:T(8,128)(2,1)S(1)}, u32[]{:S(2)}, u32[]{:S(2)}) collective-permute-start(bf16[4,40,512]{2,1,0:T(8,128)(2,1)S(1)} %get-tuple-element.65), channel_id=1, source_target_pairs={{0,6},{1,7},{2,4},{3,5},{4,2},{5,3},{6,0},{7,1},{8,14},{9,15},{10,... | collective-permute-start | bytes 491528 | tf_op jit(solution)/shard_map/ppermute | solution.py:251
  192.9 6.4 %shard_map.105 = bf16[2048,1024]{1,0:T(8,128)(2,1)} custom-call(s32[1]{0:T(128)} %bitcast.place, s32[16,8]{1,0:T(8,128)S(1)} %copy.18.refs_0_.flags, bf16[160,1024]{1,0:T(8,128)(2,1)S(1)} %pad_maximum_fusion.4.refs_0_, bf16[160,1024]{1,0:T(8,128)(2,1)S(1)} %collective-permute-done.15.refs_1_, bf16[160,1024]{1,0:T(8,128)(2,1)S(1)} %collective-permute-done.16.refs_2_, ...), custom_call_target="tpu_custom_call" | custom-call | flops 2684354560 | bytes 8126464 | tf_op jit(solution)/shard_map/pallas_call | solution.py:200
  201.3 5.8 %collective-permute-done.45 = bf16[4,40,512]{2,1,0:T(8,128)(2,1)S(1)} collective-permute-done((bf16[4,40,512]{2,1,0:T(8,128)(2,1)S(1)}, bf16[4,40,512]{2,1,0:T(8,128)(2,1)S(1)}, u32[]{:S(2)}, u32[]{:S(2)}) %collective-permute-start.45) | collective-permute-done | bytes 163872 | tf_op jit(solution)/shard_map/ppermute | solution.py:251
  215.5 2.4 %collective-permute-start.53 = (bf16[40,512]{1,0:T(8,128)(2,1)S(1)}, bf16[40,512]{1,0:T(8,128)(2,1)S(1)}, u32[]{:S(2)}, u32[]{:S(2)}) collective-permute-start(bf16[40,512]{1,0:T(8,128)(2,1)S(1)} %get-tuple-element.79), channel_id=1, source_target_pairs={{0,2},{1,3},{2,0},{3,1},{4,6},{5,7},{6,4},{7,5},{8,10},{9,11},{10,... | collective-permute-start | bytes 122888 | tf_op jit(solution)/shard_map/ppermute | solution.py:251
  (167 shorter events, 65.5 us)
Async XLA Ops:
  27.3 12.5 %collective-permute-start.10 = (bf16[4,40,512]{2,1,0:T(8,128)(2,1)S(1)}, bf16[4,40,512]{2,1,0:T(8,128)(2,1)S(1)}, u32[]{:S(2)}, u32[]{:S(2)}) collective-permute-start(bf16[4,40,512]{2,1,0:T(8,128)(2,1)S(1)} %get-tuple-element.33), channel_id=1, source_target_pairs={{0,4},{1,5},{2,6},{3,7},{4,0},{5,1},{6,2},{7,3},{8,12},{9,13},{10,... | collective-permute-start | bytes 491528 | tf_op jit(solution)/shard_map/ppermute | solution.py:251
  39.9 14.7 %collective-permute-start.12 = (bf16[4,80,512]{2,1,0:T(8,128)(2,1)S(1)}, bf16[4,80,512]{2,1,0:T(8,128)(2,1)S(1)}, u32[]{:S(2)}, u32[]{:S(2)}) collective-permute-start(bf16[4,80,512]{2,1,0:T(8,128)(2,1)S(1)} %constant_dynamic-update-slice_fusion.refs_2_), channel_id=1, source_target_pairs={{0,1},{1,0},{2,3},{3,2},{4,5},{5,4},{6,7},{7,6},{8,9},{9,8},{10,11... | collective-permute-start | bytes 983048 | tf_op jit(solution)/shard_map/ppermute | solution.py:254
  44.2 25.2 %collective-permute-start.8 = (bf16[2,2,80,1024]{3,2,1,0:T(8,128)(2,1)S(1)}, bf16[2,2,80,1024]{3,2,1,0:T(8,128)(2,1)S(1)}, u32[]{:S(2)}, u32[]{:S(2)}) collective-permute-start(bf16[2,2,80,1024]{3,2,1,0:T(8,128)(2,1)S(1)} %get-tuple-element.28), channel_id=1, source_target_pairs={{0,8},{8,0},{16,24},{24,16},{1,9},{9,1},{17,25},{25,17},{2,10},{10... | collective-permute-start | bytes 1966088 | tf_op jit(solution)/shard_map/ppermute | solution.py:248
  48.8 22.3 %collective-permute-start.17 = (bf16[2,2,80,1024]{3,2,1,0:T(8,128)(2,1)S(1)}, bf16[2,2,80,1024]{3,2,1,0:T(8,128)(2,1)S(1)}, u32[]{:S(2)}, u32[]{:S(2)}) collective-permute-start(bf16[2,2,80,1024]{3,2,1,0:T(8,128)(2,1)S(1)} %get-tuple-element.31), channel_id=1, source_target_pairs={{0,16},{8,24},{16,0},{24,8},{1,17},{9,25},{17,1},{25,9},{2,18},{10... | collective-permute-start | bytes 1966088 | tf_op jit(solution)/shard_map/ppermute | solution.py:248
  50.6 13.8 %collective-permute-start.23 = (bf16[4,40,512]{2,1,0:T(8,128)(2,1)S(1)}, bf16[4,40,512]{2,1,0:T(8,128)(2,1)S(1)}, u32[]{:S(2)}, u32[]{:S(2)}) collective-permute-start(bf16[4,40,512]{2,1,0:T(8,128)(2,1)S(1)} %get-tuple-element.41), channel_id=1, source_target_pairs={{0,2},{1,3},{2,0},{3,1},{4,6},{5,7},{6,4},{7,5},{8,10},{9,11},{10,... | collective-permute-start | bytes 491528 | tf_op jit(solution)/shard_map/ppermute | solution.py:251
  53.6 15.0 %collective-permute-start.24 = (bf16[4,40,512]{2,1,0:T(8,128)(2,1)S(1)}, bf16[4,40,512]{2,1,0:T(8,128)(2,1)S(1)}, u32[]{:S(2)}, u32[]{:S(2)}) collective-permute-start(bf16[4,40,512]{2,1,0:T(8,128)(2,1)S(1)} %get-tuple-element.41), channel_id=1, source_target_pairs={{0,4},{1,5},{2,6},{3,7},{4,0},{5,1},{6,2},{7,3},{8,12},{9,13},{10,... | collective-permute-start | bytes 491528 | tf_op jit(solution)/shard_map/ppermute | solution.py:251
  54.6 14.7 %collective-permute-start.25 = (bf16[4,40,512]{2,1,0:T(8,128)(2,1)S(1)}, bf16[4,40,512]{2,1,0:T(8,128)(2,1)S(1)}, u32[]{:S(2)}, u32[]{:S(2)}) collective-permute-start(bf16[4,40,512]{2,1,0:T(8,128)(2,1)S(1)} %get-tuple-element.41), channel_id=1, source_target_pairs={{0,6},{1,7},{2,4},{3,5},{4,2},{5,3},{6,0},{7,1},{8,14},{9,15},{10,... | collective-permute-start | bytes 491528 | tf_op jit(solution)/shard_map/ppermute | solution.py:251
  64.5 17.7 %collective-permute-start.13 = (bf16[2,2,80,1024]{3,2,1,0:T(8,128)(2,1)S(1)}, bf16[2,2,80,1024]{3,2,1,0:T(8,128)(2,1)S(1)}, u32[]{:S(2)}, u32[]{:S(2)}) collective-permute-start(bf16[2,2,80,1024]{3,2,1,0:T(8,128)(2,1)S(1)} %get-tuple-element.35), channel_id=1, source_target_pairs={{0,8},{8,0},{16,24},{24,16},{1,9},{9,1},{17,25},{25,17},{2,10},{10... | collective-permute-start | bytes 1966088 | tf_op jit(solution)/shard_map/ppermute | solution.py:248
  68.7 17.7 %collective-permute-start.19 = (bf16[2,2,80,1024]{3,2,1,0:T(8,128)(2,1)S(1)}, bf16[2,2,80,1024]{3,2,1,0:T(8,128)(2,1)S(1)}, u32[]{:S(2)}, u32[]{:S(2)}) collective-permute-start(bf16[2,2,80,1024]{3,2,1,0:T(8,128)(2,1)S(1)} %get-tuple-element.38), channel_id=1, source_target_pairs={{0,16},{8,24},{16,0},{24,8},{1,17},{9,25},{17,1},{25,9},{2,18},{10... | collective-permute-start | bytes 1966088 | tf_op jit(solution)/shard_map/ppermute | solution.py:248
  69.3 18.9 %collective-permute-start.26 = (bf16[4,160,512]{2,1,0:T(8,128)(2,1)S(1)}, bf16[4,160,512]{2,1,0:T(8,128)(2,1)S(1)}, u32[]{:S(2)}, u32[]{:S(2)}) collective-permute-start(bf16[4,160,512]{2,1,0:T(8,128)(2,1)S(1)} %constant_dynamic-update-slice_fusion.2.refs_1_.refs_8_), channel_id=1, source_target_pairs={{0,1},{1,0},{2,3},{3,2},{4,5},{5,4},{6,7},{7,6},{8,9},{9,8},{10,11... | collective-permute-start | bytes 1966088 | tf_op jit(solution)/shard_map/ppermute | solution.py:254
  69.7 26.9 %collective-permute-start.9 = (bf16[1,2,80,1024]{3,2,1,0:T(8,128)(2,1)S(1)}, bf16[1,2,80,1024]{3,2,1,0:T(8,128)(2,1)S(1)}, u32[]{:S(2)}, u32[]{:S(2)}) collective-permute-start(bf16[1,2,80,1024]{3,2,1,0:T(8,128)(2,1)S(1)} %slice.319), channel_id=1, source_target_pairs={{0,16},{8,24},{16,0},{24,8},{1,17},{9,25},{17,1},{25,9},{2,18},{10... | collective-permute-start | bytes 983048 | tf_op jit(solution)/shard_map/ppermute | solution.py:248
  71.5 25.9 %collective-permute-start.18 = (bf16[1,2,80,1024]{3,2,1,0:T(8,128)(2,1)S(1)}, bf16[1,2,80,1024]{3,2,1,0:T(8,128)(2,1)S(1)}, u32[]{:S(2)}, u32[]{:S(2)}) collective-permute-start(bf16[1,2,80,1024]{3,2,1,0:T(8,128)(2,1)S(1)} %slice.317), channel_id=1, source_target_pairs={{0,8},{8,0},{16,24},{24,16},{1,9},{9,1},{17,25},{25,17},{2,10},{10... | collective-permute-start | bytes 983048 | tf_op jit(solution)/shard_map/ppermute | solution.py:248
  82.4 17.3 %collective-permute-start.14 = (bf16[1,2,80,1024]{3,2,1,0:T(8,128)(2,1)S(1)}, bf16[1,2,80,1024]{3,2,1,0:T(8,128)(2,1)S(1)}, u32[]{:S(2)}, u32[]{:S(2)}) collective-permute-start(bf16[1,2,80,1024]{3,2,1,0:T(8,128)(2,1)S(1)} %slice.318), channel_id=1, source_target_pairs={{0,16},{8,24},{16,0},{24,8},{1,17},{9,25},{17,1},{25,9},{2,18},{10... | collective-permute-start | bytes 983048 | tf_op jit(solution)/shard_map/ppermute | solution.py:248
  86.6 14.3 %collective-permute-start.20 = (bf16[1,2,80,1024]{3,2,1,0:T(8,128)(2,1)S(1)}, bf16[1,2,80,1024]{3,2,1,0:T(8,128)(2,1)S(1)}, u32[]{:S(2)}, u32[]{:S(2)}) collective-permute-start(bf16[1,2,80,1024]{3,2,1,0:T(8,128)(2,1)S(1)} %slice.316), channel_id=1, source_target_pairs={{0,8},{8,0},{16,24},{24,16},{1,9},{9,1},{17,25},{25,17},{2,10},{10... | collective-permute-start | bytes 983048 | tf_op jit(solution)/shard_map/ppermute | solution.py:248
  92.1 19.3 %collective-permute-start.27 = (bf16[2,1,160,1024]{3,2,1,0:T(8,128)(2,1)S(1)}, bf16[2,1,160,1024]{3,2,1,0:T(8,128)(2,1)S(1)}, u32[]{:S(2)}, u32[]{:S(2)}) collective-permute-start(bf16[2,1,160,1024]{3,2,1,0:T(8,128)(2,1)S(1)} %get-tuple-element.43), channel_id=1, source_target_pairs={{0,8},{8,0},{16,24},{24,16},{1,9},{9,1},{17,25},{25,17},{2,10},{10... | collective-permute-start | bytes 1966088 | tf_op jit(solution)/shard_map/ppermute | solution.py:248
  96.6 17.7 %collective-permute-start.32 = (bf16[2,1,160,1024]{3,2,1,0:T(8,128)(2,1)S(1)}, bf16[2,1,160,1024]{3,2,1,0:T(8,128)(2,1)S(1)}, u32[]{:S(2)}, u32[]{:S(2)}) collective-permute-start(bf16[2,1,160,1024]{3,2,1,0:T(8,128)(2,1)S(1)} %get-tuple-element.46), channel_id=1, source_target_pairs={{0,16},{8,24},{16,0},{24,8},{1,17},{9,25},{17,1},{25,9},{2,18},{10... | collective-permute-start | bytes 1966088 | tf_op jit(solution)/shard_map/ppermute | solution.py:248
  100.0 39.1 %collective-permute-start.15 = (bf16[160,1024]{1,0:T(8,128)(2,1)S(1)}, bf16[160,1024]{1,0:T(8,128)(2,1)S(1)}, u32[]{:S(2)}, u32[]{:S(2)}) collective-permute-start(bf16[160,1024]{1,0:T(8,128)(2,1)S(1)} %pad_maximum_fusion.4.refs_0_), channel_id=1, source_target_pairs={{0,8},{8,0},{16,24},{24,16},{1,9},{9,1},{17,25},{25,17},{2,10},{10... | collective-permute-start | bytes 983048 | tf_op jit(solution)/shard_map/ppermute | solution.py:248
  100.1 40.0 %collective-permute-start.16 = (bf16[160,1024]{1,0:T(8,128)(2,1)S(1)}, bf16[160,1024]{1,0:T(8,128)(2,1)S(1)}, u32[]{:S(2)}, u32[]{:S(2)}) collective-permute-start(bf16[160,1024]{1,0:T(8,128)(2,1)S(1)} %pad_maximum_fusion.4.refs_0_), channel_id=1, source_target_pairs={{0,16},{8,24},{16,0},{24,8},{1,17},{9,25},{17,1},{25,9},{2,18},{10... | collective-permute-start | bytes 983048 | tf_op jit(solution)/shard_map/ppermute | solution.py:248
  111.6 15.8 %collective-permute-start.28 = (bf16[1,1,160,1024]{3,2,1,0:T(8,128)(2,1)S(1)}, bf16[1,1,160,1024]{3,2,1,0:T(8,128)(2,1)S(1)}, u32[]{:S(2)}, u32[]{:S(2)}) collective-permute-start(bf16[1,1,160,1024]{3,2,1,0:T(8,128)(2,1)S(1)} %slice.315), channel_id=1, source_target_pairs={{0,16},{8,24},{16,0},{24,8},{1,17},{9,25},{17,1},{25,9},{2,18},{10... | collective-permute-start | bytes 983048 | tf_op jit(solution)/shard_map/ppermute | solution.py:248
  112.3 29.1 %collective-permute-start.21 = (bf16[160,1024]{1,0:T(8,128)(2,1)S(1)}, bf16[160,1024]{1,0:T(8,128)(2,1)S(1)}, u32[]{:S(2)}, u32[]{:S(2)}) collective-permute-start(bf16[160,1024]{1,0:T(8,128)(2,1)S(1)} %pad_maximum_fusion.5.refs_4_), channel_id=1, source_target_pairs={{0,8},{8,0},{16,24},{24,16},{1,9},{9,1},{17,25},{25,17},{2,10},{10... | collective-permute-start | bytes 983048 | tf_op jit(solution)/shard_map/ppermute | solution.py:248
  114.4 28.7 %collective-permute-start.22 = (bf16[160,1024]{1,0:T(8,128)(2,1)S(1)}, bf16[160,1024]{1,0:T(8,128)(2,1)S(1)}, u32[]{:S(2)}, u32[]{:S(2)}) collective-permute-start(bf16[160,1024]{1,0:T(8,128)(2,1)S(1)} %pad_maximum_fusion.5.refs_4_), channel_id=1, source_target_pairs={{0,16},{8,24},{16,0},{24,8},{1,17},{9,25},{17,1},{25,9},{2,18},{10... | collective-permute-start | bytes 983048 | tf_op jit(solution)/shard_map/ppermute | solution.py:248
  140.1 16.8 %collective-permute-start.35 = (bf16[2,80,1024]{2,1,0:T(8,128)(2,1)S(1)}, bf16[2,80,1024]{2,1,0:T(8,128)(2,1)S(1)}, u32[]{:S(2)}, u32[]{:S(2)}) collective-permute-start(bf16[2,80,1024]{2,1,0:T(8,128)(2,1)S(1)} %pad_maximum_fusion.7.refs_4_), channel_id=1, source_target_pairs={{0,16},{8,24},{16,0},{24,8},{1,17},{9,25},{17,1},{25,9},{2,18},{10... | collective-permute-start | bytes 983048 | tf_op jit(solution)/shard_map/ppermute | solution.py:248
  141.4 17.0 %collective-permute-start.34 = (bf16[2,80,1024]{2,1,0:T(8,128)(2,1)S(1)}, bf16[2,80,1024]{2,1,0:T(8,128)(2,1)S(1)}, u32[]{:S(2)}, u32[]{:S(2)}) collective-permute-start(bf16[2,80,1024]{2,1,0:T(8,128)(2,1)S(1)} %pad_maximum_fusion.7.refs_4_), channel_id=1, source_target_pairs={{0,8},{8,0},{16,24},{24,16},{1,9},{9,1},{17,25},{25,17},{2,10},{10... | collective-permute-start | bytes 983048 | tf_op jit(solution)/shard_map/ppermute | solution.py:248
  143.0 19.8 %collective-permute-start.37 = (bf16[2,80,1024]{2,1,0:T(8,128)(2,1)S(1)}, bf16[2,80,1024]{2,1,0:T(8,128)(2,1)S(1)}, u32[]{:S(2)}, u32[]{:S(2)}) collective-permute-start(bf16[2,80,1024]{2,1,0:T(8,128)(2,1)S(1)} %pad_maximum_fusion.8.refs_0_), channel_id=1, source_target_pairs={{0,8},{8,0},{16,24},{24,16},{1,9},{9,1},{17,25},{25,17},{2,10},{10... | collective-permute-start | bytes 983048 | tf_op jit(solution)/shard_map/ppermute | solution.py:248
  148.8 14.5 %collective-permute-start.41 = (bf16[2,80,1024]{2,1,0:T(8,128)(2,1)S(1)}, bf16[2,80,1024]{2,1,0:T(8,128)(2,1)S(1)}, u32[]{:S(2)}, u32[]{:S(2)}) collective-permute-start(bf16[2,80,1024]{2,1,0:T(8,128)(2,1)S(1)} %pad_maximum_fusion.9.refs_4_), channel_id=1, source_target_pairs={{0,16},{8,24},{16,0},{24,8},{1,17},{9,25},{17,1},{25,9},{2,18},{10... | collective-permute-start | bytes 983048 | tf_op jit(solution)/shard_map/ppermute | solution.py:248
  149.8 16.3 %collective-permute-start.31 = (bf16[2,80,1024]{2,1,0:T(8,128)(2,1)S(1)}, bf16[2,80,1024]{2,1,0:T(8,128)(2,1)S(1)}, u32[]{:S(2)}, u32[]{:S(2)}) collective-permute-start(bf16[2,80,1024]{2,1,0:T(8,128)(2,1)S(1)} %collective-permute-done.29.refs_1_), channel_id=1, source_target_pairs={{0,16},{8,24},{16,0},{24,8},{1,17},{9,25},{17,1},{25,9},{2,18},{10... | collective-permute-start | bytes 983048 | tf_op jit(solution)/shard_map/ppermute | solution.py:248
  158.4 17.8 %collective-permute-start.38 = (bf16[2,80,1024]{2,1,0:T(8,128)(2,1)S(1)}, bf16[2,80,1024]{2,1,0:T(8,128)(2,1)S(1)}, u32[]{:S(2)}, u32[]{:S(2)}) collective-permute-start(bf16[2,80,1024]{2,1,0:T(8,128)(2,1)S(1)} %pad_maximum_fusion.8.refs_0_), channel_id=1, source_target_pairs={{0,16},{8,24},{16,0},{24,8},{1,17},{9,25},{17,1},{25,9},{2,18},{10... | collective-permute-start | bytes 983048 | tf_op jit(solution)/shard_map/ppermute | solution.py:248
  162.8 13.4 %collective-permute-start.40 = (bf16[2,80,1024]{2,1,0:T(8,128)(2,1)S(1)}, bf16[2,80,1024]{2,1,0:T(8,128)(2,1)S(1)}, u32[]{:S(2)}, u32[]{:S(2)}) collective-permute-start(bf16[2,80,1024]{2,1,0:T(8,128)(2,1)S(1)} %pad_maximum_fusion.9.refs_4_), channel_id=1, source_target_pairs={{0,8},{8,0},{16,24},{24,16},{1,9},{9,1},{17,25},{25,17},{2,10},{10... | collective-permute-start | bytes 983048 | tf_op jit(solution)/shard_map/ppermute | solution.py:248
  163.3 12.9 %collective-permute-start.39 = (bf16[2,80,1024]{2,1,0:T(8,128)(2,1)S(1)}, bf16[2,80,1024]{2,1,0:T(8,128)(2,1)S(1)}, u32[]{:S(2)}, u32[]{:S(2)}) collective-permute-start(bf16[2,80,1024]{2,1,0:T(8,128)(2,1)S(1)} %collective-permute-done.37.refs_1_), channel_id=1, source_target_pairs={{0,16},{8,24},{16,0},{24,8},{1,17},{9,25},{17,1},{25,9},{2,18},{10... | collective-permute-start | bytes 983048 | tf_op jit(solution)/shard_map/ppermute | solution.py:248
  180.6 12.3 %collective-permute-start.48 = (bf16[160,1024]{1,0:T(8,128)(2,1)S(1)}, bf16[160,1024]{1,0:T(8,128)(2,1)S(1)}, u32[]{:S(2)}, u32[]{:S(2)}) collective-permute-start(bf16[160,1024]{1,0:T(8,128)(2,1)S(1)} %collective-permute-done.15.refs_1_), channel_id=1, source_target_pairs={{0,16},{8,24},{16,0},{24,8},{1,17},{9,25},{17,1},{25,9},{2,18},{10... | collective-permute-start | bytes 983048 | tf_op jit(solution)/shard_map/ppermute | solution.py:248
  187.0 12.3 %collective-permute-start.47 = (bf16[4,40,512]{2,1,0:T(8,128)(2,1)S(1)}, bf16[4,40,512]{2,1,0:T(8,128)(2,1)S(1)}, u32[]{:S(2)}, u32[]{:S(2)}) collective-permute-start(bf16[4,40,512]{2,1,0:T(8,128)(2,1)S(1)} %slice.320), channel_id=1, source_target_pairs={{0,2},{1,3},{2,0},{3,1},{4,6},{5,7},{6,4},{7,5},{8,10},{9,11},{10,... | collective-permute-start | bytes 491528 | tf_op jit(solution)/shard_map/ppermute | solution.py:251
  192.9 14.2 %collective-permute-start.45 = (bf16[4,40,512]{2,1,0:T(8,128)(2,1)S(1)}, bf16[4,40,512]{2,1,0:T(8,128)(2,1)S(1)}, u32[]{:S(2)}, u32[]{:S(2)}) collective-permute-start(bf16[4,40,512]{2,1,0:T(8,128)(2,1)S(1)} %get-tuple-element.64), channel_id=1, source_target_pairs={{0,4},{1,5},{2,6},{3,7},{4,0},{5,1},{6,2},{7,3},{8,12},{9,13},{10,... | collective-permute-start | bytes 491528 | tf_op jit(solution)/shard_map/ppermute | solution.py:251
  (26 other events, 185.0 us)

commit v4 on v3

--- a/solution.py
+++ b/solution.py
@@ -8,7 +8,7 @@
 from jax.sharding import PartitionSpec as P
 
 BLOCK = 128
-VMEM_BYTES = 48 * 1024 * 1024
+VMEM_BYTES = 28 * 1024 * 1024
 
 
 def keep_blocks(weight, flag_of):
@@ -341,30 +341,30 @@
     def both_halves(p):
         return [x for half in range(2) for x in gathered(grads[p][half], bit_orders[half])]
 
-    def plane_sums(part, first):
-        return [
-            along(part[:, i * sub : (i + 1) * sub].astype(jnp.bfloat16), first + i)
-            for i in range(part.shape[1] // sub)
-            if first + i
-        ]
-
     hidden_pieces = [
         gathered(jnp.concatenate(hidden[half]), bit_orders[half]) for half in range(2)
     ]
     far_part, far_mine = chip_sum(
         both_halves(1), *[x for held in hidden_pieces for x in held[:-1]]
     )
-    far_sums = plane_sums(far_part, n_f // 2)
     near_part, near_mine = chip_sum(both_halves(0), far_mine)
-    near_sums = plane_sums(near_part, 0)
-    down_grad = down_product(after(place, near_mine), down_flags, g_parts, hidden_pieces)
-    near_sums[-1] = after(near_sums[-1], down_grad)
-    total = near_part[:, :sub]
-    for received in far_sums + near_sums:
-        total = total + received.astype(jnp.float32)
-    back = swapped(total.astype(jnp.bfloat16), across)
-    back = swapped(reordered(back, plane ^ f_index), along)
-    input_grad = reordered(back, plane).reshape(rows, width)
+    def to_rows(part):
+        part = part.astype(jnp.bfloat16)
+        terms = [part[0]] + [across(part[m], m) for m in range(1, n_f)]
+        for b in range(bits):
+            odd = ((plane ^ f_index) >> b) & 1 == 1
+            terms = [jnp.where(odd, terms[i ^ (1 << b)], x) for i, x in enumerate(terms)]
+        return terms
+
+    terms = [jnp.concatenate(x) for x in zip(to_rows(near_part), to_rows(far_part))]
+    total = jnp.zeros((n_f, sub, width), jnp.float32)
+    for k in range(n_f):
+        term = along(terms[k], k) if k else terms[k]
+        axes = [bits - 1 - b for b in range(bits) if (k >> b) & 1]
+        flipped = jnp.flip(term.reshape((2,) * bits + (sub, width)), axes)
+        total = total + flipped.reshape(n_f, sub, width).astype(jnp.float32)
+    input_grad = reordered(total.astype(jnp.bfloat16), plane).reshape(rows, width)
+    down_grad = down_product(after(place, *terms), down_flags, g_parts, hidden_pieces)
     return (input_grad, down_grad)
 
 

time: 222 us -> 215 us (0.968)
  Pallas kernels: 48.1 us -> 35.1 us
  starting transfers between devices: 61.3 us -> 69.7 us
  waiting for transfers between devices: 102 us -> 94.6 us
  local copies, waits for them, and re-layouts: 2.98 us -> 7.3 us
    ppermute x36 -> x39, starting transfers between devices: 35.1 us -> 48 us  [across(): return lax.ppermute(x, 'fsdp', [(f, f ^ k) for f in range(n_f)])]
    pallas_call x6, Pallas kernels: 24.6 us -> 17.3 us  [forward_half(): pl.pallas_call(kernel, grid_spec=pltpu.PrefetchScalarGridSpec(num_scalar_...]
    pallas_call x4, Pallas kernels: 17.2 us -> 11.4 us  [input_side(): pl.pallas_call(kernel, grid_spec=pltpu.PrefetchScalarGridSpec(num_scalar_...]
    ppermute x36 -> x39, waiting for transfers between devices: 71.5 us -> 66.9 us  [across(): return lax.ppermute(x, 'fsdp', [(f, f ^ k) for f in range(n_f)])]
    ppermute x15 -> x12, starting transfers between devices: 25.9 us -> 21.3 us  [along(): return lax.ppermute(x, 'tensor', [(t, t ^ 2 * k) for t in range(n_t)])]
    unnamed x9 -> x19, local copies, waits for them, and re-layouts: 0.13 us -> 4.51 us
    ppermute x15 -> x12, waiting for transfers between devices: 30 us -> 27.8 us  [along(): return lax.ppermute(x, 'tensor', [(t, t ^ 2 * k) for t in range(n_t)])]
  transfers between devices with their start and end apart: 56 -> 56, of which waited for: 28 -> 24; matrix products, arithmetic and copies ran while one was open for 3% -> 3% of each run, Pallas kernels for 20% -> 16%
where the time goes in v4:
time: 215 us; the launch traced here: 214 us
  waiting for transfers between devices  94.6 us (44%)
  starting transfers between devices  69.7 us (32%)
  Pallas kernels  35.1 us (16%)
  local copies, waits for them, and re-layouts  7.3 us (3%)
  other arithmetic  6.09 us (3%)
    ppermute x39, waiting for transfers between devices, across(): return lax.ppermute(x, 'fsdp', [(f, f ^ k) for f in range(n_f)])  66.9 us
    ppermute x39, starting transfers between devices, across(): return lax.ppermute(x, 'fsdp', [(f, f ^ k) for f in range(n_f)])  48 us
    ppermute x12, waiting for transfers between devices, along(): return lax.ppermute(x, 'tensor', [(t, t ^ 2 * k) for t in range(n_t)])  27.8 us
    ppermute x12, starting transfers between devices, along(): return lax.ppermute(x, 'tensor', [(t, t ^ 2 * k) for t in range(n_t)])  21.3 us
    pallas_call x6, Pallas kernels, forward_half(): pl.pallas_call(kernel, grid_spec=pltpu.PrefetchScalarGridSpec(num_scalar_...  17.3 us
    pallas_call x4, Pallas kernels, input_side(): pl.pallas_call(kernel, grid_spec=pltpu.PrefetchScalarGridSpec(num_scalar_...  11.4 us
    pallas_call x1, Pallas kernels, down_product(): pl.pallas_call(kernel, grid_spec=pltpu.PrefetchScalarGridSpec(num_scalar_...  6.42 us
    unnamed x19, local copies, waits for them, and re-layouts  4.51 us
  transfers between devices with their start and end apart: 56, of which 24 were waited for; matrix products, arithmetic and copies ran while one was open for 3% of the time, Pallas kernels for 16%

profile of v4, /device:TPU:0, one launch (start us, length us, event | category | flops | bytes accessed | tf_op | source)
XLA Modules:
  0.0 214.2 jit_solution(5883761250750644933)
XLA Ops:
  2.1 5.1 %collective-permute-start.2 = (bf16[2,40,512]{2,1,0:T(8,128)(2,1)S(1)}, bf16[2,40,512]{2,1,0:T(8,128)(2,1)S(1)}, u32[]{:S(2)}, u32[]{:S(2)}) collective-permute-start(bf16[2,40,512]{2,1,0:T(8,128)(2,1)S(1)} %get-tuple-element.83), channel_id=1, source_target_pairs={{0,6},{1,7},{2,4},{3,5},{4,2},{5,3},{6,0},{7,1},{8,14},{9,15},{10,... | collective-permute-start | bytes 245768 | tf_op jit(solution)/shard_map/ppermute | solution.py:251
  10.2 3.8 %collective-permute-done.1 = bf16[2,40,512]{2,1,0:T(8,128)(2,1)S(1)} collective-permute-done((bf16[2,40,512]{2,1,0:T(8,128)(2,1)S(1)}, bf16[2,40,512]{2,1,0:T(8,128)(2,1)S(1)}, u32[]{:S(2)}, u32[]{:S(2)}) %collective-permute-start.1) | collective-permute-done | bytes 81952 | tf_op jit(solution)/shard_map/ppermute | solution.py:251
  14.4 2.5 %collective-permute-start.5 = (bf16[2,40,512]{2,1,0:T(8,128)(2,1)S(1)}, bf16[2,40,512]{2,1,0:T(8,128)(2,1)S(1)}, u32[]{:S(2)}, u32[]{:S(2)}) collective-permute-start(bf16[2,40,512]{2,1,0:T(8,128)(2,1)S(1)} %get-tuple-element.79), channel_id=1, source_target_pairs={{0,24},{8,16},{16,8},{24,0},{1,25},{9,17},{17,9},{25,1},{2,26},{10... | collective-permute-start | bytes 245768 | tf_op jit(solution)/shard_map/ppermute | solution.py:248
  22.9 4.4 %collective-permute-done.6 = bf16[4,40,512]{2,1,0:T(8,128)(2,1)S(1)} collective-permute-done((bf16[4,40,512]{2,1,0:T(8,128)(2,1)S(1)}, bf16[4,40,512]{2,1,0:T(8,128)(2,1)S(1)}, u32[]{:S(2)}, u32[]{:S(2)}) %collective-permute-start.6) | collective-permute-done | bytes 163872 | tf_op jit(solution)/shard_map/ppermute | solution.py:251
  33.3 6.5 %collective-permute-done.10 = bf16[4,40,512]{2,1,0:T(8,128)(2,1)S(1)} collective-permute-done((bf16[4,40,512]{2,1,0:T(8,128)(2,1)S(1)}, bf16[4,40,512]{2,1,0:T(8,128)(2,1)S(1)}, u32[]{:S(2)}, u32[]{:S(2)}) %collective-permute-start.10) | collective-permute-done | bytes 163872 | tf_op jit(solution)/shard_map/ppermute | solution.py:251
  44.4 3.0 %shard_map.95 = (f32[2,2,80,1024]{3,2,1,0:T(8,128)S(1)}, bf16[2,2,80,1024]{3,2,1,0:T(8,128)(2,1)S(1)}) custom-call(s32[1]{0:T(128)} %bitcast.place, s32[8,16]{1,0:T(8,128)S(1)} %dynamic_slice.9.refs_0_.gate_flags, s32[8,16]{1,0:T(8,128)S(1)} %dynamic_slice.10.refs_1_.up_flags, bf16[4,80,512]{2,1,0:T(8,128)(2,1)S(1)} %pad_maximum_fusion.3.refs_2_, ...), custom_call_target="tpu_custom_call" | custom-call | flops 1342177280 | bytes 6815744 | tf_op jit(solution)/shard_map/pallas_call | solution.py:76
  47.8 3.0 %shard_map.96 = (f32[2,2,80,1024]{3,2,1,0:T(8,128)S(1)}, bf16[2,2,80,1024]{3,2,1,0:T(8,128)(2,1)S(1)}) custom-call(s32[1]{0:T(128)} %bitcast.place, s32[8,16]{1,0:T(8,128)S(1)} %dynamic_slice.9.refs_0_.gate_flags, s32[8,16]{1,0:T(8,128)S(1)} %dynamic_slice.10.refs_1_.up_flags, bf16[4,80,512]{2,1,0:T(8,128)(2,1)S(1)} %pad_maximum_fusion.3.refs_2_, ...), custom_call_target="tpu_custom_call" | custom-call | flops 1342177280 | bytes 6815744 | tf_op jit(solution)/shard_map/pallas_call | solution.py:76
  52.6 3.0 %collective-permute-start.23 = (bf16[4,40,512]{2,1,0:T(8,128)(2,1)S(1)}, bf16[4,40,512]{2,1,0:T(8,128)(2,1)S(1)}, u32[]{:S(2)}, u32[]{:S(2)}) collective-permute-start(bf16[4,40,512]{2,1,0:T(8,128)(2,1)S(1)} %get-tuple-element.40), channel_id=1, source_target_pairs={{0,2},{1,3},{2,0},{3,1},{4,6},{5,7},{6,4},{7,5},{8,10},{9,11},{10,... | collective-permute-start | bytes 491528 | tf_op jit(solution)/shard_map/ppermute | solution.py:251
  58.1 3.0 %shard_map.97 = (f32[2,2,80,1024]{3,2,1,0:T(8,128)S(1)}, bf16[2,2,80,1024]{3,2,1,0:T(8,128)(2,1)S(1)}) custom-call(s32[1]{0:T(128)} %bitcast.place, s32[8,16]{1,0:T(8,128)S(1)} %dynamic_slice.9.refs_0_.gate_flags, s32[8,16]{1,0:T(8,128)S(1)} %dynamic_slice.10.refs_1_.up_flags, bf16[4,80,512]{2,1,0:T(8,128)(2,1)S(1)} %constant_dynamic-update-slice_fusion.refs_2_, ...), custom_call_target="tpu_custom_call" | custom-call | flops 1342177280 | bytes 6815744 | tf_op jit(solution)/shard_map/pallas_call | solution.py:76
  61.0 3.0 %shard_map.98 = (f32[2,2,80,1024]{3,2,1,0:T(8,128)S(1)}, bf16[2,2,80,1024]{3,2,1,0:T(8,128)(2,1)S(1)}) custom-call(s32[1]{0:T(128)} %bitcast.place, s32[8,16]{1,0:T(8,128)S(1)} %dynamic_slice.9.refs_0_.gate_flags, s32[8,16]{1,0:T(8,128)S(1)} %dynamic_slice.10.refs_1_.up_flags, bf16[4,80,512]{2,1,0:T(8,128)(2,1)S(1)} %constant_dynamic-update-slice_fusion.refs_2_, ...), custom_call_target="tpu_custom_call" | custom-call | flops 1342177280 | bytes 6815744 | tf_op jit(solution)/shard_map/pallas_call | solution.py:76
  65.6 5.0 %collective-permute-done.24 = bf16[4,40,512]{2,1,0:T(8,128)(2,1)S(1)} collective-permute-done((bf16[4,40,512]{2,1,0:T(8,128)(2,1)S(1)}, bf16[4,40,512]{2,1,0:T(8,128)(2,1)S(1)}, u32[]{:S(2)}, u32[]{:S(2)}) %collective-permute-start.24) | collective-permute-done | bytes 163872 | tf_op jit(solution)/shard_map/ppermute | solution.py:251
  75.0 6.8 %collective-permute-done.13 = bf16[2,2,80,1024]{3,2,1,0:T(8,128)(2,1)S(1)} collective-permute-done((bf16[2,2,80,1024]{3,2,1,0:T(8,128)(2,1)S(1)}, bf16[2,2,80,1024]{3,2,1,0:T(8,128)(2,1)S(1)}, u32[]{:S(2)}, u32[]{:S(2)}) %collective-permute-start.13) | collective-permute-done | bytes 655392 | tf_op jit(solution)/shard_map/ppermute | solution.py:248
  82.7 5.6 %collective-permute-done.19 = bf16[2,2,80,1024]{3,2,1,0:T(8,128)(2,1)S(1)} collective-permute-done((bf16[2,2,80,1024]{3,2,1,0:T(8,128)(2,1)S(1)}, bf16[2,2,80,1024]{3,2,1,0:T(8,128)(2,1)S(1)}, u32[]{:S(2)}, u32[]{:S(2)}) %collective-permute-start.19) | collective-permute-done | bytes 655392 | tf_op jit(solution)/shard_map/ppermute | solution.py:248
  90.2 2.7 %shard_map.99 = (f32[2,1,160,1024]{3,2,1,0:T(8,128)S(1)}, bf16[2,1,160,1024]{3,2,1,0:T(8,128)(2,1)S(1)}) custom-call(s32[1]{0:T(128)} %bitcast.place, s32[16,8]{1,0:T(8,128)S(1)} %copy.18.refs_0_.flags, bf16[4,160,512]{2,1,0:T(8,128)(2,1)S(1)} %constant_dynamic-update-slice_fusion.2.refs_1_.refs_8_, ...), custom_call_target="tpu_custom_call" | custom-call | flops 1342177280 | bytes 5373952 | tf_op jit(solution)/shard_map/pallas_call | solution.py:76
  93.5 2.7 %shard_map.100 = (f32[2,1,160,1024]{3,2,1,0:T(8,128)S(1)}, bf16[2,1,160,1024]{3,2,1,0:T(8,128)(2,1)S(1)}) custom-call(s32[1]{0:T(128)} %bitcast.place, s32[16,8]{1,0:T(8,128)S(1)} %copy.18.refs_0_.flags, bf16[4,160,512]{2,1,0:T(8,128)(2,1)S(1)} %constant_dynamic-update-slice_fusion.2.refs_1_.refs_8_, ...), custom_call_target="tpu_custom_call" | custom-call | flops 1342177280 | bytes 5373952 | tf_op jit(solution)/shard_map/pallas_call | solution.py:76
  97.3 3.9 %collective-permute-done.14 = bf16[1,2,80,1024]{3,2,1,0:T(8,128)(2,1)S(1)} collective-permute-done((bf16[1,2,80,1024]{3,2,1,0:T(8,128)(2,1)S(1)}, bf16[1,2,80,1024]{3,2,1,0:T(8,128)(2,1)S(1)}, u32[]{:S(2)}, u32[]{:S(2)}) %collective-permute-start.14) | collective-permute-done | bytes 327712 | tf_op jit(solution)/shard_map/ppermute | solution.py:248
  101.4 2.7 %collective-permute-start.15 = (bf16[160,1024]{1,0:T(8,128)(2,1)S(1)}, bf16[160,1024]{1,0:T(8,128)(2,1)S(1)}, u32[]{:S(2)}, u32[]{:S(2)}) collective-permute-start(bf16[160,1024]{1,0:T(8,128)(2,1)S(1)} %pad_maximum_fusion.4.refs_0_), channel_id=1, source_target_pairs={{0,8},{8,0},{16,24},{24,16},{1,9},{9,1},{17,25},{25,17},{2,10},{10... | collective-permute-start | bytes 983048 | tf_op jit(solution)/shard_map/ppermute | solution.py:248
  104.9 8.5 %collective-permute-done.27 = bf16[2,1,160,1024]{3,2,1,0:T(8,128)(2,1)S(1)} collective-permute-done((bf16[2,1,160,1024]{3,2,1,0:T(8,128)(2,1)S(1)}, bf16[2,1,160,1024]{3,2,1,0:T(8,128)(2,1)S(1)}, u32[]{:S(2)}, u32[]{:S(2)}) %collective-permute-start.27) | collective-permute-done | bytes 655392 | tf_op jit(solution)/shard_map/ppermute | solution.py:248
  117.6 9.8 %collective-permute-done.28 = bf16[1,1,160,1024]{3,2,1,0:T(8,128)(2,1)S(1)} collective-permute-done((bf16[1,1,160,1024]{3,2,1,0:T(8,128)(2,1)S(1)}, bf16[1,1,160,1024]{3,2,1,0:T(8,128)(2,1)S(1)}, u32[]{:S(2)}, u32[]{:S(2)}) %collective-permute-start.28) | collective-permute-done | bytes 327712 | tf_op jit(solution)/shard_map/ppermute | solution.py:248
  129.6 8.5 %collective-permute-done.33 = bf16[1,1,160,1024]{3,2,1,0:T(8,128)(2,1)S(1)} collective-permute-done((bf16[1,1,160,1024]{3,2,1,0:T(8,128)(2,1)S(1)}, bf16[1,1,160,1024]{3,2,1,0:T(8,128)(2,1)S(1)}, u32[]{:S(2)}, u32[]{:S(2)}) %collective-permute-start.33) | collective-permute-done | bytes 327712 | tf_op jit(solution)/shard_map/ppermute | solution.py:248
  144.6 4.1 %collective-permute-done.29.refs_1_ = bf16[2,80,1024]{2,1,0:T(8,128)(2,1)S(1)} collective-permute-done((bf16[2,80,1024]{2,1,0:T(8,128)(2,1)S(1)}, bf16[2,80,1024]{2,1,0:T(8,128)(2,1)S(1)}, u32[]{:S(2)}, u32[]{:S(2)}) %collective-permute-start.29) | collective-permute-done | bytes 327712 | tf_op jit(solution)/shard_map/ppermute | solution.py:248
  152.7 5.3 %collective-permute-done.35.refs_6_ = bf16[2,80,1024]{2,1,0:T(8,128)(2,1)S(1)} collective-permute-done((bf16[2,80,1024]{2,1,0:T(8,128)(2,1)S(1)}, bf16[2,80,1024]{2,1,0:T(8,128)(2,1)S(1)}, u32[]{:S(2)}, u32[]{:S(2)}) %collective-permute-start.35) | collective-permute-done | bytes 327712 | tf_op jit(solution)/shard_map/ppermute | solution.py:248
  159.8 2.9 %collective-permute-done.37.refs_1_ = bf16[2,80,1024]{2,1,0:T(8,128)(2,1)S(1)} collective-permute-done((bf16[2,80,1024]{2,1,0:T(8,128)(2,1)S(1)}, bf16[2,80,1024]{2,1,0:T(8,128)(2,1)S(1)}, u32[]{:S(2)}, u32[]{:S(2)}) %collective-permute-start.37) | collective-permute-done | bytes 327712 | tf_op jit(solution)/shard_map/ppermute | solution.py:248
  167.7 3.0 %shard_map.101 = bf16[4,80,512]{2,1,0:T(8,128)(2,1)S(1)} custom-call(s32[1]{0:T(128)} %bitcast.place, s32[8,16]{1,0:T(8,128)S(1)} %dynamic_slice.9.refs_0_.gate_flags, s32[8,16]{1,0:T(8,128)S(1)} %dynamic_slice.10.refs_1_.up_flags, bf16[2,80,1024]{2,1,0:T(8,128)(2,1)S(1)} %pad_maximum_fusion.6.refs_0_, ...), custom_call_target="tpu_custom_call" | custom-call | flops 1342177280 | bytes 7471104 | tf_op jit(solution)/shard_map/pallas_call | solution.py:138
  170.7 2.8 %shard_map.102 = f32[4,80,512]{2,1,0:T(8,128)S(1)} custom-call(s32[1]{0:T(128)} %bitcast.place, s32[8,16]{1,0:T(8,128)S(1)} %dynamic_slice.9.refs_0_.gate_flags, s32[8,16]{1,0:T(8,128)S(1)} %dynamic_slice.10.refs_1_.up_flags, bf16[2,80,1024]{2,1,0:T(8,128)(2,1)S(1)} %pad_maximum_fusion.6.refs_0_, bf16[2,80,1024]{2,1,0:T(8,128)(2,1)S(1)} %collective-permute-done.29.refs_1_, ...), custom_call_target="tpu_custom_call" | custom-call | flops 1342177280 | bytes 7471104 | tf_op jit(solution)/shard_map/pallas_call | solution.py:138
  175.7 2.8 %shard_map.103 = bf16[4,80,512]{2,1,0:T(8,128)(2,1)S(1)} custom-call(s32[1]{0:T(128)} %bitcast.place, s32[8,16]{1,0:T(8,128)S(1)} %dynamic_slice.9.refs_0_.gate_flags, s32[8,16]{1,0:T(8,128)S(1)} %dynamic_slice.10.refs_1_.up_flags, bf16[2,80,1024]{2,1,0:T(8,128)(2,1)S(1)} %pad_maximum_fusion.8.refs_0_, ...), custom_call_target="tpu_custom_call" | custom-call | flops 1342177280 | bytes 7471104 | tf_op jit(solution)/shard_map/pallas_call | solution.py:138
  178.6 2.8 %shard_map.104 = f32[4,80,512]{2,1,0:T(8,128)S(1)} custom-call(s32[1]{0:T(128)} %bitcast.place, s32[8,16]{1,0:T(8,128)S(1)} %dynamic_slice.9.refs_0_.gate_flags, s32[8,16]{1,0:T(8,128)S(1)} %dynamic_slice.10.refs_1_.up_flags, bf16[2,80,1024]{2,1,0:T(8,128)(2,1)S(1)} %pad_maximum_fusion.8.refs_0_, bf16[2,80,1024]{2,1,0:T(8,128)(2,1)S(1)} %collective-permute-done.37.refs_1_, ...), custom_call_target="tpu_custom_call" | custom-call | flops 1342177280 | bytes 7471104 | tf_op jit(solution)/shard_map/pallas_call | solution.py:138
  185.2 2.5 %collective-permute-done.48 = bf16[80,512]{1,0:T(8,128)(2,1)S(1)} collective-permute-done((bf16[80,512]{1,0:T(8,128)(2,1)S(1)}, bf16[80,512]{1,0:T(8,128)(2,1)S(1)}, u32[]{:S(2)}, u32[]{:S(2)}) %collective-permute-start.48) | collective-permute-done | bytes 81952 | tf_op jit(solution)/shard_map/ppermute | solution.py:248
  195.4 2.7 %collective-permute-start.53 = (bf16[160,512]{1,0:T(8,128)(2,1)S(1)}, bf16[160,512]{1,0:T(8,128)(2,1)S(1)}, u32[]{:S(2)}, u32[]{:S(2)}) collective-permute-start(bf16[160,512]{1,0:T(8,128)(2,1)S(1)} %pad_maximum_fusion.13), channel_id=1, source_target_pairs={{0,6},{1,7},{2,4},{3,5},{4,2},{5,3},{6,0},{7,1},{8,14},{9,15},{10,... | collective-permute-start | bytes 491528 | tf_op jit(solution)/shard_map/ppermute | solution.py:251
  198.1 2.9 %collective-permute-start.52 = (bf16[160,512]{1,0:T(8,128)(2,1)S(1)}, bf16[160,512]{1,0:T(8,128)(2,1)S(1)}, u32[]{:S(2)}, u32[]{:S(2)}) collective-permute-start(bf16[160,512]{1,0:T(8,128)(2,1)S(1)} %pad_maximum_fusion.12), channel_id=1, source_target_pairs={{0,4},{1,5},{2,6},{3,7},{4,0},{5,1},{6,2},{7,3},{8,12},{9,13},{10,... | collective-permute-start | bytes 491528 | tf_op jit(solution)/shard_map/ppermute | solution.py:251
  201.1 6.4 %shard_map.105 = bf16[2048,1024]{1,0:T(8,128)(2,1)} custom-call(s32[1]{0:T(128)} %bitcast.place, s32[16,8]{1,0:T(8,128)S(1)} %copy.18.refs_0_.flags, bf16[160,1024]{1,0:T(8,128)(2,1)S(1)} %pad_maximum_fusion.4.refs_0_, bf16[160,1024]{1,0:T(8,128)(2,1)S(1)} %collective-permute-done.15.refs_1_, bf16[160,1024]{1,0:T(8,128)(2,1)S(1)} %collective-permute-done.16.refs_2_, ...), custom_call_target="tpu_custom_call" | custom-call | flops 2684354560 | bytes 8126464 | tf_op jit(solution)/shard_map/pallas_call | solution.py:200
  207.6 5.6 %collective-permute-done.52 = bf16[160,512]{1,0:T(8,128)(2,1)S(1)} collective-permute-done((bf16[160,512]{1,0:T(8,128)(2,1)S(1)}, bf16[160,512]{1,0:T(8,128)(2,1)S(1)}, u32[]{:S(2)}, u32[]{:S(2)}) %collective-permute-start.52) | collective-permute-done | bytes 163872 | tf_op jit(solution)/shard_map/ppermute | solution.py:251
  (178 shorter events, 75.6 us)
Async XLA Ops:
  27.3 12.5 %collective-permute-start.10 = (bf16[4,40,512]{2,1,0:T(8,128)(2,1)S(1)}, bf16[4,40,512]{2,1,0:T(8,128)(2,1)S(1)}, u32[]{:S(2)}, u32[]{:S(2)}) collective-permute-start(bf16[4,40,512]{2,1,0:T(8,128)(2,1)S(1)} %get-tuple-element.32), channel_id=1, source_target_pairs={{0,4},{1,5},{2,6},{3,7},{4,0},{5,1},{6,2},{7,3},{8,12},{9,13},{10,... | collective-permute-start | bytes 491528 | tf_op jit(solution)/shard_map/ppermute | solution.py:251
  39.9 16.7 %collective-permute-start.12 = (bf16[4,80,512]{2,1,0:T(8,128)(2,1)S(1)}, bf16[4,80,512]{2,1,0:T(8,128)(2,1)S(1)}, u32[]{:S(2)}, u32[]{:S(2)}) collective-permute-start(bf16[4,80,512]{2,1,0:T(8,128)(2,1)S(1)} %constant_dynamic-update-slice_fusion.refs_2_), channel_id=1, source_target_pairs={{0,1},{1,0},{2,3},{3,2},{4,5},{5,4},{6,7},{7,6},{8,9},{9,8},{10,11... | collective-permute-start | bytes 983048 | tf_op jit(solution)/shard_map/ppermute | solution.py:254
  47.3 24.0 %collective-permute-start.8 = (bf16[2,2,80,1024]{3,2,1,0:T(8,128)(2,1)S(1)}, bf16[2,2,80,1024]{3,2,1,0:T(8,128)(2,1)S(1)}, u32[]{:S(2)}, u32[]{:S(2)}) collective-permute-start(bf16[2,2,80,1024]{3,2,1,0:T(8,128)(2,1)S(1)} %get-tuple-element.27), channel_id=1, source_target_pairs={{0,8},{8,0},{16,24},{24,16},{1,9},{9,1},{17,25},{25,17},{2,10},{10... | collective-permute-start | bytes 1966088 | tf_op jit(solution)/shard_map/ppermute | solution.py:248
  50.8 22.3 %collective-permute-start.17 = (bf16[2,2,80,1024]{3,2,1,0:T(8,128)(2,1)S(1)}, bf16[2,2,80,1024]{3,2,1,0:T(8,128)(2,1)S(1)}, u32[]{:S(2)}, u32[]{:S(2)}) collective-permute-start(bf16[2,2,80,1024]{3,2,1,0:T(8,128)(2,1)S(1)} %get-tuple-element.30), channel_id=1, source_target_pairs={{0,16},{8,24},{16,0},{24,8},{1,17},{9,25},{17,1},{25,9},{2,18},{10... | collective-permute-start | bytes 1966088 | tf_op jit(solution)/shard_map/ppermute | solution.py:248
  55.6 15.0 %collective-permute-start.24 = (bf16[4,40,512]{2,1,0:T(8,128)(2,1)S(1)}, bf16[4,40,512]{2,1,0:T(8,128)(2,1)S(1)}, u32[]{:S(2)}, u32[]{:S(2)}) collective-permute-start(bf16[4,40,512]{2,1,0:T(8,128)(2,1)S(1)} %get-tuple-element.40), channel_id=1, source_target_pairs={{0,4},{1,5},{2,6},{3,7},{4,0},{5,1},{6,2},{7,3},{8,12},{9,13},{10,... | collective-permute-start | bytes 491528 | tf_op jit(solution)/shard_map/ppermute | solution.py:251
  56.6 14.7 %collective-permute-start.25 = (bf16[4,40,512]{2,1,0:T(8,128)(2,1)S(1)}, bf16[4,40,512]{2,1,0:T(8,128)(2,1)S(1)}, u32[]{:S(2)}, u32[]{:S(2)}) collective-permute-start(bf16[4,40,512]{2,1,0:T(8,128)(2,1)S(1)} %get-tuple-element.40), channel_id=1, source_target_pairs={{0,6},{1,7},{2,4},{3,5},{4,2},{5,3},{6,0},{7,1},{8,14},{9,15},{10,... | collective-permute-start | bytes 491528 | tf_op jit(solution)/shard_map/ppermute | solution.py:251
  64.0 17.7 %collective-permute-start.13 = (bf16[2,2,80,1024]{3,2,1,0:T(8,128)(2,1)S(1)}, bf16[2,2,80,1024]{3,2,1,0:T(8,128)(2,1)S(1)}, u32[]{:S(2)}, u32[]{:S(2)}) collective-permute-start(bf16[2,2,80,1024]{3,2,1,0:T(8,128)(2,1)S(1)} %get-tuple-element.34), channel_id=1, source_target_pairs={{0,8},{8,0},{16,24},{24,16},{1,9},{9,1},{17,25},{25,17},{2,10},{10... | collective-permute-start | bytes 1966088 | tf_op jit(solution)/shard_map/ppermute | solution.py:248
  70.6 17.7 %collective-permute-start.19 = (bf16[2,2,80,1024]{3,2,1,0:T(8,128)(2,1)S(1)}, bf16[2,2,80,1024]{3,2,1,0:T(8,128)(2,1)S(1)}, u32[]{:S(2)}, u32[]{:S(2)}) collective-permute-start(bf16[2,2,80,1024]{3,2,1,0:T(8,128)(2,1)S(1)} %get-tuple-element.37), channel_id=1, source_target_pairs={{0,16},{8,24},{16,0},{24,8},{1,17},{9,25},{17,1},{25,9},{2,18},{10... | collective-permute-start | bytes 1966088 | tf_op jit(solution)/shard_map/ppermute | solution.py:248
  71.3 18.9 %collective-permute-start.26 = (bf16[4,160,512]{2,1,0:T(8,128)(2,1)S(1)}, bf16[4,160,512]{2,1,0:T(8,128)(2,1)S(1)}, u32[]{:S(2)}, u32[]{:S(2)}) collective-permute-start(bf16[4,160,512]{2,1,0:T(8,128)(2,1)S(1)} %constant_dynamic-update-slice_fusion.2.refs_1_.refs_8_), channel_id=1, source_target_pairs={{0,1},{1,0},{2,3},{3,2},{4,5},{5,4},{6,7},{7,6},{8,9},{9,8},{10,11... | collective-permute-start | bytes 1966088 | tf_op jit(solution)/shard_map/ppermute | solution.py:254
  71.6 24.5 %collective-permute-start.9 = (bf16[1,2,80,1024]{3,2,1,0:T(8,128)(2,1)S(1)}, bf16[1,2,80,1024]{3,2,1,0:T(8,128)(2,1)S(1)}, u32[]{:S(2)}, u32[]{:S(2)}) collective-permute-start(bf16[1,2,80,1024]{3,2,1,0:T(8,128)(2,1)S(1)} %slice.314), channel_id=1, source_target_pairs={{0,16},{8,24},{16,0},{24,8},{1,17},{9,25},{17,1},{25,9},{2,18},{10... | collective-permute-start | bytes 983048 | tf_op jit(solution)/shard_map/ppermute | solution.py:248
  73.4 23.5 %collective-permute-start.18 = (bf16[1,2,80,1024]{3,2,1,0:T(8,128)(2,1)S(1)}, bf16[1,2,80,1024]{3,2,1,0:T(8,128)(2,1)S(1)}, u32[]{:S(2)}, u32[]{:S(2)}) collective-permute-start(bf16[1,2,80,1024]{3,2,1,0:T(8,128)(2,1)S(1)} %slice.312), channel_id=1, source_target_pairs={{0,8},{8,0},{16,24},{24,16},{1,9},{9,1},{17,25},{25,17},{2,10},{10... | collective-permute-start | bytes 983048 | tf_op jit(solution)/shard_map/ppermute | solution.py:248
  82.0 19.2 %collective-permute-start.14 = (bf16[1,2,80,1024]{3,2,1,0:T(8,128)(2,1)S(1)}, bf16[1,2,80,1024]{3,2,1,0:T(8,128)(2,1)S(1)}, u32[]{:S(2)}, u32[]{:S(2)}) collective-permute-start(bf16[1,2,80,1024]{3,2,1,0:T(8,128)(2,1)S(1)} %slice.313), channel_id=1, source_target_pairs={{0,16},{8,24},{16,0},{24,8},{1,17},{9,25},{17,1},{25,9},{2,18},{10... | collective-permute-start | bytes 983048 | tf_op jit(solution)/shard_map/ppermute | solution.py:248
  88.6 16.1 %collective-permute-start.20 = (bf16[1,2,80,1024]{3,2,1,0:T(8,128)(2,1)S(1)}, bf16[1,2,80,1024]{3,2,1,0:T(8,128)(2,1)S(1)}, u32[]{:S(2)}, u32[]{:S(2)}) collective-permute-start(bf16[1,2,80,1024]{3,2,1,0:T(8,128)(2,1)S(1)} %slice.311), channel_id=1, source_target_pairs={{0,8},{8,0},{16,24},{24,16},{1,9},{9,1},{17,25},{25,17},{2,10},{10... | collective-permute-start | bytes 983048 | tf_op jit(solution)/shard_map/ppermute | solution.py:248
  92.9 20.5 %collective-permute-start.27 = (bf16[2,1,160,1024]{3,2,1,0:T(8,128)(2,1)S(1)}, bf16[2,1,160,1024]{3,2,1,0:T(8,128)(2,1)S(1)}, u32[]{:S(2)}, u32[]{:S(2)}) collective-permute-start(bf16[2,1,160,1024]{3,2,1,0:T(8,128)(2,1)S(1)} %get-tuple-element.42), channel_id=1, source_target_pairs={{0,8},{8,0},{16,24},{24,16},{1,9},{9,1},{17,25},{25,17},{2,10},{10... | collective-permute-start | bytes 1966088 | tf_op jit(solution)/shard_map/ppermute | solution.py:248
  96.2 19.6 %collective-permute-start.32 = (bf16[2,1,160,1024]{3,2,1,0:T(8,128)(2,1)S(1)}, bf16[2,1,160,1024]{3,2,1,0:T(8,128)(2,1)S(1)}, u32[]{:S(2)}, u32[]{:S(2)}) collective-permute-start(bf16[2,1,160,1024]{3,2,1,0:T(8,128)(2,1)S(1)} %get-tuple-element.45), channel_id=1, source_target_pairs={{0,16},{8,24},{16,0},{24,8},{1,17},{9,25},{17,1},{25,9},{2,18},{10... | collective-permute-start | bytes 1966088 | tf_op jit(solution)/shard_map/ppermute | solution.py:248
  101.4 38.8 %collective-permute-start.15 = (bf16[160,1024]{1,0:T(8,128)(2,1)S(1)}, bf16[160,1024]{1,0:T(8,128)(2,1)S(1)}, u32[]{:S(2)}, u32[]{:S(2)}) collective-permute-start(bf16[160,1024]{1,0:T(8,128)(2,1)S(1)} %pad_maximum_fusion.4.refs_0_), channel_id=1, source_target_pairs={{0,8},{8,0},{16,24},{24,16},{1,9},{9,1},{17,25},{25,17},{2,10},{10... | collective-permute-start | bytes 983048 | tf_op jit(solution)/shard_map/ppermute | solution.py:248
  104.1 37.9 %collective-permute-start.16 = (bf16[160,1024]{1,0:T(8,128)(2,1)S(1)}, bf16[160,1024]{1,0:T(8,128)(2,1)S(1)}, u32[]{:S(2)}, u32[]{:S(2)}) collective-permute-start(bf16[160,1024]{1,0:T(8,128)(2,1)S(1)} %pad_maximum_fusion.4.refs_0_), channel_id=1, source_target_pairs={{0,16},{8,24},{16,0},{24,8},{1,17},{9,25},{17,1},{25,9},{2,18},{10... | collective-permute-start | bytes 983048 | tf_op jit(solution)/shard_map/ppermute | solution.py:248
  113.6 13.8 %collective-permute-start.28 = (bf16[1,1,160,1024]{3,2,1,0:T(8,128)(2,1)S(1)}, bf16[1,1,160,1024]{3,2,1,0:T(8,128)(2,1)S(1)}, u32[]{:S(2)}, u32[]{:S(2)}) collective-permute-start(bf16[1,1,160,1024]{3,2,1,0:T(8,128)(2,1)S(1)} %slice.310), channel_id=1, source_target_pairs={{0,16},{8,24},{16,0},{24,8},{1,17},{9,25},{17,1},{25,9},{2,18},{10... | collective-permute-start | bytes 983048 | tf_op jit(solution)/shard_map/ppermute | solution.py:248
  114.3 28.2 %collective-permute-start.21 = (bf16[160,1024]{1,0:T(8,128)(2,1)S(1)}, bf16[160,1024]{1,0:T(8,128)(2,1)S(1)}, u32[]{:S(2)}, u32[]{:S(2)}) collective-permute-start(bf16[160,1024]{1,0:T(8,128)(2,1)S(1)} %pad_maximum_fusion.5.refs_4_), channel_id=1, source_target_pairs={{0,8},{8,0},{16,24},{24,16},{1,9},{9,1},{17,25},{25,17},{2,10},{10... | collective-permute-start | bytes 983048 | tf_op jit(solution)/shard_map/ppermute | solution.py:248
  115.8 27.2 %collective-permute-start.22 = (bf16[160,1024]{1,0:T(8,128)(2,1)S(1)}, bf16[160,1024]{1,0:T(8,128)(2,1)S(1)}, u32[]{:S(2)}, u32[]{:S(2)}) collective-permute-start(bf16[160,1024]{1,0:T(8,128)(2,1)S(1)} %pad_maximum_fusion.5.refs_4_), channel_id=1, source_target_pairs={{0,16},{8,24},{16,0},{24,8},{1,17},{9,25},{17,1},{25,9},{2,18},{10... | collective-permute-start | bytes 983048 | tf_op jit(solution)/shard_map/ppermute | solution.py:248
  142.1 15.9 %collective-permute-start.35 = (bf16[2,80,1024]{2,1,0:T(8,128)(2,1)S(1)}, bf16[2,80,1024]{2,1,0:T(8,128)(2,1)S(1)}, u32[]{:S(2)}, u32[]{:S(2)}) collective-permute-start(bf16[2,80,1024]{2,1,0:T(8,128)(2,1)S(1)} %pad_maximum_fusion.7.refs_4_), channel_id=1, source_target_pairs={{0,16},{8,24},{16,0},{24,8},{1,17},{9,25},{17,1},{25,9},{2,18},{10... | collective-permute-start | bytes 983048 | tf_op jit(solution)/shard_map/ppermute | solution.py:248
  142.5 15.8 %collective-permute-start.34 = (bf16[2,80,1024]{2,1,0:T(8,128)(2,1)S(1)}, bf16[2,80,1024]{2,1,0:T(8,128)(2,1)S(1)}, u32[]{:S(2)}, u32[]{:S(2)}) collective-permute-start(bf16[2,80,1024]{2,1,0:T(8,128)(2,1)S(1)} %pad_maximum_fusion.7.refs_4_), channel_id=1, source_target_pairs={{0,8},{8,0},{16,24},{24,16},{1,9},{9,1},{17,25},{25,17},{2,10},{10... | collective-permute-start | bytes 983048 | tf_op jit(solution)/shard_map/ppermute | solution.py:248
  143.0 19.8 %collective-permute-start.37 = (bf16[2,80,1024]{2,1,0:T(8,128)(2,1)S(1)}, bf16[2,80,1024]{2,1,0:T(8,128)(2,1)S(1)}, u32[]{:S(2)}, u32[]{:S(2)}) collective-permute-start(bf16[2,80,1024]{2,1,0:T(8,128)(2,1)S(1)} %pad_maximum_fusion.8.refs_0_), channel_id=1, source_target_pairs={{0,8},{8,0},{16,24},{24,16},{1,9},{9,1},{17,25},{25,17},{2,10},{10... | collective-permute-start | bytes 983048 | tf_op jit(solution)/shard_map/ppermute | solution.py:248
  148.7 15.7 %collective-permute-start.41 = (bf16[2,80,1024]{2,1,0:T(8,128)(2,1)S(1)}, bf16[2,80,1024]{2,1,0:T(8,128)(2,1)S(1)}, u32[]{:S(2)}, u32[]{:S(2)}) collective-permute-start(bf16[2,80,1024]{2,1,0:T(8,128)(2,1)S(1)} %pad_maximum_fusion.9.refs_4_), channel_id=1, source_target_pairs={{0,16},{8,24},{16,0},{24,8},{1,17},{9,25},{17,1},{25,9},{2,18},{10... | collective-permute-start | bytes 983048 | tf_op jit(solution)/shard_map/ppermute | solution.py:248
  150.9 15.2 %collective-permute-start.31 = (bf16[2,80,1024]{2,1,0:T(8,128)(2,1)S(1)}, bf16[2,80,1024]{2,1,0:T(8,128)(2,1)S(1)}, u32[]{:S(2)}, u32[]{:S(2)}) collective-permute-start(bf16[2,80,1024]{2,1,0:T(8,128)(2,1)S(1)} %collective-permute-done.29.refs_1_), channel_id=1, source_target_pairs={{0,16},{8,24},{16,0},{24,8},{1,17},{9,25},{17,1},{25,9},{2,18},{10... | collective-permute-start | bytes 983048 | tf_op jit(solution)/shard_map/ppermute | solution.py:248
  158.3 15.2 %collective-permute-start.38 = (bf16[2,80,1024]{2,1,0:T(8,128)(2,1)S(1)}, bf16[2,80,1024]{2,1,0:T(8,128)(2,1)S(1)}, u32[]{:S(2)}, u32[]{:S(2)}) collective-permute-start(bf16[2,80,1024]{2,1,0:T(8,128)(2,1)S(1)} %pad_maximum_fusion.8.refs_0_), channel_id=1, source_target_pairs={{0,16},{8,24},{16,0},{24,8},{1,17},{9,25},{17,1},{25,9},{2,18},{10... | collective-permute-start | bytes 983048 | tf_op jit(solution)/shard_map/ppermute | solution.py:248
  162.8 12.6 %collective-permute-start.40 = (bf16[2,80,1024]{2,1,0:T(8,128)(2,1)S(1)}, bf16[2,80,1024]{2,1,0:T(8,128)(2,1)S(1)}, u32[]{:S(2)}, u32[]{:S(2)}) collective-permute-start(bf16[2,80,1024]{2,1,0:T(8,128)(2,1)S(1)} %pad_maximum_fusion.9.refs_4_), channel_id=1, source_target_pairs={{0,8},{8,0},{16,24},{24,16},{1,9},{9,1},{17,25},{25,17},{2,10},{10... | collective-permute-start | bytes 983048 | tf_op jit(solution)/shard_map/ppermute | solution.py:248
  173.5 27.5 %collective-permute-start.54 = (bf16[160,1024]{1,0:T(8,128)(2,1)S(1)}, bf16[160,1024]{1,0:T(8,128)(2,1)S(1)}, u32[]{:S(2)}, u32[]{:S(2)}) collective-permute-start(bf16[160,1024]{1,0:T(8,128)(2,1)S(1)} %collective-permute-done.15.refs_1_), channel_id=1, source_target_pairs={{0,16},{8,24},{16,0},{24,8},{1,17},{9,25},{17,1},{25,9},{2,18},{10... | collective-permute-start | bytes 983048 | tf_op jit(solution)/shard_map/ppermute | solution.py:248
  175.4 25.7 %collective-permute-start.55 = (bf16[160,1024]{1,0:T(8,128)(2,1)S(1)}, bf16[160,1024]{1,0:T(8,128)(2,1)S(1)}, u32[]{:S(2)}, u32[]{:S(2)}) collective-permute-start(bf16[160,1024]{1,0:T(8,128)(2,1)S(1)} %collective-permute-done.22.refs_6_), channel_id=1, source_target_pairs={{0,8},{8,0},{16,24},{24,16},{1,9},{9,1},{17,25},{25,17},{2,10},{10... | collective-permute-start | bytes 983048 | tf_op jit(solution)/shard_map/ppermute | solution.py:248
  195.4 12.1 %collective-permute-start.53 = (bf16[160,512]{1,0:T(8,128)(2,1)S(1)}, bf16[160,512]{1,0:T(8,128)(2,1)S(1)}, u32[]{:S(2)}, u32[]{:S(2)}) collective-permute-start(bf16[160,512]{1,0:T(8,128)(2,1)S(1)} %pad_maximum_fusion.13), channel_id=1, source_target_pairs={{0,6},{1,7},{2,4},{3,5},{4,2},{5,3},{6,0},{7,1},{8,14},{9,15},{10,... | collective-permute-start | bytes 491528 | tf_op jit(solution)/shard_map/ppermute | solution.py:251
  198.1 15.0 %collective-permute-start.52 = (bf16[160,512]{1,0:T(8,128)(2,1)S(1)}, bf16[160,512]{1,0:T(8,128)(2,1)S(1)}, u32[]{:S(2)}, u32[]{:S(2)}) collective-permute-start(bf16[160,512]{1,0:T(8,128)(2,1)S(1)} %pad_maximum_fusion.12), channel_id=1, source_target_pairs={{0,4},{1,5},{2,6},{3,7},{4,0},{5,1},{6,2},{7,3},{8,12},{9,13},{10,... | collective-permute-start | bytes 491528 | tf_op jit(solution)/shard_map/ppermute | solution.py:251
  201.0 12.2 %collective-permute-start.51 = (bf16[160,512]{1,0:T(8,128)(2,1)S(1)}, bf16[160,512]{1,0:T(8,128)(2,1)S(1)}, u32[]{:S(2)}, u32[]{:S(2)}) collective-permute-start(bf16[160,512]{1,0:T(8,128)(2,1)S(1)} %pad_maximum_fusion.11), channel_id=1, source_target_pairs={{0,2},{1,3},{2,0},{3,1},{4,6},{5,7},{6,4},{7,5},{8,10},{9,11},{10,... | collective-permute-start | bytes 491528 | tf_op jit(solution)/shard_map/ppermute | solution.py:251
  (31 other events, 224.2 us)

commit v5 on v4

--- a/solution.py
+++ b/solution.py
@@ -63,7 +63,7 @@
                 dims = (((1,), (0,)), ((), ()))
             part = lax.dot_general(x_all[...], masked, dims, preferred_element_type=jnp.float32)
             part = part.reshape(groups, group_rows, tile)
-            kept[:, w] = part[: groups // 2]
+            kept[:, w] = part[: groups // 2].astype(jnp.bfloat16)
             sent[:, w] = part[groups // 2 :].astype(jnp.bfloat16)
 
     full = pl.BlockSpec((groups, rows, width), lambda j, *_: (0, 0, 0))
@@ -83,7 +83,7 @@
             scratch_shapes=[pltpu.VMEM((groups * group_rows, inner), jnp.bfloat16)],
         ),
         out_shape=[
-            jax.ShapeDtypeStruct(shape, jnp.float32),
+            jax.ShapeDtypeStruct(shape, jnp.bfloat16),
             jax.ShapeDtypeStruct(shape, jnp.bfloat16),
         ],
         compiler_params=pltpu.CompilerParams(vmem_limit_bytes=VMEM_BYTES),
@@ -282,9 +282,9 @@
 
     def owner_sum(kept, sent, bit_order):
         for bit in bit_order:
-            total = kept + across(sent, 1 << bit).astype(jnp.float32)
-            groups = total.shape[0]
-            kept, sent = total[: groups // 2], total[groups // 2 :].astype(jnp.bfloat16)
+            total = kept.astype(jnp.float32) + across(sent, 1 << bit).astype(jnp.float32)
+            groups, low = total.shape[0], total.astype(jnp.bfloat16)
+            kept, sent = low[: groups // 2], low[groups // 2 :]
         return total[0]
 
     def gathered(piece, bit_order):
@@ -316,7 +316,7 @@
     products_b = forward([part_b], *projections, products_a[1])
     g_start = after(g_own, far[-1], products_a[1])
     g_parts = [part_of([g_start] + [along(g_start, k) for k in range(1, n_f)])]
-    products_g = forward(g_parts, [down_weight], [down_flags], True, products_b[1])
+    products_g = forward(g_parts, [down_weight], [down_flags], True)
     pre = [sums(products_a), sums(products_b)]
     hidden_grad = sums(products_g)
 

time: 215 us -> 214 us (level)
  no operation moved by 1% of the time
where the time goes in v5:
time: 214 us
  waiting for transfers between devices  95.3 us (45%)
  starting transfers between devices  69.2 us (32%)
  Pallas kernels  34.9 us (16%)
  local copies, waits for them, and re-layouts  7.18 us (3%)
  other arithmetic  6.22 us (3%)
    ppermute x39, waiting for transfers between devices, across(): return lax.ppermute(x, 'fsdp', [(f, f ^ k) for f in range(n_f)])  67.4 us
    ppermute x39, starting transfers between devices, across(): return lax.ppermute(x, 'fsdp', [(f, f ^ k) for f in range(n_f)])  47.5 us
    ppermute x12, waiting for transfers between devices, along(): return lax.ppermute(x, 'tensor', [(t, t ^ 2 * k) for t in range(n_t)])  27.9 us
    ppermute x12, starting transfers between devices, along(): return lax.ppermute(x, 'tensor', [(t, t ^ 2 * k) for t in range(n_t)])  21.3 us
    pallas_call x6, Pallas kernels, forward_half(): pl.pallas_call(kernel, grid_spec=pltpu.PrefetchScalarGridSpec(num_scalar_...  17.1 us
    pallas_call x4, Pallas kernels, input_side(): pl.pallas_call(kernel, grid_spec=pltpu.PrefetchScalarGridSpec(num_scalar_...  11.4 us
    pallas_call x1, Pallas kernels, down_product(): pl.pallas_call(kernel, grid_spec=pltpu.PrefetchScalarGridSpec(num_scalar_...  6.4 us
    unnamed x19, local copies, waits for them, and re-layouts  4.51 us
  transfers between devices with their start and end apart: 56, of which 24 were waited for; matrix products, arithmetic and copies ran while one was open for 3% of the time, Pallas kernels for 16%

profile of v5, /device:TPU:0, one launch (start us, length us, event | category | flops | bytes accessed | tf_op | source)
XLA Modules:
  0.0 214.2 jit_solution(7251114251360850281)
XLA Ops:
  2.1 5.1 %collective-permute-start.2 = (bf16[2,40,512]{2,1,0:T(8,128)(2,1)S(1)}, bf16[2,40,512]{2,1,0:T(8,128)(2,1)S(1)}, u32[]{:S(2)}, u32[]{:S(2)}) collective-permute-start(bf16[2,40,512]{2,1,0:T(8,128)(2,1)S(1)} %get-tuple-element.81), channel_id=1, source_target_pairs={{0,6},{1,7},{2,4},{3,5},{4,2},{5,3},{6,0},{7,1},{8,14},{9,15},{10,... | collective-permute-start | bytes 245768 | tf_op jit(solution)/shard_map/ppermute | solution.py:251
  7.8 2.4 %collective-permute-done.2 = bf16[2,40,512]{2,1,0:T(8,128)(2,1)S(1)} collective-permute-done((bf16[2,40,512]{2,1,0:T(8,128)(2,1)S(1)}, bf16[2,40,512]{2,1,0:T(8,128)(2,1)S(1)}, u32[]{:S(2)}, u32[]{:S(2)}) %collective-permute-start.2) | collective-permute-done | bytes 81952 | tf_op jit(solution)/shard_map/ppermute | solution.py:251
  10.2 3.8 %collective-permute-done.1 = bf16[2,40,512]{2,1,0:T(8,128)(2,1)S(1)} collective-permute-done((bf16[2,40,512]{2,1,0:T(8,128)(2,1)S(1)}, bf16[2,40,512]{2,1,0:T(8,128)(2,1)S(1)}, u32[]{:S(2)}, u32[]{:S(2)}) %collective-permute-start.1) | collective-permute-done | bytes 81952 | tf_op jit(solution)/shard_map/ppermute | solution.py:251
  14.4 2.5 %collective-permute-start.5 = (bf16[2,40,512]{2,1,0:T(8,128)(2,1)S(1)}, bf16[2,40,512]{2,1,0:T(8,128)(2,1)S(1)}, u32[]{:S(2)}, u32[]{:S(2)}) collective-permute-start(bf16[2,40,512]{2,1,0:T(8,128)(2,1)S(1)} %get-tuple-element.77), channel_id=1, source_target_pairs={{0,24},{8,16},{16,8},{24,0},{1,25},{9,17},{17,9},{25,1},{2,26},{10... | collective-permute-start | bytes 245768 | tf_op jit(solution)/shard_map/ppermute | solution.py:248
  22.9 4.4 %collective-permute-done.6 = bf16[4,40,512]{2,1,0:T(8,128)(2,1)S(1)} collective-permute-done((bf16[4,40,512]{2,1,0:T(8,128)(2,1)S(1)}, bf16[4,40,512]{2,1,0:T(8,128)(2,1)S(1)}, u32[]{:S(2)}, u32[]{:S(2)}) %collective-permute-start.6) | collective-permute-done | bytes 163872 | tf_op jit(solution)/shard_map/ppermute | solution.py:251
  33.3 6.5 %collective-permute-done.10 = bf16[4,40,512]{2,1,0:T(8,128)(2,1)S(1)} collective-permute-done((bf16[4,40,512]{2,1,0:T(8,128)(2,1)S(1)}, bf16[4,40,512]{2,1,0:T(8,128)(2,1)S(1)}, u32[]{:S(2)}, u32[]{:S(2)}) %collective-permute-start.10) | collective-permute-done | bytes 163872 | tf_op jit(solution)/shard_map/ppermute | solution.py:251
  44.4 2.9 %shard_map.95 = (bf16[2,2,80,1024]{3,2,1,0:T(8,128)(2,1)S(1)}, bf16[2,2,80,1024]{3,2,1,0:T(8,128)(2,1)S(1)}) custom-call(s32[1]{0:T(128)} %bitcast.place, s32[8,16]{1,0:T(8,128)S(1)} %dynamic_slice.9.refs_0_.gate_flags, s32[8,16]{1,0:T(8,128)S(1)} %dynamic_slice.10.refs_1_.up_flags, bf16[4,80,512]{2,1,0:T(8,128)(2,1)S(1)} %pad_maximum_fusion.3.refs_2_, ...), custom_call_target="tpu_custom_call" | custom-call | flops 1342177280 | bytes 6815744 | tf_op jit(solution)/shard_map/pallas_call | solution.py:76
  47.8 2.9 %shard_map.96 = (bf16[2,2,80,1024]{3,2,1,0:T(8,128)(2,1)S(1)}, bf16[2,2,80,1024]{3,2,1,0:T(8,128)(2,1)S(1)}) custom-call(s32[1]{0:T(128)} %bitcast.place, s32[8,16]{1,0:T(8,128)S(1)} %dynamic_slice.9.refs_0_.gate_flags, s32[8,16]{1,0:T(8,128)S(1)} %dynamic_slice.10.refs_1_.up_flags, bf16[4,80,512]{2,1,0:T(8,128)(2,1)S(1)} %pad_maximum_fusion.3.refs_2_, ...), custom_call_target="tpu_custom_call" | custom-call | flops 1342177280 | bytes 6815744 | tf_op jit(solution)/shard_map/pallas_call | solution.py:76
  52.5 3.0 %collective-permute-start.23 = (bf16[4,40,512]{2,1,0:T(8,128)(2,1)S(1)}, bf16[4,40,512]{2,1,0:T(8,128)(2,1)S(1)}, u32[]{:S(2)}, u32[]{:S(2)}) collective-permute-start(bf16[4,40,512]{2,1,0:T(8,128)(2,1)S(1)} %get-tuple-element.38), channel_id=1, source_target_pairs={{0,2},{1,3},{2,0},{3,1},{4,6},{5,7},{6,4},{7,5},{8,10},{9,11},{10,... | collective-permute-start | bytes 491528 | tf_op jit(solution)/shard_map/ppermute | solution.py:251
  58.0 2.9 %shard_map.97 = (bf16[2,2,80,1024]{3,2,1,0:T(8,128)(2,1)S(1)}, bf16[2,2,80,1024]{3,2,1,0:T(8,128)(2,1)S(1)}) custom-call(s32[1]{0:T(128)} %bitcast.place, s32[8,16]{1,0:T(8,128)S(1)} %dynamic_slice.9.refs_0_.gate_flags, s32[8,16]{1,0:T(8,128)S(1)} %dynamic_slice.10.refs_1_.up_flags, bf16[4,80,512]{2,1,0:T(8,128)(2,1)S(1)} %constant_dynamic-update-slice_fusion.refs_2_, ...), custom_call_target="tpu_custom_call" | custom-call | flops 1342177280 | bytes 6815744 | tf_op jit(solution)/shard_map/pallas_call | solution.py:76
  60.9 3.0 %shard_map.98 = (bf16[2,2,80,1024]{3,2,1,0:T(8,128)(2,1)S(1)}, bf16[2,2,80,1024]{3,2,1,0:T(8,128)(2,1)S(1)}) custom-call(s32[1]{0:T(128)} %bitcast.place, s32[8,16]{1,0:T(8,128)S(1)} %dynamic_slice.9.refs_0_.gate_flags, s32[8,16]{1,0:T(8,128)S(1)} %dynamic_slice.10.refs_1_.up_flags, bf16[4,80,512]{2,1,0:T(8,128)(2,1)S(1)} %constant_dynamic-update-slice_fusion.refs_2_, ...), custom_call_target="tpu_custom_call" | custom-call | flops 1342177280 | bytes 6815744 | tf_op jit(solution)/shard_map/pallas_call | solution.py:76
  65.5 5.1 %collective-permute-done.24 = bf16[4,40,512]{2,1,0:T(8,128)(2,1)S(1)} collective-permute-done((bf16[4,40,512]{2,1,0:T(8,128)(2,1)S(1)}, bf16[4,40,512]{2,1,0:T(8,128)(2,1)S(1)}, u32[]{:S(2)}, u32[]{:S(2)}) %collective-permute-start.24) | collective-permute-done | bytes 163872 | tf_op jit(solution)/shard_map/ppermute | solution.py:251
  74.9 6.7 %collective-permute-done.13 = bf16[2,2,80,1024]{3,2,1,0:T(8,128)(2,1)S(1)} collective-permute-done((bf16[2,2,80,1024]{3,2,1,0:T(8,128)(2,1)S(1)}, bf16[2,2,80,1024]{3,2,1,0:T(8,128)(2,1)S(1)}, u32[]{:S(2)}, u32[]{:S(2)}) %collective-permute-start.13) | collective-permute-done | bytes 655392 | tf_op jit(solution)/shard_map/ppermute | solution.py:248
  82.6 5.7 %collective-permute-done.19 = bf16[2,2,80,1024]{3,2,1,0:T(8,128)(2,1)S(1)} collective-permute-done((bf16[2,2,80,1024]{3,2,1,0:T(8,128)(2,1)S(1)}, bf16[2,2,80,1024]{3,2,1,0:T(8,128)(2,1)S(1)}, u32[]{:S(2)}, u32[]{:S(2)}) %collective-permute-start.19) | collective-permute-done | bytes 655392 | tf_op jit(solution)/shard_map/ppermute | solution.py:248
  90.1 2.7 %shard_map.99 = (bf16[2,1,160,1024]{3,2,1,0:T(8,128)(2,1)S(1)}, bf16[2,1,160,1024]{3,2,1,0:T(8,128)(2,1)S(1)}) custom-call(s32[1]{0:T(128)} %bitcast.place, s32[16,8]{1,0:T(8,128)S(1)} %copy.18.refs_0_.flags, bf16[4,160,512]{2,1,0:T(8,128)(2,1)S(1)} %constant_dynamic-update-slice_fusion.2.refs_1_.refs_8_, ...), custom_call_target="tpu_custom_call" | custom-call | flops 1342177280 | bytes 5373952 | tf_op jit(solution)/shard_map/pallas_call | solution.py:76
  93.4 2.7 %shard_map.100 = (bf16[2,1,160,1024]{3,2,1,0:T(8,128)(2,1)S(1)}, bf16[2,1,160,1024]{3,2,1,0:T(8,128)(2,1)S(1)}) custom-call(s32[1]{0:T(128)} %bitcast.place, s32[16,8]{1,0:T(8,128)S(1)} %copy.18.refs_0_.flags, bf16[4,160,512]{2,1,0:T(8,128)(2,1)S(1)} %constant_dynamic-update-slice_fusion.2.refs_1_.refs_8_, ...), custom_call_target="tpu_custom_call" | custom-call | flops 1342177280 | bytes 5373952 | tf_op jit(solution)/shard_map/pallas_call | solution.py:76
  97.1 4.4 %collective-permute-done.14 = bf16[1,2,80,1024]{3,2,1,0:T(8,128)(2,1)S(1)} collective-permute-done((bf16[1,2,80,1024]{3,2,1,0:T(8,128)(2,1)S(1)}, bf16[1,2,80,1024]{3,2,1,0:T(8,128)(2,1)S(1)}, u32[]{:S(2)}, u32[]{:S(2)}) %collective-permute-start.14) | collective-permute-done | bytes 327712 | tf_op jit(solution)/shard_map/ppermute | solution.py:248
  104.8 8.5 %collective-permute-done.27 = bf16[2,1,160,1024]{3,2,1,0:T(8,128)(2,1)S(1)} collective-permute-done((bf16[2,1,160,1024]{3,2,1,0:T(8,128)(2,1)S(1)}, bf16[2,1,160,1024]{3,2,1,0:T(8,128)(2,1)S(1)}, u32[]{:S(2)}, u32[]{:S(2)}) %collective-permute-start.27) | collective-permute-done | bytes 655392 | tf_op jit(solution)/shard_map/ppermute | solution.py:248
  117.5 9.8 %collective-permute-done.28 = bf16[1,1,160,1024]{3,2,1,0:T(8,128)(2,1)S(1)} collective-permute-done((bf16[1,1,160,1024]{3,2,1,0:T(8,128)(2,1)S(1)}, bf16[1,1,160,1024]{3,2,1,0:T(8,128)(2,1)S(1)}, u32[]{:S(2)}, u32[]{:S(2)}) %collective-permute-start.28) | collective-permute-done | bytes 327712 | tf_op jit(solution)/shard_map/ppermute | solution.py:248
  129.5 8.5 %collective-permute-done.33 = bf16[1,1,160,1024]{3,2,1,0:T(8,128)(2,1)S(1)} collective-permute-done((bf16[1,1,160,1024]{3,2,1,0:T(8,128)(2,1)S(1)}, bf16[1,1,160,1024]{3,2,1,0:T(8,128)(2,1)S(1)}, u32[]{:S(2)}, u32[]{:S(2)}) %collective-permute-start.33) | collective-permute-done | bytes 327712 | tf_op jit(solution)/shard_map/ppermute | solution.py:248
  144.5 4.1 %collective-permute-done.29.refs_1_ = bf16[2,80,1024]{2,1,0:T(8,128)(2,1)S(1)} collective-permute-done((bf16[2,80,1024]{2,1,0:T(8,128)(2,1)S(1)}, bf16[2,80,1024]{2,1,0:T(8,128)(2,1)S(1)}, u32[]{:S(2)}, u32[]{:S(2)}) %collective-permute-start.29) | collective-permute-done | bytes 327712 | tf_op jit(solution)/shard_map/ppermute | solution.py:248
  152.6 5.3 %collective-permute-done.35.refs_6_ = bf16[2,80,1024]{2,1,0:T(8,128)(2,1)S(1)} collective-permute-done((bf16[2,80,1024]{2,1,0:T(8,128)(2,1)S(1)}, bf16[2,80,1024]{2,1,0:T(8,128)(2,1)S(1)}, u32[]{:S(2)}, u32[]{:S(2)}) %collective-permute-start.35) | collective-permute-done | bytes 327712 | tf_op jit(solution)/shard_map/ppermute | solution.py:248
  159.8 2.9 %collective-permute-done.37.refs_1_ = bf16[2,80,1024]{2,1,0:T(8,128)(2,1)S(1)} collective-permute-done((bf16[2,80,1024]{2,1,0:T(8,128)(2,1)S(1)}, bf16[2,80,1024]{2,1,0:T(8,128)(2,1)S(1)}, u32[]{:S(2)}, u32[]{:S(2)}) %collective-permute-start.37) | collective-permute-done | bytes 327712 | tf_op jit(solution)/shard_map/ppermute | solution.py:248
  167.6 3.0 %shard_map.101 = bf16[4,80,512]{2,1,0:T(8,128)(2,1)S(1)} custom-call(s32[1]{0:T(128)} %bitcast.place, s32[8,16]{1,0:T(8,128)S(1)} %dynamic_slice.9.refs_0_.gate_flags, s32[8,16]{1,0:T(8,128)S(1)} %dynamic_slice.10.refs_1_.up_flags, bf16[2,80,1024]{2,1,0:T(8,128)(2,1)S(1)} %pad_maximum_fusion.6.refs_0_, ...), custom_call_target="tpu_custom_call" | custom-call | flops 1342177280 | bytes 7471104 | tf_op jit(solution)/shard_map/pallas_call | solution.py:138
  170.7 2.8 %shard_map.102 = f32[4,80,512]{2,1,0:T(8,128)S(1)} custom-call(s32[1]{0:T(128)} %bitcast.place, s32[8,16]{1,0:T(8,128)S(1)} %dynamic_slice.9.refs_0_.gate_flags, s32[8,16]{1,0:T(8,128)S(1)} %dynamic_slice.10.refs_1_.up_flags, bf16[2,80,1024]{2,1,0:T(8,128)(2,1)S(1)} %pad_maximum_fusion.6.refs_0_, bf16[2,80,1024]{2,1,0:T(8,128)(2,1)S(1)} %collective-permute-done.29.refs_1_, ...), custom_call_target="tpu_custom_call" | custom-call | flops 1342177280 | bytes 7471104 | tf_op jit(solution)/shard_map/pallas_call | solution.py:138
  175.6 2.8 %shard_map.103 = bf16[4,80,512]{2,1,0:T(8,128)(2,1)S(1)} custom-call(s32[1]{0:T(128)} %bitcast.place, s32[8,16]{1,0:T(8,128)S(1)} %dynamic_slice.9.refs_0_.gate_flags, s32[8,16]{1,0:T(8,128)S(1)} %dynamic_slice.10.refs_1_.up_flags, bf16[2,80,1024]{2,1,0:T(8,128)(2,1)S(1)} %pad_maximum_fusion.8.refs_0_, ...), custom_call_target="tpu_custom_call" | custom-call | flops 1342177280 | bytes 7471104 | tf_op jit(solution)/shard_map/pallas_call | solution.py:138
  178.5 2.8 %shard_map.104 = f32[4,80,512]{2,1,0:T(8,128)S(1)} custom-call(s32[1]{0:T(128)} %bitcast.place, s32[8,16]{1,0:T(8,128)S(1)} %dynamic_slice.9.refs_0_.gate_flags, s32[8,16]{1,0:T(8,128)S(1)} %dynamic_slice.10.refs_1_.up_flags, bf16[2,80,1024]{2,1,0:T(8,128)(2,1)S(1)} %pad_maximum_fusion.8.refs_0_, bf16[2,80,1024]{2,1,0:T(8,128)(2,1)S(1)} %collective-permute-done.37.refs_1_, ...), custom_call_target="tpu_custom_call" | custom-call | flops 1342177280 | bytes 7471104 | tf_op jit(solution)/shard_map/pallas_call | solution.py:138
  185.1 2.5 %collective-permute-done.48 = bf16[80,512]{1,0:T(8,128)(2,1)S(1)} collective-permute-done((bf16[80,512]{1,0:T(8,128)(2,1)S(1)}, bf16[80,512]{1,0:T(8,128)(2,1)S(1)}, u32[]{:S(2)}, u32[]{:S(2)}) %collective-permute-start.48) | collective-permute-done | bytes 81952 | tf_op jit(solution)/shard_map/ppermute | solution.py:248
  195.4 2.7 %collective-permute-start.53 = (bf16[160,512]{1,0:T(8,128)(2,1)S(1)}, bf16[160,512]{1,0:T(8,128)(2,1)S(1)}, u32[]{:S(2)}, u32[]{:S(2)}) collective-permute-start(bf16[160,512]{1,0:T(8,128)(2,1)S(1)} %pad_maximum_fusion.13), channel_id=1, source_target_pairs={{0,6},{1,7},{2,4},{3,5},{4,2},{5,3},{6,0},{7,1},{8,14},{9,15},{10,... | collective-permute-start | bytes 491528 | tf_op jit(solution)/shard_map/ppermute | solution.py:251
  198.0 2.8 %collective-permute-start.52 = (bf16[160,512]{1,0:T(8,128)(2,1)S(1)}, bf16[160,512]{1,0:T(8,128)(2,1)S(1)}, u32[]{:S(2)}, u32[]{:S(2)}) collective-permute-start(bf16[160,512]{1,0:T(8,128)(2,1)S(1)} %pad_maximum_fusion.12), channel_id=1, source_target_pairs={{0,4},{1,5},{2,6},{3,7},{4,0},{5,1},{6,2},{7,3},{8,12},{9,13},{10,... | collective-permute-start | bytes 491528 | tf_op jit(solution)/shard_map/ppermute | solution.py:251
  201.0 6.4 %shard_map.105 = bf16[2048,1024]{1,0:T(8,128)(2,1)} custom-call(s32[1]{0:T(128)} %bitcast.place, s32[16,8]{1,0:T(8,128)S(1)} %copy.18.refs_0_.flags, bf16[160,1024]{1,0:T(8,128)(2,1)S(1)} %pad_maximum_fusion.4.refs_0_, bf16[160,1024]{1,0:T(8,128)(2,1)S(1)} %collective-permute-done.15.refs_1_, bf16[160,1024]{1,0:T(8,128)(2,1)S(1)} %collective-permute-done.16.refs_2_, ...), custom_call_target="tpu_custom_call" | custom-call | flops 2684354560 | bytes 8126464 | tf_op jit(solution)/shard_map/pallas_call | solution.py:200
  207.5 5.6 %collective-permute-done.52 = bf16[160,512]{1,0:T(8,128)(2,1)S(1)} collective-permute-done((bf16[160,512]{1,0:T(8,128)(2,1)S(1)}, bf16[160,512]{1,0:T(8,128)(2,1)S(1)}, u32[]{:S(2)}, u32[]{:S(2)}) %collective-permute-start.52) | collective-permute-done | bytes 163872 | tf_op jit(solution)/shard_map/ppermute | solution.py:251
  (178 shorter events, 75.4 us)
Async XLA Ops:
  27.3 12.5 %collective-permute-start.10 = (bf16[4,40,512]{2,1,0:T(8,128)(2,1)S(1)}, bf16[4,40,512]{2,1,0:T(8,128)(2,1)S(1)}, u32[]{:S(2)}, u32[]{:S(2)}) collective-permute-start(bf16[4,40,512]{2,1,0:T(8,128)(2,1)S(1)} %get-tuple-element.31), channel_id=1, source_target_pairs={{0,4},{1,5},{2,6},{3,7},{4,0},{5,1},{6,2},{7,3},{8,12},{9,13},{10,... | collective-permute-start | bytes 491528 | tf_op jit(solution)/shard_map/ppermute | solution.py:251
  39.9 16.6 %collective-permute-start.12 = (bf16[4,80,512]{2,1,0:T(8,128)(2,1)S(1)}, bf16[4,80,512]{2,1,0:T(8,128)(2,1)S(1)}, u32[]{:S(2)}, u32[]{:S(2)}) collective-permute-start(bf16[4,80,512]{2,1,0:T(8,128)(2,1)S(1)} %constant_dynamic-update-slice_fusion.refs_2_), channel_id=1, source_target_pairs={{0,1},{1,0},{2,3},{3,2},{4,5},{5,4},{6,7},{7,6},{8,9},{9,8},{10,11... | collective-permute-start | bytes 983048 | tf_op jit(solution)/shard_map/ppermute | solution.py:254
  47.3 24.0 %collective-permute-start.8 = (bf16[2,2,80,1024]{3,2,1,0:T(8,128)(2,1)S(1)}, bf16[2,2,80,1024]{3,2,1,0:T(8,128)(2,1)S(1)}, u32[]{:S(2)}, u32[]{:S(2)}) collective-permute-start(bf16[2,2,80,1024]{3,2,1,0:T(8,128)(2,1)S(1)} %get-tuple-element.26), channel_id=1, source_target_pairs={{0,8},{8,0},{16,24},{24,16},{1,9},{9,1},{17,25},{25,17},{2,10},{10... | collective-permute-start | bytes 1966088 | tf_op jit(solution)/shard_map/ppermute | solution.py:248
  50.7 22.3 %collective-permute-start.17 = (bf16[2,2,80,1024]{3,2,1,0:T(8,128)(2,1)S(1)}, bf16[2,2,80,1024]{3,2,1,0:T(8,128)(2,1)S(1)}, u32[]{:S(2)}, u32[]{:S(2)}) collective-permute-start(bf16[2,2,80,1024]{3,2,1,0:T(8,128)(2,1)S(1)} %get-tuple-element.29), channel_id=1, source_target_pairs={{0,16},{8,24},{16,0},{24,8},{1,17},{9,25},{17,1},{25,9},{2,18},{10... | collective-permute-start | bytes 1966088 | tf_op jit(solution)/shard_map/ppermute | solution.py:248
  55.5 15.0 %collective-permute-start.24 = (bf16[4,40,512]{2,1,0:T(8,128)(2,1)S(1)}, bf16[4,40,512]{2,1,0:T(8,128)(2,1)S(1)}, u32[]{:S(2)}, u32[]{:S(2)}) collective-permute-start(bf16[4,40,512]{2,1,0:T(8,128)(2,1)S(1)} %get-tuple-element.38), channel_id=1, source_target_pairs={{0,4},{1,5},{2,6},{3,7},{4,0},{5,1},{6,2},{7,3},{8,12},{9,13},{10,... | collective-permute-start | bytes 491528 | tf_op jit(solution)/shard_map/ppermute | solution.py:251
  56.5 14.7 %collective-permute-start.25 = (bf16[4,40,512]{2,1,0:T(8,128)(2,1)S(1)}, bf16[4,40,512]{2,1,0:T(8,128)(2,1)S(1)}, u32[]{:S(2)}, u32[]{:S(2)}) collective-permute-start(bf16[4,40,512]{2,1,0:T(8,128)(2,1)S(1)} %get-tuple-element.38), channel_id=1, source_target_pairs={{0,6},{1,7},{2,4},{3,5},{4,2},{5,3},{6,0},{7,1},{8,14},{9,15},{10,... | collective-permute-start | bytes 491528 | tf_op jit(solution)/shard_map/ppermute | solution.py:251
  63.9 17.7 %collective-permute-start.13 = (bf16[2,2,80,1024]{3,2,1,0:T(8,128)(2,1)S(1)}, bf16[2,2,80,1024]{3,2,1,0:T(8,128)(2,1)S(1)}, u32[]{:S(2)}, u32[]{:S(2)}) collective-permute-start(bf16[2,2,80,1024]{3,2,1,0:T(8,128)(2,1)S(1)} %get-tuple-element.33), channel_id=1, source_target_pairs={{0,8},{8,0},{16,24},{24,16},{1,9},{9,1},{17,25},{25,17},{2,10},{10... | collective-permute-start | bytes 1966088 | tf_op jit(solution)/shard_map/ppermute | solution.py:248
  70.6 17.7 %collective-permute-start.19 = (bf16[2,2,80,1024]{3,2,1,0:T(8,128)(2,1)S(1)}, bf16[2,2,80,1024]{3,2,1,0:T(8,128)(2,1)S(1)}, u32[]{:S(2)}, u32[]{:S(2)}) collective-permute-start(bf16[2,2,80,1024]{3,2,1,0:T(8,128)(2,1)S(1)} %get-tuple-element.36), channel_id=1, source_target_pairs={{0,16},{8,24},{16,0},{24,8},{1,17},{9,25},{17,1},{25,9},{2,18},{10... | collective-permute-start | bytes 1966088 | tf_op jit(solution)/shard_map/ppermute | solution.py:248
  71.2 18.9 %collective-permute-start.26 = (bf16[4,160,512]{2,1,0:T(8,128)(2,1)S(1)}, bf16[4,160,512]{2,1,0:T(8,128)(2,1)S(1)}, u32[]{:S(2)}, u32[]{:S(2)}) collective-permute-start(bf16[4,160,512]{2,1,0:T(8,128)(2,1)S(1)} %constant_dynamic-update-slice_fusion.2.refs_1_.refs_8_), channel_id=1, source_target_pairs={{0,1},{1,0},{2,3},{3,2},{4,5},{5,4},{6,7},{7,6},{8,9},{9,8},{10,11... | collective-permute-start | bytes 1966088 | tf_op jit(solution)/shard_map/ppermute | solution.py:254
  71.6 24.5 %collective-permute-start.9 = (bf16[1,2,80,1024]{3,2,1,0:T(8,128)(2,1)S(1)}, bf16[1,2,80,1024]{3,2,1,0:T(8,128)(2,1)S(1)}, u32[]{:S(2)}, u32[]{:S(2)}) collective-permute-start(bf16[1,2,80,1024]{3,2,1,0:T(8,128)(2,1)S(1)} %slice.186), channel_id=1, source_target_pairs={{0,16},{8,24},{16,0},{24,8},{1,17},{9,25},{17,1},{25,9},{2,18},{10... | collective-permute-start | bytes 983048 | tf_op jit(solution)/shard_map/ppermute | solution.py:248
  73.4 23.4 %collective-permute-start.18 = (bf16[1,2,80,1024]{3,2,1,0:T(8,128)(2,1)S(1)}, bf16[1,2,80,1024]{3,2,1,0:T(8,128)(2,1)S(1)}, u32[]{:S(2)}, u32[]{:S(2)}) collective-permute-start(bf16[1,2,80,1024]{3,2,1,0:T(8,128)(2,1)S(1)} %slice.194), channel_id=1, source_target_pairs={{0,8},{8,0},{16,24},{24,16},{1,9},{9,1},{17,25},{25,17},{2,10},{10... | collective-permute-start | bytes 983048 | tf_op jit(solution)/shard_map/ppermute | solution.py:248
  81.9 19.6 %collective-permute-start.14 = (bf16[1,2,80,1024]{3,2,1,0:T(8,128)(2,1)S(1)}, bf16[1,2,80,1024]{3,2,1,0:T(8,128)(2,1)S(1)}, u32[]{:S(2)}, u32[]{:S(2)}) collective-permute-start(bf16[1,2,80,1024]{3,2,1,0:T(8,128)(2,1)S(1)} %slice.190), channel_id=1, source_target_pairs={{0,16},{8,24},{16,0},{24,8},{1,17},{9,25},{17,1},{25,9},{2,18},{10... | collective-permute-start | bytes 983048 | tf_op jit(solution)/shard_map/ppermute | solution.py:248
  88.5 16.0 %collective-permute-start.20 = (bf16[1,2,80,1024]{3,2,1,0:T(8,128)(2,1)S(1)}, bf16[1,2,80,1024]{3,2,1,0:T(8,128)(2,1)S(1)}, u32[]{:S(2)}, u32[]{:S(2)}) collective-permute-start(bf16[1,2,80,1024]{3,2,1,0:T(8,128)(2,1)S(1)} %slice.198), channel_id=1, source_target_pairs={{0,8},{8,0},{16,24},{24,16},{1,9},{9,1},{17,25},{25,17},{2,10},{10... | collective-permute-start | bytes 983048 | tf_op jit(solution)/shard_map/ppermute | solution.py:248
  92.8 20.5 %collective-permute-start.27 = (bf16[2,1,160,1024]{3,2,1,0:T(8,128)(2,1)S(1)}, bf16[2,1,160,1024]{3,2,1,0:T(8,128)(2,1)S(1)}, u32[]{:S(2)}, u32[]{:S(2)}) collective-permute-start(bf16[2,1,160,1024]{3,2,1,0:T(8,128)(2,1)S(1)} %get-tuple-element.40), channel_id=1, source_target_pairs={{0,8},{8,0},{16,24},{24,16},{1,9},{9,1},{17,25},{25,17},{2,10},{10... | collective-permute-start | bytes 1966088 | tf_op jit(solution)/shard_map/ppermute | solution.py:248
  96.1 19.6 %collective-permute-start.32 = (bf16[2,1,160,1024]{3,2,1,0:T(8,128)(2,1)S(1)}, bf16[2,1,160,1024]{3,2,1,0:T(8,128)(2,1)S(1)}, u32[]{:S(2)}, u32[]{:S(2)}) collective-permute-start(bf16[2,1,160,1024]{3,2,1,0:T(8,128)(2,1)S(1)} %get-tuple-element.43), channel_id=1, source_target_pairs={{0,16},{8,24},{16,0},{24,8},{1,17},{9,25},{17,1},{25,9},{2,18},{10... | collective-permute-start | bytes 1966088 | tf_op jit(solution)/shard_map/ppermute | solution.py:248
  101.8 38.4 %collective-permute-start.15 = (bf16[160,1024]{1,0:T(8,128)(2,1)S(1)}, bf16[160,1024]{1,0:T(8,128)(2,1)S(1)}, u32[]{:S(2)}, u32[]{:S(2)}) collective-permute-start(bf16[160,1024]{1,0:T(8,128)(2,1)S(1)} %pad_maximum_fusion.4.refs_0_), channel_id=1, source_target_pairs={{0,8},{8,0},{16,24},{24,16},{1,9},{9,1},{17,25},{25,17},{2,10},{10... | collective-permute-start | bytes 983048 | tf_op jit(solution)/shard_map/ppermute | solution.py:248
  104.1 37.9 %collective-permute-start.16 = (bf16[160,1024]{1,0:T(8,128)(2,1)S(1)}, bf16[160,1024]{1,0:T(8,128)(2,1)S(1)}, u32[]{:S(2)}, u32[]{:S(2)}) collective-permute-start(bf16[160,1024]{1,0:T(8,128)(2,1)S(1)} %pad_maximum_fusion.4.refs_0_), channel_id=1, source_target_pairs={{0,16},{8,24},{16,0},{24,8},{1,17},{9,25},{17,1},{25,9},{2,18},{10... | collective-permute-start | bytes 983048 | tf_op jit(solution)/shard_map/ppermute | solution.py:248
  113.6 13.8 %collective-permute-start.28 = (bf16[1,1,160,1024]{3,2,1,0:T(8,128)(2,1)S(1)}, bf16[1,1,160,1024]{3,2,1,0:T(8,128)(2,1)S(1)}, u32[]{:S(2)}, u32[]{:S(2)}) collective-permute-start(bf16[1,1,160,1024]{3,2,1,0:T(8,128)(2,1)S(1)} %slice.203), channel_id=1, source_target_pairs={{0,16},{8,24},{16,0},{24,8},{1,17},{9,25},{17,1},{25,9},{2,18},{10... | collective-permute-start | bytes 983048 | tf_op jit(solution)/shard_map/ppermute | solution.py:248
  114.2 28.2 %collective-permute-start.21 = (bf16[160,1024]{1,0:T(8,128)(2,1)S(1)}, bf16[160,1024]{1,0:T(8,128)(2,1)S(1)}, u32[]{:S(2)}, u32[]{:S(2)}) collective-permute-start(bf16[160,1024]{1,0:T(8,128)(2,1)S(1)} %pad_maximum_fusion.5.refs_4_), channel_id=1, source_target_pairs={{0,8},{8,0},{16,24},{24,16},{1,9},{9,1},{17,25},{25,17},{2,10},{10... | collective-permute-start | bytes 983048 | tf_op jit(solution)/shard_map/ppermute | solution.py:248
  115.7 27.2 %collective-permute-start.22 = (bf16[160,1024]{1,0:T(8,128)(2,1)S(1)}, bf16[160,1024]{1,0:T(8,128)(2,1)S(1)}, u32[]{:S(2)}, u32[]{:S(2)}) collective-permute-start(bf16[160,1024]{1,0:T(8,128)(2,1)S(1)} %pad_maximum_fusion.5.refs_4_), channel_id=1, source_target_pairs={{0,16},{8,24},{16,0},{24,8},{1,17},{9,25},{17,1},{25,9},{2,18},{10... | collective-permute-start | bytes 983048 | tf_op jit(solution)/shard_map/ppermute | solution.py:248
  142.0 15.9 %collective-permute-start.35 = (bf16[2,80,1024]{2,1,0:T(8,128)(2,1)S(1)}, bf16[2,80,1024]{2,1,0:T(8,128)(2,1)S(1)}, u32[]{:S(2)}, u32[]{:S(2)}) collective-permute-start(bf16[2,80,1024]{2,1,0:T(8,128)(2,1)S(1)} %pad_maximum_fusion.7.refs_4_), channel_id=1, source_target_pairs={{0,16},{8,24},{16,0},{24,8},{1,17},{9,25},{17,1},{25,9},{2,18},{10... | collective-permute-start | bytes 983048 | tf_op jit(solution)/shard_map/ppermute | solution.py:248
  142.4 15.8 %collective-permute-start.34 = (bf16[2,80,1024]{2,1,0:T(8,128)(2,1)S(1)}, bf16[2,80,1024]{2,1,0:T(8,128)(2,1)S(1)}, u32[]{:S(2)}, u32[]{:S(2)}) collective-permute-start(bf16[2,80,1024]{2,1,0:T(8,128)(2,1)S(1)} %pad_maximum_fusion.7.refs_4_), channel_id=1, source_target_pairs={{0,8},{8,0},{16,24},{24,16},{1,9},{9,1},{17,25},{25,17},{2,10},{10... | collective-permute-start | bytes 983048 | tf_op jit(solution)/shard_map/ppermute | solution.py:248
  142.9 19.8 %collective-permute-start.37 = (bf16[2,80,1024]{2,1,0:T(8,128)(2,1)S(1)}, bf16[2,80,1024]{2,1,0:T(8,128)(2,1)S(1)}, u32[]{:S(2)}, u32[]{:S(2)}) collective-permute-start(bf16[2,80,1024]{2,1,0:T(8,128)(2,1)S(1)} %pad_maximum_fusion.8.refs_0_), channel_id=1, source_target_pairs={{0,8},{8,0},{16,24},{24,16},{1,9},{9,1},{17,25},{25,17},{2,10},{10... | collective-permute-start | bytes 983048 | tf_op jit(solution)/shard_map/ppermute | solution.py:248
  148.6 15.7 %collective-permute-start.41 = (bf16[2,80,1024]{2,1,0:T(8,128)(2,1)S(1)}, bf16[2,80,1024]{2,1,0:T(8,128)(2,1)S(1)}, u32[]{:S(2)}, u32[]{:S(2)}) collective-permute-start(bf16[2,80,1024]{2,1,0:T(8,128)(2,1)S(1)} %pad_maximum_fusion.9.refs_4_), channel_id=1, source_target_pairs={{0,16},{8,24},{16,0},{24,8},{1,17},{9,25},{17,1},{25,9},{2,18},{10... | collective-permute-start | bytes 983048 | tf_op jit(solution)/shard_map/ppermute | solution.py:248
  150.8 15.2 %collective-permute-start.31 = (bf16[2,80,1024]{2,1,0:T(8,128)(2,1)S(1)}, bf16[2,80,1024]{2,1,0:T(8,128)(2,1)S(1)}, u32[]{:S(2)}, u32[]{:S(2)}) collective-permute-start(bf16[2,80,1024]{2,1,0:T(8,128)(2,1)S(1)} %collective-permute-done.29.refs_1_), channel_id=1, source_target_pairs={{0,16},{8,24},{16,0},{24,8},{1,17},{9,25},{17,1},{25,9},{2,18},{10... | collective-permute-start | bytes 983048 | tf_op jit(solution)/shard_map/ppermute | solution.py:248
  158.3 15.2 %collective-permute-start.38 = (bf16[2,80,1024]{2,1,0:T(8,128)(2,1)S(1)}, bf16[2,80,1024]{2,1,0:T(8,128)(2,1)S(1)}, u32[]{:S(2)}, u32[]{:S(2)}) collective-permute-start(bf16[2,80,1024]{2,1,0:T(8,128)(2,1)S(1)} %pad_maximum_fusion.8.refs_0_), channel_id=1, source_target_pairs={{0,16},{8,24},{16,0},{24,8},{1,17},{9,25},{17,1},{25,9},{2,18},{10... | collective-permute-start | bytes 983048 | tf_op jit(solution)/shard_map/ppermute | solution.py:248
  162.7 12.6 %collective-permute-start.40 = (bf16[2,80,1024]{2,1,0:T(8,128)(2,1)S(1)}, bf16[2,80,1024]{2,1,0:T(8,128)(2,1)S(1)}, u32[]{:S(2)}, u32[]{:S(2)}) collective-permute-start(bf16[2,80,1024]{2,1,0:T(8,128)(2,1)S(1)} %pad_maximum_fusion.9.refs_4_), channel_id=1, source_target_pairs={{0,8},{8,0},{16,24},{24,16},{1,9},{9,1},{17,25},{25,17},{2,10},{10... | collective-permute-start | bytes 983048 | tf_op jit(solution)/shard_map/ppermute | solution.py:248
  173.5 27.5 %collective-permute-start.54 = (bf16[160,1024]{1,0:T(8,128)(2,1)S(1)}, bf16[160,1024]{1,0:T(8,128)(2,1)S(1)}, u32[]{:S(2)}, u32[]{:S(2)}) collective-permute-start(bf16[160,1024]{1,0:T(8,128)(2,1)S(1)} %collective-permute-done.15.refs_1_), channel_id=1, source_target_pairs={{0,16},{8,24},{16,0},{24,8},{1,17},{9,25},{17,1},{25,9},{2,18},{10... | collective-permute-start | bytes 983048 | tf_op jit(solution)/shard_map/ppermute | solution.py:248
  175.3 25.7 %collective-permute-start.55 = (bf16[160,1024]{1,0:T(8,128)(2,1)S(1)}, bf16[160,1024]{1,0:T(8,128)(2,1)S(1)}, u32[]{:S(2)}, u32[]{:S(2)}) collective-permute-start(bf16[160,1024]{1,0:T(8,128)(2,1)S(1)} %collective-permute-done.22.refs_6_), channel_id=1, source_target_pairs={{0,8},{8,0},{16,24},{24,16},{1,9},{9,1},{17,25},{25,17},{2,10},{10... | collective-permute-start | bytes 983048 | tf_op jit(solution)/shard_map/ppermute | solution.py:248
  195.4 12.1 %collective-permute-start.53 = (bf16[160,512]{1,0:T(8,128)(2,1)S(1)}, bf16[160,512]{1,0:T(8,128)(2,1)S(1)}, u32[]{:S(2)}, u32[]{:S(2)}) collective-permute-start(bf16[160,512]{1,0:T(8,128)(2,1)S(1)} %pad_maximum_fusion.13), channel_id=1, source_target_pairs={{0,6},{1,7},{2,4},{3,5},{4,2},{5,3},{6,0},{7,1},{8,14},{9,15},{10,... | collective-permute-start | bytes 491528 | tf_op jit(solution)/shard_map/ppermute | solution.py:251
  198.0 15.0 %collective-permute-start.52 = (bf16[160,512]{1,0:T(8,128)(2,1)S(1)}, bf16[160,512]{1,0:T(8,128)(2,1)S(1)}, u32[]{:S(2)}, u32[]{:S(2)}) collective-permute-start(bf16[160,512]{1,0:T(8,128)(2,1)S(1)} %pad_maximum_fusion.12), channel_id=1, source_target_pairs={{0,4},{1,5},{2,6},{3,7},{4,0},{5,1},{6,2},{7,3},{8,12},{9,13},{10,... | collective-permute-start | bytes 491528 | tf_op jit(solution)/shard_map/ppermute | solution.py:251
  200.9 12.2 %collective-permute-start.51 = (bf16[160,512]{1,0:T(8,128)(2,1)S(1)}, bf16[160,512]{1,0:T(8,128)(2,1)S(1)}, u32[]{:S(2)}, u32[]{:S(2)}) collective-permute-start(bf16[160,512]{1,0:T(8,128)(2,1)S(1)} %pad_maximum_fusion.11), channel_id=1, source_target_pairs={{0,2},{1,3},{2,0},{3,1},{4,6},{5,7},{6,4},{7,5},{8,10},{9,11},{10,... | collective-permute-start | bytes 491528 | tf_op jit(solution)/shard_map/ppermute | solution.py:251
  (31 other events, 224.3 us)
